TPU v7x, 32 devices: a whole 2x2x4 slice. The times are simulated.
32 devices in a mesh: groups: 2 (over x), tensor: 4 (over y, core), dp: 4 (over z).
Axes of the slice: x: 2, y: 2, z: 4, core: 2. Of those that a mesh axis runs over, the one named last changes fastest.
Arguments:
- queries: bfloat16 [4096, 12288], P(('groups', 'dp'), 'tensor'), parts along dimension 0, may hold values from -24 to 24
- keys: bfloat16 [4096, 1024], P(('groups', 'dp')), parts along dimension 0, may hold values from -14 to 14
- values: bfloat16 [4096, 1024], P(('groups', 'dp')), parts along dimension 0, may hold values from -6 to 6
- page_start: int32 [4096], P(('groups', 'dp')), parts along dimension 0, may hold values from 0 to 2047, as said below
Outputs:
- gram_band: float32 [24576, 9216], P(('groups', 'tensor', 'dp')), parts along dimension 0
There are 2 independent parts, one for each index of `groups`. A program takes and returns all parts, laid end to end along the dimension named above; each array names one. Nothing has to cross between parts.
Inputs may be any that keep to these rules, and one draw needn't show every extreme that they name: p - page_start[p] < 512, page_start never falls and starts each page at its first position; some page has exactly 512 tokens, and pages cross from one run of 512 tokens into the next.
All inputs are finite; a program needn't handle non-finite values.
Results may differ from a plain program's by a relative error of at most 0.012.
Values may be sent and summed in bfloat16 or wider, within the bound.
No kernel may reach another device: no remote copies, remote signals or barrier semaphores. Data moves between devices by JAX's collectives and lax.ppermute only.
A program may use at most 256 MiB of HBM per device.

v0:
```python
import functools

import jax
import jax.numpy as jnp
from jax import lax
from jax.experimental import pallas as pl
from jax.experimental.pallas import tpu as pltpu
from jax.sharding import PartitionSpec as P

HEADS = 96
HD = 128
KV_HEADS = 8
PAGE = 512
TILE = 256
ROWS = 256
STEP = 2
LOG2E = 1.4426950408889634
VMEM_LIMIT = 56 * 1024 * 1024


def shifted(x, axis, by):
    devices = lax.axis_size(axis)
    pairs = [(i, i + by) for i in range(devices) if 0 <= i + by < devices]
    return lax.ppermute(x, axis, pairs)


def from_behind(value, axis, steps):
    count = lax.axis_size(axis)
    pairs = [(source, (source + steps) % count) for source in range(count)]
    return lax.ppermute(value, axis, pairs)


def over_tensor(value, bit):
    count = lax.axis_size("tensor")
    return lax.ppermute(value, "tensor", [(t, t ^ bit) for t in range(count)])


def tie(value, *after):
    return lax.optimization_barrier((value, *after))[0] if after else value


def held(value, sums, *after):
    return lax.optimization_barrier((value, sums, *after))[:2]


def attend_kernel(start_ref, q_ref, kp_ref, ko_ref, vp_ref, vo_ref, out_ref, bias_ref):
    rows = q_ref.shape[0]
    tiles = rows // TILE
    keys_seen = PAGE + TILE

    @pl.when(pl.program_id(0) == 0)
    def _():
        for tile in range(tiles):
            shape = (TILE, keys_seen)
            query = lax.broadcasted_iota(jnp.int32, shape, 0) + tile * TILE
            key = lax.broadcasted_iota(jnp.int32, shape, 1) + (tile * TILE - PAGE)
            first = start_ref[tile * TILE : (tile + 1) * TILE, :]
            visible = (key >= first) & (key <= query)
            bias_ref[tile] = jnp.where(visible, 0.0, -1e30)

    for tile in range(tiles):
        lo = tile * TILE
        key = jnp.concatenate([kp_ref[lo:, :], ko_ref[: lo + TILE, :]], 0)
        value = jnp.concatenate([vp_ref[lo:, :], vo_ref[: lo + TILE, :]], 0)
        value = jnp.concatenate([value, jnp.ones_like(value)], 1)
        for head in range(q_ref.shape[1] // HD):
            columns = slice(head * HD, (head + 1) * HD)
            scores = lax.dot_general(
                q_ref[lo : lo + TILE, columns],
                key,
                (((1,), (1,)), ((), ())),
                preferred_element_type=jnp.float32,
            )
            scores = scores + bias_ref[tile]
            top = jnp.max(scores, axis=-1, keepdims=True)
            expo = jnp.exp2((scores - top) * (LOG2E / HD**0.5)).astype(jnp.bfloat16)
            mixed = jnp.dot(expo, value, preferred_element_type=jnp.float32)
            out_ref[lo : lo + TILE, columns] = (mixed[:, :HD] / mixed[:, HD:]).astype(jnp.bfloat16)


def attend(queries, own_kv, prev_kv, start, first_head, heads):
    rows = queries.shape[0]
    step = STEP if heads % STEP == 0 and first_head % STEP == 0 else 1
    key_spec = pl.BlockSpec((PAGE, HD), lambda h: (0, 0))
    value_spec = pl.BlockSpec((PAGE, HD), lambda h: (0, 1))
    return pl.pallas_call(
        attend_kernel,
        grid=(heads // step,),
        out_shape=jax.ShapeDtypeStruct((rows, heads * HD), jnp.bfloat16),
        in_specs=[
            pl.BlockSpec((rows, 1), lambda h: (0, 0)),
            pl.BlockSpec((rows, step * HD), lambda h: (0, first_head // step + h)),
            key_spec,
            key_spec,
            value_spec,
            value_spec,
        ],
        out_specs=pl.BlockSpec((rows, step * HD), lambda h: (0, h)),
        scratch_shapes=[pltpu.VMEM((rows // TILE, TILE, PAGE + TILE), jnp.float32)],
        compiler_params=pltpu.CompilerParams(vmem_limit_bytes=VMEM_LIMIT),
        cost_estimate=pl.CostEstimate(flops=10**15, bytes_accessed=1, transcendentals=0),
    )(start, queries, prev_kv, own_kv, prev_kv, own_kv)


def rows_kernel(widths, rows, place_ref, *refs):
    chunks = len(widths)
    sources, (out_ref, raw, sem) = refs[:chunks], refs[chunks:]
    offsets = [sum(widths[:c]) for c in range(chunks)]
    for where in range(sum(widths) // rows):

        @pl.when(place_ref[0] == where)
        def _():
            lo, hi = where * rows, (where + 1) * rows
            copies = []
            for c in range(chunks):
                first, last = max(lo, offsets[c]), min(hi, offsets[c] + widths[c])
                if first < last:
                    copies.append(
                        pltpu.make_async_copy(
                            sources[c].at[:, pl.ds(first - offsets[c], last - first)],
                            raw.at[:, pl.ds(first - lo, last - first)],
                            sem.at[len(copies)],
                        )
                    )
            for copy in copies:
                copy.start()
            for copy in copies:
                copy.wait()

    out_ref[...] = raw[...].T


def rows_of(place, pieces, rows):
    depth = pieces[0].shape[0]
    widths = tuple(x.shape[1] for x in pieces)
    return pl.pallas_call(
        functools.partial(rows_kernel, widths, rows),
        out_shape=jax.ShapeDtypeStruct((rows, depth), jnp.bfloat16),
        in_specs=[pl.BlockSpec(memory_space=pltpu.SMEM)]
        + [pl.BlockSpec(memory_space=pltpu.HBM)] * len(pieces),
        scratch_shapes=[
            pltpu.VMEM((depth, rows), jnp.bfloat16),
            pltpu.SemaphoreType.DMA((len(pieces),)),
        ],
        compiler_params=pltpu.CompilerParams(vmem_limit_bytes=VMEM_LIMIT),
        cost_estimate=pl.CostEstimate(flops=10**15, bytes_accessed=1, transcendentals=0),
    )(place, *pieces)


def gram_kernel(runs, tiles, starts, depth, scale, kept, added, *refs):
    lefts, refs = refs[:runs], refs[runs:]
    data, refs = refs[: runs * len(tiles)], list(refs[runs * len(tiles) :])
    old_ref = refs.pop(0) if added else None
    if kept:
        refs.pop(0)
    out_ref, left, b_buf, o_buf, left_sem, b_sem, o_sem = refs[:7]
    c_buf, c_sem = refs[7:] if added else (None, None)
    slots = b_buf.shape[0]

    def in_copies(i):
        slot = i % slots
        width = tiles[i][1]
        copies = [
            pltpu.make_async_copy(
                data[i * runs + run].at[:, pl.ds(starts[i * runs + run], width)],
                b_buf.at[slot, pl.ds(run * depth, depth), pl.ds(0, width)],
                b_sem.at[slot, run],
            )
            for run in range(runs)
        ]
        if added:
            copies.append(
                pltpu.make_async_copy(
                    old_ref.at[:, pl.ds(*tiles[i])],
                    c_buf.at[slot, :, pl.ds(0, width)],
                    c_sem.at[slot],
                )
            )
        return copies

    def out_copy(i):
        slot = i % slots
        return pltpu.make_async_copy(
            o_buf.at[slot, :, pl.ds(0, tiles[i][1])],
            out_ref.at[:, pl.ds(*tiles[i])],
            o_sem.at[slot],
        )

    left_copies = [
        pltpu.make_async_copy(
            lefts[run], left.at[:, pl.ds(run * depth, depth)], left_sem.at[run]
        )
        for run in range(runs)
    ]
    for copy in left_copies + in_copies(0):
        copy.start()
    for copy in left_copies:
        copy.wait()
    for i in range(1, min(slots - 1, len(tiles))):
        for copy in in_copies(i):
            copy.start()
    for i, (_, width) in enumerate(tiles):
        slot = i % slots
        if i + slots - 1 < len(tiles):
            for copy in in_copies(i + slots - 1):
                copy.start()
        for copy in in_copies(i):
            copy.wait()
        if i >= slots:
            out_copy(i - slots).wait()

        def block(part, slot=slot, width=width):
            result = scale * jnp.dot(
                left[part, :], b_buf[slot, :, :width], preferred_element_type=jnp.float32
            )
            if added:
                result = result + c_buf[slot, part, :width].astype(jnp.float32)
            o_buf[slot, part, :width] = result.astype(o_buf.dtype)

        if added:
            block(slice(None))
        else:
            pl.loop(0, left.shape[0] // ROWS)(lambda n: block(pl.ds(pl.multiple_of(n * ROWS, ROWS), ROWS)))
        out_copy(i).start()
    for i in range(max(0, len(tiles) - slots), len(tiles)):
        out_copy(i).wait()


def gram(out, lefts, tiles, width, columns, scale, kind, old=None):
    runs = len(lefts)
    rows, depth = lefts[0].shape
    places = [(first, width) for first, _ in tiles]
    data = [x for _, arrays in tiles for x, _ in arrays]
    starts = [x for _, arrays in tiles for _, x in arrays]
    kept, added = out is not None, old is not None
    any_spec = pl.BlockSpec(memory_space=pltpu.HBM)
    operands = [*lefts, *data] + ([old] if added else []) + ([out] if kept else [])
    slots = min(4, len(tiles))
    scratch = [
        pltpu.VMEM((rows, runs * depth), jnp.bfloat16),
        pltpu.VMEM((slots, runs * depth, width), jnp.bfloat16),
        pltpu.VMEM((slots, rows, width), kind),
        pltpu.SemaphoreType.DMA((runs,)),
        pltpu.SemaphoreType.DMA((slots, runs)),
        pltpu.SemaphoreType.DMA((slots,)),
    ]
    if added:
        scratch += [pltpu.VMEM((slots, rows, width), old.dtype), pltpu.SemaphoreType.DMA((slots,))]
    total = sum(width for _, width in places)
    return pl.pallas_call(
        functools.partial(gram_kernel, runs, places, starts, depth, scale, kept, added),
        out_shape=jax.ShapeDtypeStruct((rows, columns), kind),
        in_specs=[any_spec] * len(operands),
        out_specs=any_spec,
        scratch_shapes=scratch,
        input_output_aliases={len(operands) - 1: 0} if kept else {},
        compiler_params=pltpu.CompilerParams(vmem_limit_bytes=VMEM_LIMIT),
        cost_estimate=pl.CostEstimate(flops=10**15, bytes_accessed=1, transcendentals=0),
    )(*operands)


def kv_of(keys, values, local_heads):
    group = HEADS // KV_HEADS
    kv_count = max(1, local_heads // group)
    kv_first = lax.axis_index("tensor") * local_heads // group
    own, prev = [], []
    for k in range(kv_count):
        parts = [lax.dynamic_slice_in_dim(x, (kv_first + k) * HD, HD, 1) for x in (keys, values)]
        own.append(jnp.concatenate(parts, 1))
        prev.append(shifted(own[k], "dp", 1))
    return list(zip(own, prev)), local_heads // kv_count


CHUNKS = 6


def per_device(queries, keys, values, page_start):
    tok_rows, slab = queries.shape
    local_heads = slab // HD
    runs = lax.axis_size("dp")
    kv, per_kv = kv_of(keys, values, local_heads)
    run_index = lax.axis_index("dp")
    start = (page_start - run_index * tok_rows).reshape(tok_rows, 1)
    place = run_index.reshape(1)
    rows = slab // runs
    scale = 2.0 / (tok_rows * runs)
    even = lax.axis_index("tensor") % 2 == 0

    size = local_heads // CHUNKS
    width = size * HD
    own, mirror, sibling = {}, {}, {}
    within = {}
    half = CHUNKS // 2
    last = runs - 1
    over_z = [("own", c, r) for r in range(1, runs) for c in range(CHUNKS)]
    over_z += [("mirror", c, last) for c in range(half, CHUNKS)]
    over_y = [(c, r) for r in range(last) for c in range(CHUNKS)]
    over_y += [(c, last) for c in range(half)]

    left = {}
    sums = {}
    steps = max(len(over_z), len(over_y))
    ended = {}
    swapped = []
    def tiles(kinds, chosen, some_runs):
        tables = (own, sibling, mirror)
        return [
            (
                k * slab + c * width,
                [(tables[k][c, r], within[c, r] if k == 1 else 0) for r in some_runs],
            )
            for c in chosen
            for k in kinds
        ]

    def rows_for(some_runs):
        for r in some_runs:
            if r not in left:
                left[r] = rows_of(place, [own[c, r] for c in range(CHUNKS)], rows)
        return [left[r] for r in some_runs]

    every = list(range(runs))
    everything = list(range(CHUNKS))
    first_runs, last_runs = every[: runs // 2], every[runs // 2 :]
    moved = (2, 1)
    done = last * CHUNKS
    work = {
        done - 12: [("rows", 0)],
        done - 11: [("rows", 1)],
        done - 10: [((0,), everything, first_runs, False)],
        done - 8: [(moved, [0, 1], first_runs, False)],
        done - 6: [(moved, [2, 3], first_runs, False)],
        done - 4: [(moved, [4, 5], first_runs, False)],
        done - 2: [("rows", 2)],
        done + 1: [("rows", 3)],
        done + 2: [((0,), everything, last_runs, True)],
        done + 3: [(moved, [0, half], last_runs, True)],
        done + 4: [(moved, [1, half + 1], last_runs, True)],
        done + 5: [(moved, [half - 1, CHUNKS - 1], last_runs, True)],
    }

    for step in range(steps + 3):
        before = ended.get(step - 2, [])
        if step < CHUNKS:
            first = step * size
            some = tie(start, *[prev for _, prev in kv]) if step == 1 else start
            own[step, 0] = attend(queries, *kv[first // per_kv], some, first, size)
        arrived = []
        if step < len(over_z):
            kind, c, r = over_z[step]
            table = own if kind == "own" else mirror
            value, sums = held(table[c, r - 1], sums, *before)
            table[c, r] = from_behind(value, "dp", 1)
            arrived.append(table[c, r])
        if step < len(over_y):
            c, r = over_y[step]
            value, sums = held(own[c, r], sums, *before)
            mirror[c, r] = over_tensor(value, 2)
            arrived.append(mirror[c, r])
        ended[step] = arrived
        past = step - 2
        swaps = []
        if 0 <= past < steps:
            swaps = [over_y[past]] + [x[1:] for x in over_z[past : past + 1] if x[0] == "mirror"]
        if swaps:
            pair = ([mirror[x] for x in swaps], [own[x] for x in swaps])
            pair, sums = held(pair, sums, *before, *swapped)
            sent = jnp.where(even, *[jnp.concatenate(x, 1) for x in pair])
            sent = over_tensor(sent, 1)
            swapped = [sent]
            sibling.update({x: sent for x in swaps})
            within.update({x: i * width for i, x in enumerate(swaps)})
        for job in work.pop(step, ()):
            if job[0] == "rows":
                ended[step] += rows_for([job[1]])
            else:
                kinds, chosen, some_runs, added = job
                lefts, pieces = rows_for(some_runs), tiles(kinds, chosen, some_runs)
                if added:
                    sums["all"] = gram(
                        sums.get("all"), lefts, pieces, width, 3 * slab, scale, jnp.float32, sums["half"]
                    )
                else:
                    sums["half"] = gram(
                        sums.get("half"), lefts, pieces, width, 3 * slab, scale, jnp.bfloat16
                    )
    assert not work
    return sums["all"]


def per_device_general(queries, keys, values, page_start):
    tok_rows, slab_width = queries.shape
    local_heads = slab_width // HD
    runs = lax.axis_size("dp")
    kv, per_kv = kv_of(keys, values, local_heads)
    run_index = lax.axis_index("dp")
    start = (page_start - run_index * tok_rows).reshape(tok_rows, 1)
    outputs = jnp.concatenate(
        [attend(queries, *kv[h // per_kv], start, h, per_kv) for h in range(0, local_heads, per_kv)], 1
    )
    steps = lax.axis_size("tensor") // 2 + 1
    rows = slab_width // runs
    moving = lax.all_gather(outputs, "dp", axis=0, tiled=True)
    left = lax.dynamic_slice_in_dim(moving, run_index * rows, rows, 1)
    tiles = []
    for offset in range(steps):
        if offset:
            moving = from_behind(moving, "tensor", -1)
        tiles.append(
            lax.dot_general(
                left, moving, (((0,), (0,)), ((), ())), preferred_element_type=jnp.float32
            )
        )
    return jnp.concatenate(tiles, 1) * (2.0 / (tok_rows * runs))


def solution(mesh):
    cores = mesh.shape["tensor"]
    rows = HEADS * HD // cores // mesh.shape["dp"]
    tuned = cores == 4 and rows % HD == 0
    return jax.shard_map(
        per_device if tuned else per_device_general,
        mesh=mesh,
        in_specs=(
            P(("groups", "dp"), "tensor"),
            P(("groups", "dp"), None),
            P(("groups", "dp"), None),
            P(("groups", "dp")),
        ),
        out_specs=P(("groups", "tensor", "dp"), None),
        check_vma=False,
    )
```

profile of v0, /device:TPU:1, one launch (start us, length us, event | category | flops | bytes accessed | tf_op | source)
XLA Modules:
  0.0 290.1 jit_solution(17359184391652944105)
XLA Ops:
  1.2 4.0 %collective-permute-start = (bf16[512,256]{1,0:T(8,128)(2,1)S(1)}, bf16[512,256]{1,0:T(8,128)(2,1)S(1)}, u32[]{:S(2)}, u32[]{:S(2)}) collective-permute-start(bf16[512,256]{1,0:T(8,128)(2,1)S(1)} %pad_maximum_fusion.ko_ref.vo_ref), channel_id=1, source_target_pairs={{0,1},{1,2},{2,3},{4,5},{5,6},{6,7},{8,9},{9,10},{10,11},{12,13},{... | collective-permute-start | bytes 786440 | tf_op jit(solution)/shard_map/ppermute | solution.py:24
  6.0 3.9 %collective-permute-start.2 = (bf16[512,256]{1,0:T(8,128)(2,1)}, bf16[512,256]{1,0:T(8,128)(2,1)}, u32[]{:S(2)}, u32[]{:S(2)}) collective-permute-start(bf16[512,256]{1,0:T(8,128)(2,1)} %pad_maximum_fusion.1.ko_ref.vo_ref), channel_id=1, source_target_pairs={{0,1},{1,2},{2,3},{4,5},{5,6},{6,7},{8,9},{9,10},{10,11},{12,13},{... | collective-permute-start | bytes 786440 | tf_op jit(solution)/shard_map/ppermute | solution.py:24
  11.5 4.9 %shard_map.46.refs_0_.refs_2_ = bf16[512,512]{1,0:T(8,128)(2,1)} custom-call(s32[512,1]{1,0:T(8,128)} %copy.11.start_ref, bf16[512,3072]{1,0:T(8,128)(2,1)} %q_ref.11, bf16[512,256]{1,0:T(8,128)(2,1)} %copy-done.17, bf16[512,256]{1,0:T(8,128)(2,1)} %copy-done.11, bf16[512,256]{1,0:T(8,128)(2,1)} %copy-done.17, bf16[512,256]{1,0:T(8,128)(2,1)} %copy-done.11), custom_call_target="tpu_custom_call" | custom-call | flops 999999986991104 | bytes 1 | tf_op jit(solution)/shard_map/pallas_call | solution.py:86
  20.8 5.0 %shard_map.49.refs_1_.refs_4_ = bf16[512,512]{1,0:T(8,128)(2,1)} custom-call(s32[512,1]{1,0:T(8,128)} %copy.14.start_ref, bf16[512,3072]{1,0:T(8,128)(2,1)} %q_ref.11, bf16[512,256]{1,0:T(8,128)(2,1)} %copy-done.17, bf16[512,256]{1,0:T(8,128)(2,1)} %copy-done.11, bf16[512,256]{1,0:T(8,128)(2,1)} %copy-done.17, bf16[512,256]{1,0:T(8,128)(2,1)} %copy-done.11), custom_call_target="tpu_custom_call" | custom-call | flops 999999986991104 | bytes 1 | tf_op jit(solution)/shard_map/pallas_call | solution.py:86
  27.3 2.6 collective-permute-done.1.refs_0_.refs_3_
  30.8 7.2 %collective-permute-start.20 = (bf16[512,512]{1,0:T(8,128)(2,1)}, bf16[512,512]{1,0:T(8,128)(2,1)}, u32[]{:S(2)}, u32[]{:S(2)}) collective-permute-start(bf16[512,512]{1,0:T(8,128)(2,1)} %broadcast_select_fusion.17), channel_id=1, source_target_pairs={{0,4},{4,0},{8,12},{12,8},{1,5},{5,1},{9,13},{13,9},{2,6},{6,2},{1... | collective-permute-start | bytes 1572872 | tf_op jit(solution)/shard_map/ppermute | solution.py:35
  38.0 5.0 %shard_map.48.refs_2_.refs_6_ = bf16[512,512]{1,0:T(8,128)(2,1)} custom-call(s32[512,1]{1,0:T(8,128)} %copy.11.start_ref, bf16[512,3072]{1,0:T(8,128)(2,1)} %q_ref.11, bf16[512,256]{1,0:T(8,128)(2,1)} %copy-done.17, bf16[512,256]{1,0:T(8,128)(2,1)} %copy-done.11, bf16[512,256]{1,0:T(8,128)(2,1)} %copy-done.17, bf16[512,256]{1,0:T(8,128)(2,1)} %copy-done.11), custom_call_target="tpu_custom_call" | custom-call | flops 999999986991104 | bytes 1 | tf_op jit(solution)/shard_map/pallas_call | solution.py:86
  48.1 4.9 %shard_map.51.refs_3_.refs_8_ = bf16[512,512]{1,0:T(8,128)(2,1)} custom-call(s32[512,1]{1,0:T(8,128)} %copy.11.start_ref, bf16[512,3072]{1,0:T(8,128)(2,1)} %q_ref.11, bf16[512,256]{1,0:T(8,128)(2,1)} %collective-permute-done.2.kp_ref.vp_ref, bf16[512,256]{1,0:T(8,128)(2,1)} %pad_maximum_fusion.1.ko_ref.vo_ref, ...), custom_call_target="tpu_custom_call" | custom-call | flops 999999986991104 | bytes 1 | tf_op jit(solution)/shard_map/pallas_call | solution.py:86
  54.6 4.1 %collective-permute-done.4.refs_2_.refs_7_ = bf16[512,512]{1,0:T(8,128)(2,1)} collective-permute-done((bf16[512,512]{1,0:T(8,128)(2,1)}, bf16[512,512]{1,0:T(8,128)(2,1)}, u32[]{:S(2)}, u32[]{:S(2)}) %collective-permute-start.4) | collective-permute-done | bytes 524320 | tf_op jit(solution)/shard_map/ppermute | solution.py:30
  59.5 2.2 collective-permute-start.22
  61.8 5.0 %shard_map.47.refs_4_.refs_10_ = bf16[512,512]{1,0:T(8,128)(2,1)} custom-call(s32[512,1]{1,0:T(8,128)} %copy.11.start_ref, bf16[512,3072]{1,0:T(8,128)(2,1)} %q_ref.11, bf16[512,256]{1,0:T(8,128)(2,1)} %collective-permute-done.2.kp_ref.vp_ref, bf16[512,256]{1,0:T(8,128)(2,1)} %pad_maximum_fusion.1.ko_ref.vo_ref, ...), custom_call_target="tpu_custom_call" | custom-call | flops 999999986991104 | bytes 1 | tf_op jit(solution)/shard_map/pallas_call | solution.py:86
  70.8 1.8 collective-permute-start.23
  72.6 5.0 %shard_map.50.refs_5_.refs_12_ = bf16[512,512]{1,0:T(8,128)(2,1)} custom-call(s32[512,1]{1,0:T(8,128)} %copy.11.start_ref, bf16[512,3072]{1,0:T(8,128)(2,1)} %q_ref.11, bf16[512,256]{1,0:T(8,128)(2,1)} %collective-permute-done.2.kp_ref.vp_ref, bf16[512,256]{1,0:T(8,128)(2,1)} %pad_maximum_fusion.1.ko_ref.vo_ref, ...), custom_call_target="tpu_custom_call" | custom-call | flops 999999986991104 | bytes 1 | tf_op jit(solution)/shard_map/pallas_call | solution.py:86
  79.8 2.6 collective-permute-done.6.refs_4_.refs_11_
  83.3 2.2 collective-permute-start.24
  85.5 2.4 shard_map.52.refs_0_
  89.3 4.4 %collective-permute-done.13.refs_5_.refs_13_ = bf16[512,512]{1,0:T(8,128)(2,1)} collective-permute-done((bf16[512,512]{1,0:T(8,128)(2,1)}, bf16[512,512]{1,0:T(8,128)(2,1)}, u32[]{:S(2)}, u32[]{:S(2)}) %collective-permute-start.13) | collective-permute-done | bytes 524320 | tf_op jit(solution)/shard_map/ppermute | solution.py:30
  95.8 2.5 collective-permute-start.25
  98.4 2.3 shard_map.53.refs_1_
  100.7 3.4 %collective-permute-done.16.refs_3_ = bf16[512,512]{1,0:T(8,128)(2,1)} collective-permute-done((bf16[512,512]{1,0:T(8,128)(2,1)}, bf16[512,512]{1,0:T(8,128)(2,1)}, u32[]{:S(2)}, u32[]{:S(2)}) %collective-permute-start.16) | collective-permute-done | bytes 524320 | tf_op jit(solution)/shard_map/ppermute | solution.py:35
  104.6 1.9 broadcast_select_fusion.11
  106.5 1.8 collective-permute-start.26
  108.3 10.7 %shard_map.54.refs_10_ = bf16[768,9216]{1,0:T(8,128)(2,1)} custom-call(bf16[768,512]{1,0:T(8,128)(2,1)} %shard_map.52.refs_0_, bf16[768,512]{1,0:T(8,128)(2,1)} %shard_map.53.refs_1_, bf16[512,512]{1,0:T(8,128)(2,1)} %shard_map.46.refs_0_.refs_2_, bf16[512,512]{1,0:T(8,128)(2,1)} %collective-permute-done.1.refs_0_.refs_3_, ...), custom_call_target="tpu_custom_call" | custom-call | flops 999999986991104 | bytes 1 | tf_op jit(solution)/shard_map/pallas_call | solution.py:250
  122.8 11.9 %collective-permute-done.17.refs_2_.refs_6_ = bf16[512,512]{1,0:T(8,128)(2,1)} collective-permute-done((bf16[512,512]{1,0:T(8,128)(2,1)}, bf16[512,512]{1,0:T(8,128)(2,1)}, u32[]{:S(2)}, u32[]{:S(2)}) %collective-permute-start.17) | collective-permute-done | bytes 524320 | tf_op jit(solution)/shard_map/ppermute | solution.py:30
  135.7 2.1 broadcast_select_fusion.9
  138.1 8.0 %shard_map.55.refs_10_ = bf16[768,9216]{1,0:T(8,128)(2,1)} custom-call(bf16[768,512]{1,0:T(8,128)(2,1)} %shard_map.52.refs_0_, bf16[768,512]{1,0:T(8,128)(2,1)} %shard_map.53.refs_1_, bf16[512,512]{1,0:T(8,128)(2,1)} %collective-permute-done.3.refs_2_, bf16[512,512]{1,0:T(8,128)(2,1)} %collective-permute-done.16.refs_3_, ...), custom_call_target="tpu_custom_call", output_to_operand_aliasing={{}: (10, {})} | custom-call | flops 999999986991104 | bytes 1 | tf_op jit(solution)/shard_map/pallas_call | solution.py:250
  149.3 6.2 %collective-permute-done.33.refs_3_ = bf16[512,512]{1,0:T(8,128)(2,1)} collective-permute-done((bf16[512,512]{1,0:T(8,128)(2,1)}, bf16[512,512]{1,0:T(8,128)(2,1)}, u32[]{:S(2)}, u32[]{:S(2)}) %collective-permute-start.33) | collective-permute-done | bytes 524320 | tf_op jit(solution)/shard_map/ppermute | solution.py:35
  158.2 2.1 broadcast_select_fusion.7
  161.8 8.0 %shard_map.57.refs_10_ = bf16[768,9216]{1,0:T(8,128)(2,1)} custom-call(bf16[768,512]{1,0:T(8,128)(2,1)} %shard_map.52.refs_0_, bf16[768,512]{1,0:T(8,128)(2,1)} %shard_map.53.refs_1_, bf16[512,512]{1,0:T(8,128)(2,1)} %collective-permute-done.5.refs_2_, bf16[512,512]{1,0:T(8,128)(2,1)} %copy-done.4, ...), custom_call_target="tpu_custom_call", output_to_operand_aliasing={{}: (10, {})} | custom-call | flops 999999986991104 | bytes 1 | tf_op jit(solution)/shard_map/pallas_call | solution.py:250
  172.0 5.9 %collective-permute-done.39.refs_2_ = bf16[512,512]{1,0:T(8,128)(2,1)} collective-permute-done((bf16[512,512]{1,0:T(8,128)(2,1)}, bf16[512,512]{1,0:T(8,128)(2,1)}, u32[]{:S(2)}, u32[]{:S(2)}) %collective-permute-start.39) | collective-permute-done | bytes 524320 | tf_op jit(solution)/shard_map/ppermute | solution.py:35
  180.7 2.1 broadcast_select_fusion.5
  184.2 8.0 %shard_map.58.refs_14_.refs_10_ = bf16[768,9216]{1,0:T(8,128)(2,1)} custom-call(bf16[768,512]{1,0:T(8,128)(2,1)} %shard_map.52.refs_0_, bf16[768,512]{1,0:T(8,128)(2,1)} %shard_map.53.refs_1_, bf16[512,512]{1,0:T(8,128)(2,1)} %collective-permute-done.7.refs_2_, bf16[512,512]{1,0:T(8,128)(2,1)} %collective-permute-done.33.refs_3_, ...), custom_call_target="tpu_custom_call", output_to_operand_aliasing={{}: (10, {})} | custom-call | flops 999999986991104 | bytes 1 | tf_op jit(solution)/shard_map/pallas_call | solution.py:250
  194.5 5.9 %collective-permute-done.45.refs_2_ = bf16[512,512]{1,0:T(8,128)(2,1)} collective-permute-done((bf16[512,512]{1,0:T(8,128)(2,1)}, bf16[512,512]{1,0:T(8,128)(2,1)}, u32[]{:S(2)}, u32[]{:S(2)}) %collective-permute-start.45) | collective-permute-done | bytes 524320 | tf_op jit(solution)/shard_map/ppermute | solution.py:35
  205.5 6.2 %collective-permute-done.48.refs_6_ = bf16[512,512]{1,0:T(8,128)(2,1)} collective-permute-done((bf16[512,512]{1,0:T(8,128)(2,1)}, bf16[512,512]{1,0:T(8,128)(2,1)}, u32[]{:S(2)}, u32[]{:S(2)}) %collective-permute-start.48) | collective-permute-done | bytes 524320 | tf_op jit(solution)/shard_map/ppermute | solution.py:35
  214.1 1.9 broadcast_select_fusion.2
  217.2 2.3 shard_map.56.refs_0_
  220.5 2.4 collective-permute-done.51.refs_6_
  227.7 6.5 %collective-permute-done.50.refs_6_ = bf16[512,512]{1,0:T(8,128)(2,1)} collective-permute-done((bf16[512,512]{1,0:T(8,128)(2,1)}, bf16[512,512]{1,0:T(8,128)(2,1)}, u32[]{:S(2)}, u32[]{:S(2)}) %collective-permute-start.50) | collective-permute-done | bytes 524320 | tf_op jit(solution)/shard_map/ppermute | solution.py:35
  235.7 2.1 broadcast_select_fusion
  239.6 2.4 shard_map.59.refs_1_
  242.6 2.8 collective-permute-done.56.refs_3_
  247.9 2.7 maximum_select_fusion
  251.8 9.4 %shard_map.60.refs_11_ = f32[768,9216]{1,0:T(8,128)} custom-call(bf16[768,512]{1,0:T(8,128)(2,1)} %shard_map.56.refs_0_, bf16[768,512]{1,0:T(8,128)(2,1)} %shard_map.59.refs_1_, bf16[512,512]{1,0:T(8,128)(2,1)} %collective-permute-done.8.refs_0_.refs_2_, bf16[512,512]{1,0:T(8,128)(2,1)} %collective-permute-done.34.refs_0_.refs_3_, ...), custom_call_target="tpu_custom_call" | custom-call | flops 999999986991104 | bytes 1 | tf_op jit(solution)/shard_map/pallas_call | solution.py:250
  261.3 2.9 maximum_select_fusion.1
  264.2 7.5 %shard_map.61.refs_11_ = f32[768,9216]{1,0:T(8,128)} custom-call(bf16[768,512]{1,0:T(8,128)(2,1)} %shard_map.56.refs_0_, bf16[768,512]{1,0:T(8,128)(2,1)} %shard_map.59.refs_1_, bf16[512,512]{1,0:T(8,128)(2,1)} %collective-permute-done.39.refs_2_, bf16[512,512]{1,0:T(8,128)(2,1)} %collective-permute-done.56.refs_3_, ...), custom_call_target="tpu_custom_call", output_to_operand_aliasing={{}: (11, {})} | custom-call | flops 999999986991104 | bytes 1 | tf_op jit(solution)/shard_map/pallas_call | solution.py:250
  271.8 2.7 maximum_select_fusion.2
  274.9 7.5 %shard_map.62.refs_11_ = f32[768,9216]{1,0:T(8,128)} custom-call(bf16[768,512]{1,0:T(8,128)(2,1)} %shard_map.56.refs_0_, bf16[768,512]{1,0:T(8,128)(2,1)} %shard_map.59.refs_1_, bf16[512,512]{1,0:T(8,128)(2,1)} %collective-permute-done.42.refs_2_, bf16[512,512]{1,0:T(8,128)(2,1)} %collective-permute-done.61.refs_3_, ...), custom_call_target="tpu_custom_call", output_to_operand_aliasing={{}: (11, {})} | custom-call | flops 999999986991104 | bytes 1 | tf_op jit(solution)/shard_map/pallas_call | solution.py:250
  282.4 7.5 %shard_map.63 = f32[768,9216]{1,0:T(8,128)} custom-call(bf16[768,512]{1,0:T(8,128)(2,1)} %shard_map.56.refs_0_, bf16[768,512]{1,0:T(8,128)(2,1)} %shard_map.59.refs_1_, bf16[512,512]{1,0:T(8,128)(2,1)} %collective-permute-done.45.refs_2_, bf16[512,512]{1,0:T(8,128)(2,1)} %collective-permute-done.57.refs_3_, ...), custom_call_target="tpu_custom_call", output_to_operand_aliasing={{}: (11, {})} | custom-call | flops 999999986991104 | bytes 1 | tf_op jit(solution)/shard_map/pallas_call | solution.py:250
  (163 shorter events, 72.6 us)
Async XLA Ops:
  6.0 13.3 %collective-permute-start.2 = (bf16[512,256]{1,0:T(8,128)(2,1)}, bf16[512,256]{1,0:T(8,128)(2,1)}, u32[]{:S(2)}, u32[]{:S(2)}) collective-permute-start(bf16[512,256]{1,0:T(8,128)(2,1)} %pad_maximum_fusion.1.ko_ref.vo_ref), channel_id=1, source_target_pairs={{0,1},{1,2},{2,3},{4,5},{5,6},{6,7},{8,9},{9,10},{10,11},{12,13},{... | collective-permute-start | bytes 786440 | tf_op jit(solution)/shard_map/ppermute | solution.py:24
  16.4 13.5 %collective-permute-start.1 = (bf16[512,512]{1,0:T(8,128)(2,1)}, bf16[512,512]{1,0:T(8,128)(2,1)}, u32[]{:S(2)}, u32[]{:S(2)}) collective-permute-start(bf16[512,512]{1,0:T(8,128)(2,1)} %shard_map.46.refs_0_.refs_2_), channel_id=1, source_target_pairs={{0,1},{1,2},{2,3},{3,0},{4,5},{5,6},{6,7},{7,4},{8,9},{9,10},{10,1... | collective-permute-start | bytes 1572872 | tf_op jit(solution)/shard_map/ppermute | solution.py:30
  18.0 11.9 %collective-permute-start.3 = (bf16[512,512]{1,0:T(8,128)(2,1)}, bf16[512,512]{1,0:T(8,128)(2,1)}, u32[]{:S(2)}, u32[]{:S(2)}) collective-permute-start(bf16[512,512]{1,0:T(8,128)(2,1)} %shard_map.46.refs_0_.refs_2_), channel_id=1, source_target_pairs={{0,8},{4,12},{8,0},{12,4},{1,9},{5,13},{9,1},{13,5},{2,10},{6,14},... | collective-permute-start | bytes 1572872 | tf_op jit(solution)/shard_map/ppermute | solution.py:35
  25.8 19.8 %collective-permute-start.10 = (bf16[512,512]{1,0:T(8,128)(2,1)}, bf16[512,512]{1,0:T(8,128)(2,1)}, u32[]{:S(2)}, u32[]{:S(2)}) collective-permute-start(bf16[512,512]{1,0:T(8,128)(2,1)} %shard_map.49.refs_1_.refs_4_), channel_id=1, source_target_pairs={{0,8},{4,12},{8,0},{12,4},{1,9},{5,13},{9,1},{13,5},{2,10},{6,14},... | collective-permute-start | bytes 1572872 | tf_op jit(solution)/shard_map/ppermute | solution.py:35
  26.0 19.6 %collective-permute-start.9 = (bf16[512,512]{1,0:T(8,128)(2,1)}, bf16[512,512]{1,0:T(8,128)(2,1)}, u32[]{:S(2)}, u32[]{:S(2)}) collective-permute-start(bf16[512,512]{1,0:T(8,128)(2,1)} %shard_map.49.refs_1_.refs_4_), channel_id=1, source_target_pairs={{0,1},{1,2},{2,3},{3,0},{4,5},{5,6},{6,7},{7,4},{8,9},{9,10},{10,1... | collective-permute-start | bytes 1572872 | tf_op jit(solution)/shard_map/ppermute | solution.py:30
  30.8 14.8 %collective-permute-start.20 = (bf16[512,512]{1,0:T(8,128)(2,1)}, bf16[512,512]{1,0:T(8,128)(2,1)}, u32[]{:S(2)}, u32[]{:S(2)}) collective-permute-start(bf16[512,512]{1,0:T(8,128)(2,1)} %broadcast_select_fusion.17), channel_id=1, source_target_pairs={{0,4},{4,0},{8,12},{12,8},{1,5},{5,1},{9,13},{13,9},{2,6},{6,2},{1... | collective-permute-start | bytes 1572872 | tf_op jit(solution)/shard_map/ppermute | solution.py:35
  43.0 15.7 %collective-permute-start.4 = (bf16[512,512]{1,0:T(8,128)(2,1)}, bf16[512,512]{1,0:T(8,128)(2,1)}, u32[]{:S(2)}, u32[]{:S(2)}) collective-permute-start(bf16[512,512]{1,0:T(8,128)(2,1)} %shard_map.48.refs_2_.refs_6_), channel_id=1, source_target_pairs={{0,1},{1,2},{2,3},{3,0},{4,5},{5,6},{6,7},{7,4},{8,9},{9,10},{10,1... | collective-permute-start | bytes 1572872 | tf_op jit(solution)/shard_map/ppermute | solution.py:30
  44.3 14.4 %collective-permute-start.5 = (bf16[512,512]{1,0:T(8,128)(2,1)}, bf16[512,512]{1,0:T(8,128)(2,1)}, u32[]{:S(2)}, u32[]{:S(2)}) collective-permute-start(bf16[512,512]{1,0:T(8,128)(2,1)} %shard_map.48.refs_2_.refs_6_), channel_id=1, source_target_pairs={{0,8},{4,12},{8,0},{12,4},{1,9},{5,13},{9,1},{13,5},{2,10},{6,14},... | collective-permute-start | bytes 1572872 | tf_op jit(solution)/shard_map/ppermute | solution.py:35
  46.5 12.2 %collective-permute-start.21 = (bf16[512,512]{1,0:T(8,128)(2,1)}, bf16[512,512]{1,0:T(8,128)(2,1)}, u32[]{:S(2)}, u32[]{:S(2)}) collective-permute-start(bf16[512,512]{1,0:T(8,128)(2,1)} %broadcast_select_fusion.16), channel_id=1, source_target_pairs={{0,4},{4,0},{8,12},{12,8},{1,5},{5,1},{9,13},{13,9},{2,6},{6,2},{1... | collective-permute-start | bytes 1572872 | tf_op jit(solution)/shard_map/ppermute | solution.py:35
  53.1 16.8 %collective-permute-start.11 = (bf16[512,512]{1,0:T(8,128)(2,1)}, bf16[512,512]{1,0:T(8,128)(2,1)}, u32[]{:S(2)}, u32[]{:S(2)}) collective-permute-start(bf16[512,512]{1,0:T(8,128)(2,1)} %shard_map.51.refs_3_.refs_8_), channel_id=1, source_target_pairs={{0,1},{1,2},{2,3},{3,0},{4,5},{5,6},{6,7},{7,4},{8,9},{9,10},{10,1... | collective-permute-start | bytes 1572872 | tf_op jit(solution)/shard_map/ppermute | solution.py:30
  54.4 15.5 %collective-permute-start.12 = (bf16[512,512]{1,0:T(8,128)(2,1)}, bf16[512,512]{1,0:T(8,128)(2,1)}, u32[]{:S(2)}, u32[]{:S(2)}) collective-permute-start(bf16[512,512]{1,0:T(8,128)(2,1)} %shard_map.51.refs_3_.refs_8_), channel_id=1, source_target_pairs={{0,8},{4,12},{8,0},{12,4},{1,9},{5,13},{9,1},{13,5},{2,10},{6,14},... | collective-permute-start | bytes 1572872 | tf_op jit(solution)/shard_map/ppermute | solution.py:35
  66.8 15.7 %collective-permute-start.6 = (bf16[512,512]{1,0:T(8,128)(2,1)}, bf16[512,512]{1,0:T(8,128)(2,1)}, u32[]{:S(2)}, u32[]{:S(2)}) collective-permute-start(bf16[512,512]{1,0:T(8,128)(2,1)} %shard_map.47.refs_4_.refs_10_), channel_id=1, source_target_pairs={{0,1},{1,2},{2,3},{3,0},{4,5},{5,6},{6,7},{7,4},{8,9},{9,10},{10,1... | collective-permute-start | bytes 1572872 | tf_op jit(solution)/shard_map/ppermute | solution.py:30
  67.9 14.5 %collective-permute-start.7 = (bf16[512,512]{1,0:T(8,128)(2,1)}, bf16[512,512]{1,0:T(8,128)(2,1)}, u32[]{:S(2)}, u32[]{:S(2)}) collective-permute-start(bf16[512,512]{1,0:T(8,128)(2,1)} %shard_map.47.refs_4_.refs_10_), channel_id=1, source_target_pairs={{0,8},{4,12},{8,0},{12,4},{1,9},{5,13},{9,1},{13,5},{2,10},{6,14},... | collective-permute-start | bytes 1572872 | tf_op jit(solution)/shard_map/ppermute | solution.py:35
  77.6 16.1 %collective-permute-start.13 = (bf16[512,512]{1,0:T(8,128)(2,1)}, bf16[512,512]{1,0:T(8,128)(2,1)}, u32[]{:S(2)}, u32[]{:S(2)}) collective-permute-start(bf16[512,512]{1,0:T(8,128)(2,1)} %shard_map.50.refs_5_.refs_12_), channel_id=1, source_target_pairs={{0,1},{1,2},{2,3},{3,0},{4,5},{5,6},{6,7},{7,4},{8,9},{9,10},{10,1... | collective-permute-start | bytes 1572872 | tf_op jit(solution)/shard_map/ppermute | solution.py:30
  78.5 15.1 %collective-permute-start.14 = (bf16[512,512]{1,0:T(8,128)(2,1)}, bf16[512,512]{1,0:T(8,128)(2,1)}, u32[]{:S(2)}, u32[]{:S(2)}) collective-permute-start(bf16[512,512]{1,0:T(8,128)(2,1)} %shard_map.50.refs_5_.refs_12_), channel_id=1, source_target_pairs={{0,8},{4,12},{8,0},{12,4},{1,9},{5,13},{9,1},{13,5},{2,10},{6,14},... | collective-permute-start | bytes 1572872 | tf_op jit(solution)/shard_map/ppermute | solution.py:35
  83.3 11.7 %collective-permute-start.24 = (bf16[512,512]{1,0:T(8,128)(2,1)}, bf16[512,512]{1,0:T(8,128)(2,1)}, u32[]{:S(2)}, u32[]{:S(2)}) collective-permute-start(bf16[512,512]{1,0:T(8,128)(2,1)} %broadcast_select_fusion.13), channel_id=1, source_target_pairs={{0,4},{4,0},{8,12},{12,8},{1,5},{5,1},{9,13},{13,9},{2,6},{6,2},{1... | collective-permute-start | bytes 1572872 | tf_op jit(solution)/shard_map/ppermute | solution.py:35
  87.9 16.2 %collective-permute-start.16 = (bf16[512,512]{1,0:T(8,128)(2,1)}, bf16[512,512]{1,0:T(8,128)(2,1)}, u32[]{:S(2)}, u32[]{:S(2)}) collective-permute-start(bf16[512,512]{1,0:T(8,128)(2,1)} %collective-permute-done.1.refs_0_.refs_3_), channel_id=1, source_target_pairs={{0,8},{4,12},{8,0},{12,4},{1,9},{5,13},{9,1},{13,5},{2,10},{6,14},... | collective-permute-start | bytes 1572872 | tf_op jit(solution)/shard_map/ppermute | solution.py:35
  89.3 15.3 %collective-permute-start.8 = (bf16[512,512]{1,0:T(8,128)(2,1)}, bf16[512,512]{1,0:T(8,128)(2,1)}, u32[]{:S(2)}, u32[]{:S(2)}) collective-permute-start(bf16[512,512]{1,0:T(8,128)(2,1)} %collective-permute-done.1.refs_0_.refs_3_), channel_id=1, source_target_pairs={{0,1},{1,2},{2,3},{3,0},{4,5},{5,6},{6,7},{7,4},{8,9},{9,10},{10,1... | collective-permute-start | bytes 1572872 | tf_op jit(solution)/shard_map/ppermute | solution.py:30
  93.7 26.5 %collective-permute-start.15 = (bf16[512,512]{1,0:T(8,128)(2,1)}, bf16[512,512]{1,0:T(8,128)(2,1)}, u32[]{:S(2)}, u32[]{:S(2)}) collective-permute-start(bf16[512,512]{1,0:T(8,128)(2,1)} %collective-permute-done.9.refs_1_.refs_5_), channel_id=1, source_target_pairs={{0,1},{1,2},{2,3},{3,0},{4,5},{5,6},{6,7},{7,4},{8,9},{9,10},{10,1... | collective-permute-start | bytes 1572872 | tf_op jit(solution)/shard_map/ppermute | solution.py:30
  93.7 26.5 %collective-permute-start.18 = (bf16[512,512]{1,0:T(8,128)(2,1)}, bf16[512,512]{1,0:T(8,128)(2,1)}, u32[]{:S(2)}, u32[]{:S(2)}) collective-permute-start(bf16[512,512]{1,0:T(8,128)(2,1)} %collective-permute-done.9.refs_1_.refs_5_), channel_id=1, source_target_pairs={{0,8},{4,12},{8,0},{12,4},{1,9},{5,13},{9,1},{13,5},{2,10},{6,14},... | collective-permute-start | bytes 1572872 | tf_op jit(solution)/shard_map/ppermute | solution.py:35
  106.5 13.6 %collective-permute-start.26 = (bf16[512,512]{1,0:T(8,128)(2,1)}, bf16[512,512]{1,0:T(8,128)(2,1)}, u32[]{:S(2)}, u32[]{:S(2)}) collective-permute-start(bf16[512,512]{1,0:T(8,128)(2,1)} %broadcast_select_fusion.11), channel_id=1, source_target_pairs={{0,4},{4,0},{8,12},{12,8},{1,5},{5,1},{9,13},{13,9},{2,6},{6,2},{1... | collective-permute-start | bytes 1572872 | tf_op jit(solution)/shard_map/ppermute | solution.py:35
  119.0 15.7 %collective-permute-start.17 = (bf16[512,512]{1,0:T(8,128)(2,1)}, bf16[512,512]{1,0:T(8,128)(2,1)}, u32[]{:S(2)}, u32[]{:S(2)}) collective-permute-start(bf16[512,512]{1,0:T(8,128)(2,1)} %collective-permute-done.4.refs_2_.refs_7_), channel_id=1, source_target_pairs={{0,1},{1,2},{2,3},{3,0},{4,5},{5,6},{6,7},{7,4},{8,9},{9,10},{10,1... | collective-permute-start | bytes 1572872 | tf_op jit(solution)/shard_map/ppermute | solution.py:30
  119.1 15.7 %collective-permute-start.27 = (bf16[512,512]{1,0:T(8,128)(2,1)}, bf16[512,512]{1,0:T(8,128)(2,1)S(1)}, u32[]{:S(2)}, u32[]{:S(2)}) collective-permute-start(bf16[512,512]{1,0:T(8,128)(2,1)} %collective-permute-done.4.refs_2_.refs_7_), channel_id=1, source_target_pairs={{0,8},{4,12},{8,0},{12,4},{1,9},{5,13},{9,1},{13,5},{2,10},{6,14},... | collective-permute-start | bytes 1572872 | tf_op jit(solution)/shard_map/ppermute | solution.py:35
  121.2 14.5 %collective-permute-start.29 = (bf16[512,512]{1,0:T(8,128)(2,1)S(1)}, bf16[512,512]{1,0:T(8,128)(2,1)S(1)}, u32[]{:S(2)}, u32[]{:S(2)}) collective-permute-start(bf16[512,512]{1,0:T(8,128)(2,1)S(1)} %broadcast_select_fusion.10), channel_id=1, source_target_pairs={{0,4},{4,0},{8,12},{12,8},{1,5},{5,1},{9,13},{13,9},{2,6},{6,2},{1... | collective-permute-start | bytes 1572872 | tf_op jit(solution)/shard_map/ppermute | solution.py:35
  121.6 24.5 %collective-permute-start.30 = (bf16[512,512]{1,0:T(8,128)(2,1)}, bf16[512,512]{1,0:T(8,128)(2,1)}, u32[]{:S(2)}, u32[]{:S(2)}) collective-permute-start(bf16[512,512]{1,0:T(8,128)(2,1)} %collective-permute-done.11.refs_3_.refs_9_), channel_id=1, source_target_pairs={{0,8},{4,12},{8,0},{12,4},{1,9},{5,13},{9,1},{13,5},{2,10},{6,14},... | collective-permute-start | bytes 1572872 | tf_op jit(solution)/shard_map/ppermute | solution.py:35
  122.1 24.0 %collective-permute-start.19 = (bf16[512,512]{1,0:T(8,128)(2,1)}, bf16[512,512]{1,0:T(8,128)(2,1)}, u32[]{:S(2)}, u32[]{:S(2)}) collective-permute-start(bf16[512,512]{1,0:T(8,128)(2,1)} %collective-permute-done.11.refs_3_.refs_9_), channel_id=1, source_target_pairs={{0,1},{1,2},{2,3},{3,0},{4,5},{5,6},{6,7},{7,4},{8,9},{9,10},{10,1... | collective-permute-start | bytes 1572872 | tf_op jit(solution)/shard_map/ppermute | solution.py:30
  134.7 20.7 %collective-permute-start.33 = (bf16[512,512]{1,0:T(8,128)(2,1)}, bf16[512,512]{1,0:T(8,128)(2,1)}, u32[]{:S(2)}, u32[]{:S(2)}) collective-permute-start(bf16[512,512]{1,0:T(8,128)(2,1)} %collective-permute-done.6.refs_4_.refs_11_), channel_id=1, source_target_pairs={{0,8},{4,12},{8,0},{12,4},{1,9},{5,13},{9,1},{13,5},{2,10},{6,14},... | collective-permute-start | bytes 1572872 | tf_op jit(solution)/shard_map/ppermute | solution.py:35
  135.7 21.5 %collective-permute-start.28 = (bf16[512,512]{1,0:T(8,128)(2,1)}, bf16[512,512]{1,0:T(8,128)(2,1)}, u32[]{:S(2)}, u32[]{:S(2)}) collective-permute-start(bf16[512,512]{1,0:T(8,128)(2,1)} %collective-permute-done.6.refs_4_.refs_11_), channel_id=1, source_target_pairs={{0,1},{1,2},{2,3},{3,0},{4,5},{5,6},{6,7},{7,4},{8,9},{9,10},{10,1... | collective-permute-start | bytes 1572872 | tf_op jit(solution)/shard_map/ppermute | solution.py:30
  148.3 21.5 %collective-permute-start.36 = (bf16[512,512]{1,0:T(8,128)(2,1)}, bf16[512,512]{1,0:T(8,128)(2,1)}, u32[]{:S(2)}, u32[]{:S(2)}) collective-permute-start(bf16[512,512]{1,0:T(8,128)(2,1)} %collective-permute-done.13.refs_5_.refs_13_), channel_id=1, source_target_pairs={{0,8},{4,12},{8,0},{12,4},{1,9},{5,13},{9,1},{13,5},{2,10},{6,14},... | collective-permute-start | bytes 1572872 | tf_op jit(solution)/shard_map/ppermute | solution.py:35
  149.3 20.5 %collective-permute-start.31 = (bf16[512,512]{1,0:T(8,128)(2,1)}, bf16[512,512]{1,0:T(8,128)(2,1)}, u32[]{:S(2)}, u32[]{:S(2)}) collective-permute-start(bf16[512,512]{1,0:T(8,128)(2,1)} %collective-permute-done.13.refs_5_.refs_13_), channel_id=1, source_target_pairs={{0,1},{1,2},{2,3},{3,0},{4,5},{5,6},{6,7},{7,4},{8,9},{9,10},{10,1... | collective-permute-start | bytes 1572872 | tf_op jit(solution)/shard_map/ppermute | solution.py:30
  157.2 20.8 %collective-permute-start.39 = (bf16[512,512]{1,0:T(8,128)(2,1)}, bf16[512,512]{1,0:T(8,128)(2,1)}, u32[]{:S(2)}, u32[]{:S(2)}) collective-permute-start(bf16[512,512]{1,0:T(8,128)(2,1)} %collective-permute-done.8.refs_0_.refs_2_), channel_id=1, source_target_pairs={{0,8},{4,12},{8,0},{12,4},{1,9},{5,13},{9,1},{13,5},{2,10},{6,14},... | collective-permute-start | bytes 1572872 | tf_op jit(solution)/shard_map/ppermute | solution.py:35
  158.2 21.5 %collective-permute-start.34 = (bf16[512,512]{1,0:T(8,128)(2,1)}, bf16[512,512]{1,0:T(8,128)(2,1)}, u32[]{:S(2)}, u32[]{:S(2)}) collective-permute-start(bf16[512,512]{1,0:T(8,128)(2,1)} %collective-permute-done.8.refs_0_.refs_2_), channel_id=1, source_target_pairs={{0,1},{1,2},{2,3},{3,0},{4,5},{5,6},{6,7},{7,4},{8,9},{9,10},{10,1... | collective-permute-start | bytes 1572872 | tf_op jit(solution)/shard_map/ppermute | solution.py:30
  171.0 21.3 %collective-permute-start.42 = (bf16[512,512]{1,0:T(8,128)(2,1)}, bf16[512,512]{1,0:T(8,128)(2,1)}, u32[]{:S(2)}, u32[]{:S(2)}) collective-permute-start(bf16[512,512]{1,0:T(8,128)(2,1)} %collective-permute-done.15.refs_1_.refs_4_), channel_id=1, source_target_pairs={{0,8},{4,12},{8,0},{12,4},{1,9},{5,13},{9,1},{13,5},{2,10},{6,14},... | collective-permute-start | bytes 1572872 | tf_op jit(solution)/shard_map/ppermute | solution.py:35
  171.8 20.5 %collective-permute-start.37 = (bf16[512,512]{1,0:T(8,128)(2,1)}, bf16[512,512]{1,0:T(8,128)(2,1)}, u32[]{:S(2)}, u32[]{:S(2)}) collective-permute-start(bf16[512,512]{1,0:T(8,128)(2,1)} %collective-permute-done.15.refs_1_.refs_4_), channel_id=1, source_target_pairs={{0,1},{1,2},{2,3},{3,0},{4,5},{5,6},{6,7},{7,4},{8,9},{9,10},{10,1... | collective-permute-start | bytes 1572872 | tf_op jit(solution)/shard_map/ppermute | solution.py:30
  179.7 20.8 %collective-permute-start.45 = (bf16[512,512]{1,0:T(8,128)(2,1)}, bf16[512,512]{1,0:T(8,128)(2,1)}, u32[]{:S(2)}, u32[]{:S(2)}) collective-permute-start(bf16[512,512]{1,0:T(8,128)(2,1)} %collective-permute-done.17.refs_2_.refs_6_), channel_id=1, source_target_pairs={{0,8},{4,12},{8,0},{12,4},{1,9},{5,13},{9,1},{13,5},{2,10},{6,14},... | collective-permute-start | bytes 1572872 | tf_op jit(solution)/shard_map/ppermute | solution.py:35
  180.6 21.5 %collective-permute-start.40 = (bf16[512,512]{1,0:T(8,128)(2,1)}, bf16[512,512]{1,0:T(8,128)(2,1)}, u32[]{:S(2)}, u32[]{:S(2)}) collective-permute-start(bf16[512,512]{1,0:T(8,128)(2,1)} %collective-permute-done.17.refs_2_.refs_6_), channel_id=1, source_target_pairs={{0,1},{1,2},{2,3},{3,0},{4,5},{5,6},{6,7},{7,4},{8,9},{9,10},{10,1... | collective-permute-start | bytes 1572872 | tf_op jit(solution)/shard_map/ppermute | solution.py:30
  193.5 18.2 %collective-permute-start.48 = (bf16[512,512]{1,0:T(8,128)(2,1)}, bf16[512,512]{1,0:T(8,128)(2,1)}, u32[]{:S(2)}, u32[]{:S(2)}) collective-permute-start(bf16[512,512]{1,0:T(8,128)(2,1)} %collective-permute-done.19.refs_3_.refs_8_), channel_id=1, source_target_pairs={{0,8},{4,12},{8,0},{12,4},{1,9},{5,13},{9,1},{13,5},{2,10},{6,14},... | collective-permute-start | bytes 1572872 | tf_op jit(solution)/shard_map/ppermute | solution.py:35
  194.2 19.1 %collective-permute-start.43 = (bf16[512,512]{1,0:T(8,128)(2,1)}, bf16[512,512]{1,0:T(8,128)(2,1)S(1)}, u32[]{:S(2)}, u32[]{:S(2)}) collective-permute-start(bf16[512,512]{1,0:T(8,128)(2,1)} %collective-permute-done.19.refs_3_.refs_8_), channel_id=1, source_target_pairs={{0,1},{1,2},{2,3},{3,0},{4,5},{5,6},{6,7},{7,4},{8,9},{9,10},{10,1... | collective-permute-start | bytes 1572872 | tf_op jit(solution)/shard_map/ppermute | solution.py:30
  204.5 18.4 %collective-permute-start.51 = (bf16[512,512]{1,0:T(8,128)(2,1)}, bf16[512,512]{1,0:T(8,128)(2,1)}, u32[]{:S(2)}, u32[]{:S(2)}) collective-permute-start(bf16[512,512]{1,0:T(8,128)(2,1)} %collective-permute-done.28.refs_4_.refs_10_), channel_id=1, source_target_pairs={{0,8},{4,12},{8,0},{12,4},{1,9},{5,13},{9,1},{13,5},{2,10},{6,14},... | collective-permute-start | bytes 1572872 | tf_op jit(solution)/shard_map/ppermute | solution.py:35
  205.5 19.1 %collective-permute-start.46 = (bf16[512,512]{1,0:T(8,128)(2,1)}, bf16[512,512]{1,0:T(8,128)(2,1)}, u32[]{:S(2)}, u32[]{:S(2)}) collective-permute-start(bf16[512,512]{1,0:T(8,128)(2,1)} %collective-permute-done.28.refs_4_.refs_10_), channel_id=1, source_target_pairs={{0,1},{1,2},{2,3},{3,0},{4,5},{5,6},{6,7},{7,4},{8,9},{9,10},{10,1... | collective-permute-start | bytes 1572872 | tf_op jit(solution)/shard_map/ppermute | solution.py:30
  219.5 14.7 %collective-permute-start.50 = (bf16[512,512]{1,0:T(8,128)(2,1)}, bf16[512,512]{1,0:T(8,128)(2,1)}, u32[]{:S(2)}, u32[]{:S(2)}) collective-permute-start(bf16[512,512]{1,0:T(8,128)(2,1)} %collective-permute-done.31.refs_5_.refs_12_), channel_id=1, source_target_pairs={{0,8},{4,12},{8,0},{12,4},{1,9},{5,13},{9,1},{13,5},{2,10},{6,14},... | collective-permute-start | bytes 1572872 | tf_op jit(solution)/shard_map/ppermute | solution.py:35
  220.5 15.2 %collective-permute-start.49 = (bf16[512,512]{1,0:T(8,128)(2,1)}, bf16[512,512]{1,0:T(8,128)(2,1)S(1)}, u32[]{:S(2)}, u32[]{:S(2)}) collective-permute-start(bf16[512,512]{1,0:T(8,128)(2,1)} %collective-permute-done.31.refs_5_.refs_12_), channel_id=1, source_target_pairs={{0,1},{1,2},{2,3},{3,0},{4,5},{5,6},{6,7},{7,4},{8,9},{9,10},{10,1... | collective-permute-start | bytes 1572872 | tf_op jit(solution)/shard_map/ppermute | solution.py:30
  226.6 18.8 %collective-permute-start.56 = (bf16[512,512]{1,0:T(8,128)(2,1)}, bf16[512,512]{1,0:T(8,128)(2,1)}, u32[]{:S(2)}, u32[]{:S(2)}) collective-permute-start(bf16[512,512]{1,0:T(8,128)(2,1)} %collective-permute-done.34.refs_0_.refs_3_), channel_id=1, source_target_pairs={{0,8},{4,12},{8,0},{12,4},{1,9},{5,13},{9,1},{13,5},{2,10},{6,14},... | collective-permute-start | bytes 1572872 | tf_op jit(solution)/shard_map/ppermute | solution.py:35
  227.7 19.4 %collective-permute-start.55 = (bf16[512,512]{1,0:T(8,128)(2,1)}, bf16[512,512]{1,0:T(8,128)(2,1)}, u32[]{:S(2)}, u32[]{:S(2)}) collective-permute-start(bf16[512,512]{1,0:T(8,128)(2,1)} %collective-permute-done.48.refs_6_), channel_id=1, source_target_pairs={{0,1},{1,2},{2,3},{3,0},{4,5},{5,6},{6,7},{7,4},{8,9},{9,10},{10,1... | collective-permute-start | bytes 1572872 | tf_op jit(solution)/shard_map/ppermute | solution.py:30
  242.0 19.3 %collective-permute-start.61 = (bf16[512,512]{1,0:T(8,128)(2,1)}, bf16[512,512]{1,0:T(8,128)(2,1)}, u32[]{:S(2)}, u32[]{:S(2)}) collective-permute-start(bf16[512,512]{1,0:T(8,128)(2,1)} %collective-permute-done.37.refs_1_.refs_5_), channel_id=1, source_target_pairs={{0,8},{4,12},{8,0},{12,4},{1,9},{5,13},{9,1},{13,5},{2,10},{6,14},... | collective-permute-start | bytes 1572872 | tf_op jit(solution)/shard_map/ppermute | solution.py:35
  242.6 18.7 %collective-permute-start.62 = (bf16[512,512]{1,0:T(8,128)(2,1)}, bf16[512,512]{1,0:T(8,128)(2,1)}, u32[]{:S(2)}, u32[]{:S(2)}) collective-permute-start(bf16[512,512]{1,0:T(8,128)(2,1)} %collective-permute-done.51.refs_6_), channel_id=1, source_target_pairs={{0,1},{1,2},{2,3},{3,0},{4,5},{5,6},{6,7},{7,4},{8,9},{9,10},{10,1... | collective-permute-start | bytes 1572872 | tf_op jit(solution)/shard_map/ppermute | solution.py:30
  247.1 24.7 %collective-permute-start.57 = (bf16[512,512]{1,0:T(8,128)(2,1)}, bf16[512,512]{1,0:T(8,128)(2,1)}, u32[]{:S(2)}, u32[]{:S(2)}) collective-permute-start(bf16[512,512]{1,0:T(8,128)(2,1)} %collective-permute-done.40.refs_2_.refs_7_), channel_id=1, source_target_pairs={{0,8},{4,12},{8,0},{12,4},{1,9},{5,13},{9,1},{13,5},{2,10},{6,14},... | collective-permute-start | bytes 1572872 | tf_op jit(solution)/shard_map/ppermute | solution.py:35
  247.9 23.8 %collective-permute-start.58 = (bf16[512,512]{1,0:T(8,128)(2,1)}, bf16[512,512]{1,0:T(8,128)(2,1)}, u32[]{:S(2)}, u32[]{:S(2)}) collective-permute-start(bf16[512,512]{1,0:T(8,128)(2,1)} %collective-permute-done.50.refs_6_), channel_id=1, source_target_pairs={{0,1},{1,2},{2,3},{3,0},{4,5},{5,6},{6,7},{7,4},{8,9},{9,10},{10,1... | collective-permute-start | bytes 1572872 | tf_op jit(solution)/shard_map/ppermute | solution.py:30
  (35 other events, 274.5 us)
where the time goes:
time: 292 us; the launch traced here: 290 us
  Pallas kernels  106 us (36%)
  waiting for transfers between devices  78.1 us (27%)
  starting transfers between devices  67.6 us (23%)
  other arithmetic  33 us (11%)
  local copies, waits for them, and re-layouts  5.09 us (2%)
    pallas_call x8, Pallas kernels, gram(): pl.pallas_call(functools.partial(gram_kernel, runs, places, starts, depth...  66.6 us
    ppermute x42, starting transfers between devices, over_tensor(): return lax.ppermute(value, 'tensor', [(t, t ^ bit) for t in range(count)])  50.6 us
    ppermute x42, waiting for transfers between devices, over_tensor(): return lax.ppermute(value, 'tensor', [(t, t ^ bit) for t in range(count)])  39.4 us
    ppermute x21, waiting for transfers between devices, from_behind(): return lax.ppermute(value, axis, pairs)  38.7 us
    select_n x21, other arithmetic, per_device(): sent = jnp.where(even, *[jnp.concatenate(x, 1) for x in pair])  32.2 us
    pallas_call x6, Pallas kernels, attend(): pl.pallas_call(attend_kernel, grid=(heads // step,), out_shape=jax.ShapeD...  29.8 us
    pallas_call x4, Pallas kernels, rows_of(): pl.pallas_call(functools.partial(rows_kernel, widths, rows), out_shape=ja...  9.32 us
    ppermute x21, starting transfers between devices, from_behind(): return lax.ppermute(value, axis, pairs)  9.07 us
  transfers between devices with their start and end apart: 65, of which 22 were waited for; matrix products, arithmetic and copies ran while one was open for 11% of the time, Pallas kernels for 34%

commit v1 on v0

--- a/solution.py
+++ b/solution.py
@@ -147,11 +147,11 @@
     )(place, *pieces)
 
 
-def gram_kernel(runs, tiles, starts, depth, scale, kept, added, *refs):
+def gram_kernel(runs, tiles, counts, starts, depth, scale, kept, added, in_place, *refs):
     lefts, refs = refs[:runs], refs[runs:]
-    data, refs = refs[: runs * len(tiles)], list(refs[runs * len(tiles) :])
+    data, refs = refs[: len(starts)], list(refs[len(starts) :])
     old_ref = refs.pop(0) if added else None
-    if kept:
+    if kept and not in_place:
         refs.pop(0)
     out_ref, left, b_buf, o_buf, left_sem, b_sem, o_sem = refs[:7]
     c_buf, c_sem = refs[7:] if added else (None, None)
@@ -162,11 +162,11 @@
         width = tiles[i][1]
         copies = [
             pltpu.make_async_copy(
-                data[i * runs + run].at[:, pl.ds(starts[i * runs + run], width)],
+                data[n].at[:, pl.ds(starts[n], width)],
                 b_buf.at[slot, pl.ds(run * depth, depth), pl.ds(0, width)],
                 b_sem.at[slot, run],
             )
-            for run in range(runs)
+            for run, n in zip(range(runs - counts[i], runs), range(sum(counts[:i]), sum(counts)))
         ]
         if added:
             copies.append(
@@ -209,15 +209,15 @@
         if i >= slots:
             out_copy(i - slots).wait()
 
-        def block(part, slot=slot, width=width):
+        def block(part, slot=slot, width=width, seen=slice((runs - counts[i]) * depth, None)):
             result = scale * jnp.dot(
-                left[part, :], b_buf[slot, :, :width], preferred_element_type=jnp.float32
+                left[part, seen], b_buf[slot, seen, :width], preferred_element_type=jnp.float32
             )
             if added:
                 result = result + c_buf[slot, part, :width].astype(jnp.float32)
             o_buf[slot, part, :width] = result.astype(o_buf.dtype)
 
-        if added:
+        if added and not in_place:
             block(slice(None))
         else:
             pl.loop(0, left.shape[0] // ROWS)(lambda n: block(pl.ds(pl.multiple_of(n * ROWS, ROWS), ROWS)))
@@ -226,15 +226,16 @@
         out_copy(i).wait()
 
 
-def gram(out, lefts, tiles, width, columns, scale, kind, old=None):
+def gram(out, lefts, tiles, width, columns, scale, kind, old=None, add=False):
     runs = len(lefts)
     rows, depth = lefts[0].shape
     places = [(first, width) for first, _ in tiles]
     data = [x for _, arrays in tiles for x, _ in arrays]
     starts = [x for _, arrays in tiles for _, x in arrays]
-    kept, added = out is not None, old is not None
+    counts = [len(arrays) for _, arrays in tiles]
+    kept, added = out is not None, add or old is not None
     any_spec = pl.BlockSpec(memory_space=pltpu.HBM)
-    operands = [*lefts, *data] + ([old] if added else []) + ([out] if kept else [])
+    operands = [*lefts, *data] + ([] if old is None else [old]) + ([out] if kept else [])
     slots = min(4, len(tiles))
     scratch = [
         pltpu.VMEM((rows, runs * depth), jnp.bfloat16),
@@ -245,10 +246,10 @@
         pltpu.SemaphoreType.DMA((slots,)),
     ]
     if added:
-        scratch += [pltpu.VMEM((slots, rows, width), old.dtype), pltpu.SemaphoreType.DMA((slots,))]
+        scratch += [pltpu.VMEM((slots, rows, width), out.dtype if old is None else old.dtype), pltpu.SemaphoreType.DMA((slots,))]
     total = sum(width for _, width in places)
     return pl.pallas_call(
-        functools.partial(gram_kernel, runs, places, starts, depth, scale, kept, added),
+        functools.partial(gram_kernel, runs, places, counts, starts, depth, scale, kept, added, add),
         out_shape=jax.ShapeDtypeStruct((rows, columns), kind),
         in_specs=[any_spec] * len(operands),
         out_specs=any_spec,
@@ -307,7 +308,11 @@
         return [
             (
                 k * slab + c * width,
-                [(tables[k][c, r], within[c, r] if k == 1 else 0) for r in some_runs],
+                [
+                    (tables[k][c, r], within[c, r] if k == 1 else 0)
+                    for r in some_runs
+                    if (k, c, r) not in added
+                ],
             )
             for c in chosen
             for k in kinds
@@ -321,23 +326,27 @@
 
     every = list(range(runs))
     everything = list(range(CHUNKS))
-    first_runs, last_runs = every[: runs // 2], every[runs // 2 :]
     moved = (2, 1)
     done = last * CHUNKS
     work = {
         done - 12: [("rows", 0)],
         done - 11: [("rows", 1)],
-        done - 10: [((0,), everything, first_runs, False)],
-        done - 8: [(moved, [0, 1], first_runs, False)],
-        done - 6: [(moved, [2, 3], first_runs, False)],
-        done - 4: [(moved, [4, 5], first_runs, False)],
-        done - 2: [("rows", 2)],
+        done - 10: [((0,), everything[:half], [0, 1], False)],
+        done - 9: [((0,), everything[half:], [0, 1], False)],
+        done - 8: [(moved, [0, 1], [0, 1], False)],
+        done - 6: [(moved, [2, 3], [0, 1], False)],
+        done - 5: [("rows", 2)],
+        done - 4: [(moved, [4, 5], [0, 1], False)],
+        done - 3: [((0,), everything, [2], False)],
+        done - 2: [(moved, [0, 1], [2], False)],
+        done: [(moved, [2, 3], [2], False)],
         done + 1: [("rows", 3)],
-        done + 2: [((0,), everything, last_runs, True)],
-        done + 3: [(moved, [0, half], last_runs, True)],
-        done + 4: [(moved, [1, half + 1], last_runs, True)],
-        done + 5: [(moved, [half - 1, CHUNKS - 1], last_runs, True)],
+        done + 2: [((0,), everything, [3], True)],
+        done + 3: [(moved, [0, half], [3], True)],
+        done + 4: [(moved, [1, half + 1], [2, 3], True)],
+        done + 5: [(moved, [half - 1, CHUNKS - 1], [2, 3], True)],
     }
+    added = set()
 
     for step in range(steps + 3):
         before = ended.get(step - 2, [])
@@ -374,17 +383,15 @@
             if job[0] == "rows":
                 ended[step] += rows_for([job[1]])
             else:
-                kinds, chosen, some_runs, added = job
+                kinds, chosen, some_runs, final = job
                 lefts, pieces = rows_for(some_runs), tiles(kinds, chosen, some_runs)
-                if added:
-                    sums["all"] = gram(
-                        sums.get("all"), lefts, pieces, width, 3 * slab, scale, jnp.float32, sums["half"]
-                    )
+                added.update((k, c, r) for k in kinds for c in chosen for r in some_runs)
+                args = (lefts, pieces, width, 3 * slab, scale)
+                if final:
+                    sums["all"] = gram(sums.get("all"), *args, jnp.float32, sums["half"])
                 else:
-                    sums["half"] = gram(
-                        sums.get("half"), lefts, pieces, width, 3 * slab, scale, jnp.bfloat16
-                    )
-    assert not work
+                    sums["half"] = gram(sums.get("half"), *args, jnp.bfloat16, add=some_runs[0] > 0)
+    assert not work and len(added) == 3 * CHUNKS * runs
     return sums["all"]
 
 

time: 292 us -> 285 us (0.976)
  waiting for transfers between devices: 78.1 us -> 44.9 us
  Pallas kernels: 106 us -> 124 us
  starting transfers between devices: 67.6 us -> 72.6 us
  other arithmetic: 33 us -> 36.1 us
    ppermute x42, waiting for transfers between devices: 39.4 us -> 19.5 us  [over_tensor(): return lax.ppermute(value, 'tensor', [(t, t ^ bit) for t in range(count)])]
    pallas_call x8 -> x12, Pallas kernels: 66.6 us -> 85.4 us  [gram(): pl.pallas_call(functools.partial(gram_kernel, runs, places, counts, start...]
    ppermute x21, waiting for transfers between devices: 38.7 us -> 25.4 us  [from_behind(): return lax.ppermute(value, axis, pairs)]
    select_n x21, other arithmetic: 32.2 us -> 35.4 us  [per_device(): sent = jnp.where(even, *[jnp.concatenate(x, 1) for x in pair])]
  transfers between devices with their start and end apart: 65 -> 65, of which waited for: 22 -> 17; matrix products, arithmetic and copies ran while one was open for 11% -> 13% of each run, Pallas kernels for 34% -> 42%
where the time goes in v1:
time: 285 us; the launch traced here: 283 us
  Pallas kernels  124 us (44%)
  starting transfers between devices  72.6 us (25%)
  waiting for transfers between devices  44.9 us (16%)
  other arithmetic  36.1 us (13%)
  local copies, waits for them, and re-layouts  4.28 us (2%)
    pallas_call x12, Pallas kernels, gram(): pl.pallas_call(functools.partial(gram_kernel, runs, places, counts, start...  85.4 us
    ppermute x42, starting transfers between devices, over_tensor(): return lax.ppermute(value, 'tensor', [(t, t ^ bit) for t in range(count)])  53.1 us
    select_n x21, other arithmetic, per_device(): sent = jnp.where(even, *[jnp.concatenate(x, 1) for x in pair])  35.4 us
    pallas_call x6, Pallas kernels, attend(): pl.pallas_call(attend_kernel, grid=(heads // step,), out_shape=jax.ShapeD...  29.8 us
    ppermute x21, waiting for transfers between devices, from_behind(): return lax.ppermute(value, axis, pairs)  25.4 us
    ppermute x42, waiting for transfers between devices, over_tensor(): return lax.ppermute(value, 'tensor', [(t, t ^ bit) for t in range(count)])  19.5 us
    ppermute x21, starting transfers between devices, from_behind(): return lax.ppermute(value, axis, pairs)  11.6 us
    pallas_call x4, Pallas kernels, rows_of(): pl.pallas_call(functools.partial(rows_kernel, widths, rows), out_shape=ja...  9.25 us
  transfers between devices with their start and end apart: 65, of which 17 were waited for; matrix products, arithmetic and copies ran while one was open for 13% of the time, Pallas kernels for 42%

profile of v1, /device:TPU:1, one launch (start us, length us, event | category | flops | bytes accessed | tf_op | source)
XLA Modules:
  0.0 283.0 jit_solution(303107336541563995)
XLA Ops:
  1.2 4.0 %collective-permute-start = (bf16[512,256]{1,0:T(8,128)(2,1)S(1)}, bf16[512,256]{1,0:T(8,128)(2,1)S(1)}, u32[]{:S(2)}, u32[]{:S(2)}) collective-permute-start(bf16[512,256]{1,0:T(8,128)(2,1)S(1)} %pad_maximum_fusion.ko_ref.vo_ref), channel_id=1, source_target_pairs={{0,1},{1,2},{2,3},{4,5},{5,6},{6,7},{8,9},{9,10},{10,11},{12,13},{... | collective-permute-start | bytes 786440 | tf_op jit(solution)/shard_map/ppermute | solution.py:24
  6.0 3.9 %collective-permute-start.2 = (bf16[512,256]{1,0:T(8,128)(2,1)}, bf16[512,256]{1,0:T(8,128)(2,1)}, u32[]{:S(2)}, u32[]{:S(2)}) collective-permute-start(bf16[512,256]{1,0:T(8,128)(2,1)} %pad_maximum_fusion.1.ko_ref.vo_ref), channel_id=1, source_target_pairs={{0,1},{1,2},{2,3},{4,5},{5,6},{6,7},{8,9},{9,10},{10,11},{12,13},{... | collective-permute-start | bytes 786440 | tf_op jit(solution)/shard_map/ppermute | solution.py:24
  11.5 4.9 %shard_map.46.refs_0_.refs_2_ = bf16[512,512]{1,0:T(8,128)(2,1)} custom-call(s32[512,1]{1,0:T(8,128)} %copy.15.start_ref, bf16[512,3072]{1,0:T(8,128)(2,1)} %q_ref.11, bf16[512,256]{1,0:T(8,128)(2,1)} %copy-done.11, bf16[512,256]{1,0:T(8,128)(2,1)} %copy-done.6, bf16[512,256]{1,0:T(8,128)(2,1)} %copy-done.11, bf16[512,256]{1,0:T(8,128)(2,1)} %copy-done.6), custom_call_target="tpu_custom_call" | custom-call | flops 999999986991104 | bytes 1 | tf_op jit(solution)/shard_map/pallas_call | solution.py:86
  20.8 5.0 %shard_map.49.refs_1_.refs_4_ = bf16[512,512]{1,0:T(8,128)(2,1)} custom-call(s32[512,1]{1,0:T(8,128)} %copy.18.start_ref, bf16[512,3072]{1,0:T(8,128)(2,1)} %q_ref.11, bf16[512,256]{1,0:T(8,128)(2,1)} %copy-done.11, bf16[512,256]{1,0:T(8,128)(2,1)} %copy-done.6, bf16[512,256]{1,0:T(8,128)(2,1)} %copy-done.11, bf16[512,256]{1,0:T(8,128)(2,1)} %copy-done.6), custom_call_target="tpu_custom_call" | custom-call | flops 999999986991104 | bytes 1 | tf_op jit(solution)/shard_map/pallas_call | solution.py:86
  27.3 2.6 collective-permute-done.1.refs_0_.refs_3_
  30.8 7.2 %collective-permute-start.20 = (bf16[512,512]{1,0:T(8,128)(2,1)}, bf16[512,512]{1,0:T(8,128)(2,1)}, u32[]{:S(2)}, u32[]{:S(2)}) collective-permute-start(bf16[512,512]{1,0:T(8,128)(2,1)} %broadcast_select_fusion.17), channel_id=1, source_target_pairs={{0,4},{4,0},{8,12},{12,8},{1,5},{5,1},{9,13},{13,9},{2,6},{6,2},{1... | collective-permute-start | bytes 1572872 | tf_op jit(solution)/shard_map/ppermute | solution.py:35
  38.0 5.0 %shard_map.48.refs_2_.refs_6_ = bf16[512,512]{1,0:T(8,128)(2,1)} custom-call(s32[512,1]{1,0:T(8,128)} %copy.15.start_ref, bf16[512,3072]{1,0:T(8,128)(2,1)} %q_ref.11, bf16[512,256]{1,0:T(8,128)(2,1)} %copy-done.11, bf16[512,256]{1,0:T(8,128)(2,1)} %copy-done.6, bf16[512,256]{1,0:T(8,128)(2,1)} %copy-done.11, bf16[512,256]{1,0:T(8,128)(2,1)} %copy-done.6), custom_call_target="tpu_custom_call" | custom-call | flops 999999986991104 | bytes 1 | tf_op jit(solution)/shard_map/pallas_call | solution.py:86
  48.1 5.0 %shard_map.51.refs_3_.refs_2_ = bf16[512,512]{1,0:T(8,128)(2,1)} custom-call(s32[512,1]{1,0:T(8,128)} %copy.15.start_ref, bf16[512,3072]{1,0:T(8,128)(2,1)} %q_ref.11, bf16[512,256]{1,0:T(8,128)(2,1)} %collective-permute-done.2.kp_ref.vp_ref, bf16[512,256]{1,0:T(8,128)(2,1)} %pad_maximum_fusion.1.ko_ref.vo_ref, ...), custom_call_target="tpu_custom_call" | custom-call | flops 999999986991104 | bytes 1 | tf_op jit(solution)/shard_map/pallas_call | solution.py:86
  54.5 4.1 %collective-permute-done.4.refs_2_.refs_7_ = bf16[512,512]{1,0:T(8,128)(2,1)} collective-permute-done((bf16[512,512]{1,0:T(8,128)(2,1)}, bf16[512,512]{1,0:T(8,128)(2,1)}, u32[]{:S(2)}, u32[]{:S(2)}) %collective-permute-start.4) | collective-permute-done | bytes 524320 | tf_op jit(solution)/shard_map/ppermute | solution.py:30
  59.5 2.2 collective-permute-start.22
  61.8 5.0 %shard_map.47.refs_4_ = bf16[512,512]{1,0:T(8,128)(2,1)} custom-call(s32[512,1]{1,0:T(8,128)} %copy.15.start_ref, bf16[512,3072]{1,0:T(8,128)(2,1)} %q_ref.11, bf16[512,256]{1,0:T(8,128)(2,1)} %collective-permute-done.2.kp_ref.vp_ref, bf16[512,256]{1,0:T(8,128)(2,1)} %pad_maximum_fusion.1.ko_ref.vo_ref, ...), custom_call_target="tpu_custom_call" | custom-call | flops 999999986991104 | bytes 1 | tf_op jit(solution)/shard_map/pallas_call | solution.py:86
  72.6 4.9 %shard_map.50.refs_5_.refs_6_ = bf16[512,512]{1,0:T(8,128)(2,1)} custom-call(s32[512,1]{1,0:T(8,128)} %copy.15.start_ref, bf16[512,3072]{1,0:T(8,128)(2,1)} %q_ref.11, bf16[512,256]{1,0:T(8,128)(2,1)} %collective-permute-done.2.kp_ref.vp_ref, bf16[512,256]{1,0:T(8,128)(2,1)} %pad_maximum_fusion.1.ko_ref.vo_ref, ...), custom_call_target="tpu_custom_call" | custom-call | flops 999999986991104 | bytes 1 | tf_op jit(solution)/shard_map/pallas_call | solution.py:86
  79.8 2.6 collective-permute-done.6.refs_4_.refs_5_
  83.3 2.2 collective-permute-start.24
  85.5 2.4 shard_map.52.refs_0_
  89.3 4.4 %collective-permute-done.13.refs_5_.refs_7_ = bf16[512,512]{1,0:T(8,128)(2,1)} collective-permute-done((bf16[512,512]{1,0:T(8,128)(2,1)}, bf16[512,512]{1,0:T(8,128)(2,1)}, u32[]{:S(2)}, u32[]{:S(2)}) %collective-permute-start.13) | collective-permute-done | bytes 524320 | tf_op jit(solution)/shard_map/ppermute | solution.py:30
  95.9 2.5 collective-permute-start.25
  98.4 2.3 shard_map.53.refs_1_
  100.7 3.3 %collective-permute-done.16.refs_3_ = bf16[512,512]{1,0:T(8,128)(2,1)} collective-permute-done((bf16[512,512]{1,0:T(8,128)(2,1)}, bf16[512,512]{1,0:T(8,128)(2,1)}, u32[]{:S(2)}, u32[]{:S(2)}) %collective-permute-start.16) | collective-permute-done | bytes 524320 | tf_op jit(solution)/shard_map/ppermute | solution.py:35
  104.6 1.9 broadcast_select_fusion.11
  108.3 6.7 %shard_map.54.refs_8_ = bf16[768,9216]{1,0:T(8,128)(2,1)} custom-call(bf16[768,512]{1,0:T(8,128)(2,1)} %shard_map.52.refs_0_, bf16[768,512]{1,0:T(8,128)(2,1)} %shard_map.53.refs_1_, bf16[512,512]{1,0:T(8,128)(2,1)} %shard_map.46.refs_0_.refs_2_, bf16[512,512]{1,0:T(8,128)(2,1)} %collective-permute-done.1.refs_0_.refs_3_, ...), custom_call_target="tpu_custom_call" | custom-call | flops 999999986991104 | bytes 1 | tf_op jit(solution)/shard_map/pallas_call | solution.py:251
  117.4 1.9 broadcast_select_fusion.10
  120.4 6.7 %shard_map.55.refs_10_ = bf16[768,9216]{1,0:T(8,128)(2,1)} custom-call(bf16[768,512]{1,0:T(8,128)(2,1)} %shard_map.52.refs_0_, bf16[768,512]{1,0:T(8,128)(2,1)} %shard_map.53.refs_1_, bf16[512,512]{1,0:T(8,128)(2,1)} %shard_map.51.refs_3_.refs_2_, bf16[512,512]{1,0:T(8,128)(2,1)} %collective-permute-done.11.refs_3_, ...), custom_call_target="tpu_custom_call", output_to_operand_aliasing={{}: (8, {})} | custom-call | flops 999999986991104 | bytes 1 | tf_op jit(solution)/shard_map/pallas_call | solution.py:251
  127.1 3.7 %collective-permute-done.17.refs_2_.refs_3_ = bf16[512,512]{1,0:T(8,128)(2,1)} collective-permute-done((bf16[512,512]{1,0:T(8,128)(2,1)}, bf16[512,512]{1,0:T(8,128)(2,1)}, u32[]{:S(2)}, u32[]{:S(2)}) %collective-permute-start.17) | collective-permute-done | bytes 524320 | tf_op jit(solution)/shard_map/ppermute | solution.py:30
  135.1 8.0 %shard_map.56.refs_10_ = bf16[768,9216]{1,0:T(8,128)(2,1)} custom-call(bf16[768,512]{1,0:T(8,128)(2,1)} %shard_map.52.refs_0_, bf16[768,512]{1,0:T(8,128)(2,1)} %shard_map.53.refs_1_, bf16[512,512]{1,0:T(8,128)(2,1)} %collective-permute-done.3.refs_2_, bf16[512,512]{1,0:T(8,128)(2,1)} %collective-permute-done.16.refs_3_, ...), custom_call_target="tpu_custom_call", output_to_operand_aliasing={{}: (10, {})} | custom-call | flops 999999986991104 | bytes 1 | tf_op jit(solution)/shard_map/pallas_call | solution.py:251
  145.4 6.2 %collective-permute-done.33.refs_3_ = bf16[512,512]{1,0:T(8,128)(2,1)} collective-permute-done((bf16[512,512]{1,0:T(8,128)(2,1)}, bf16[512,512]{1,0:T(8,128)(2,1)}, u32[]{:S(2)}, u32[]{:S(2)}) %collective-permute-start.33) | collective-permute-done | bytes 524320 | tf_op jit(solution)/shard_map/ppermute | solution.py:35
  154.3 2.1 broadcast_select_fusion.7
  157.8 8.1 %shard_map.58.refs_10_ = bf16[768,9216]{1,0:T(8,128)(2,1)} custom-call(bf16[768,512]{1,0:T(8,128)(2,1)} %shard_map.52.refs_0_, bf16[768,512]{1,0:T(8,128)(2,1)} %shard_map.53.refs_1_, bf16[512,512]{1,0:T(8,128)(2,1)} %collective-permute-done.5.refs_2_, bf16[512,512]{1,0:T(8,128)(2,1)} %collective-permute-done.27.refs_3_, ...), custom_call_target="tpu_custom_call", output_to_operand_aliasing={{}: (10, {})} | custom-call | flops 999999986991104 | bytes 1 | tf_op jit(solution)/shard_map/pallas_call | solution.py:251
  165.9 1.9 broadcast_select_fusion.6
  167.8 2.3 shard_map.57.refs_0_
  171.2 2.9 %collective-permute-done.39.refs_1_ = bf16[512,512]{1,0:T(8,128)(2,1)} collective-permute-done((bf16[512,512]{1,0:T(8,128)(2,1)}, bf16[512,512]{1,0:T(8,128)(2,1)}, u32[]{:S(2)}, u32[]{:S(2)}) %collective-permute-start.39) | collective-permute-done | bytes 524320 | tf_op jit(solution)/shard_map/ppermute | solution.py:35
  179.9 8.0 %shard_map.59.refs_7_ = bf16[768,9216]{1,0:T(8,128)(2,1)} custom-call(bf16[768,512]{1,0:T(8,128)(2,1)} %shard_map.52.refs_0_, bf16[768,512]{1,0:T(8,128)(2,1)} %shard_map.53.refs_1_, bf16[512,512]{1,0:T(8,128)(2,1)} %collective-permute-done.7.refs_2_, bf16[512,512]{1,0:T(8,128)(2,1)} %collective-permute-done.33.refs_3_, ...), custom_call_target="tpu_custom_call", output_to_operand_aliasing={{}: (10, {})} | custom-call | flops 999999986991104 | bytes 1 | tf_op jit(solution)/shard_map/pallas_call | solution.py:251
  191.6 8.2 %shard_map.60.refs_5_ = bf16[768,9216]{1,0:T(8,128)(2,1)} custom-call(bf16[768,512]{1,0:T(8,128)(2,1)} %shard_map.57.refs_0_, bf16[512,512]{1,0:T(8,128)(2,1)} %collective-permute-done.8.refs_0_.refs_1_, bf16[512,512]{1,0:T(8,128)(2,1)} %collective-permute-done.15.refs_1_.refs_2_, ...), custom_call_target="tpu_custom_call", output_to_operand_aliasing={{}: (7, {})} | custom-call | flops 999999986991104 | bytes 1 | tf_op jit(solution)/shard_map/pallas_call | solution.py:251
  205.4 6.3 %shard_map.61.refs_5_ = bf16[768,9216]{1,0:T(8,128)(2,1)} custom-call(bf16[768,512]{1,0:T(8,128)(2,1)} %shard_map.57.refs_0_, bf16[512,512]{1,0:T(8,128)(2,1)} %collective-permute-done.39.refs_1_, bf16[512,512]{1,0:T(8,128)(2,1)} %collective-permute-done.44.refs_2_, ...), custom_call_target="tpu_custom_call", output_to_operand_aliasing={{}: (5, {})} | custom-call | flops 999999986991104 | bytes 1 | tf_op jit(solution)/shard_map/pallas_call | solution.py:251
  214.9 4.1 %collective-permute-done.51.refs_4_ = bf16[512,512]{1,0:T(8,128)(2,1)} collective-permute-done((bf16[512,512]{1,0:T(8,128)(2,1)}, bf16[512,512]{1,0:T(8,128)(2,1)}, u32[]{:S(2)}, u32[]{:S(2)}) %collective-permute-start.51) | collective-permute-done | bytes 524320 | tf_op jit(solution)/shard_map/ppermute | solution.py:35
  221.4 2.1 broadcast_select_fusion.1
  223.5 2.0 collective-permute-start.54
  225.5 6.4 %shard_map.63.refs_7_.refs_5_.refs_8_ = bf16[768,9216]{1,0:T(8,128)(2,1)} custom-call(bf16[768,512]{1,0:T(8,128)(2,1)} %shard_map.57.refs_0_, bf16[512,512]{1,0:T(8,128)(2,1)} %collective-permute-done.45.refs_1_, bf16[512,512]{1,0:T(8,128)(2,1)} %collective-permute-done.52.refs_2_, ...), custom_call_target="tpu_custom_call", output_to_operand_aliasing={{}: (5, {})} | custom-call | flops 999999986991104 | bytes 1 | tf_op jit(solution)/shard_map/pallas_call | solution.py:251
  231.9 1.9 broadcast_select_fusion
  235.3 2.3 shard_map.62.refs_0_.refs_1_
  238.6 2.9 %collective-permute-done.56.refs_1_ = bf16[512,512]{1,0:T(8,128)(2,1)} collective-permute-done((bf16[512,512]{1,0:T(8,128)(2,1)}, bf16[512,512]{1,0:T(8,128)(2,1)}, u32[]{:S(2)}, u32[]{:S(2)}) %collective-permute-start.56) | collective-permute-done | bytes 524320 | tf_op jit(solution)/shard_map/ppermute | solution.py:35
  243.9 2.8 %maximum_select_fusion = bf16[512,1024]{1,0:T(8,128)(2,1)} fusion(bf16[512,512]{1,0:T(8,128)(2,1)} %collective-permute-done.55.refs_3_, bf16[512,512]{1,0:T(8,128)(2,1)} %collective-permute-done.56.refs_1_, bf16[512,512]{1,0:T(8,128)(2,1)} %collective-permute-done.43.refs_3_.refs_4_, bf16[512,512]{1,0:T(8,128)(2,1)} %collective-permute-done.34.refs_0_.refs_1_, ...), kind=kLoop, calls=%fused_computation | loop fusion | flops 4718592 | bytes 3145729 | tf_op jit(solution)/shard_map/jit(_where)/select_n | solution.py:377
  248.6 7.9 %shard_map.64.refs_6_ = f32[768,9216]{1,0:T(8,128)} custom-call(bf16[768,512]{1,0:T(8,128)(2,1)} %shard_map.62.refs_0_.refs_1_, bf16[512,512]{1,0:T(8,128)(2,1)} %collective-permute-done.34.refs_0_.refs_1_, bf16[512,512]{1,0:T(8,128)(2,1)} %collective-permute-done.37.refs_1_.refs_2_, bf16[512,512]{1,0:T(8,128)(2,1)} %collective-permute-done.40.refs_2_.refs_3_, ...), custom_call_target="tpu_custom_call" | custom-call | flops 999999986991104 | bytes 1 | tf_op jit(solution)/shard_map/pallas_call | solution.py:251
  256.6 2.9 %maximum_select_fusion.1 = bf16[512,1024]{1,0:T(8,128)(2,1)} fusion(bf16[512,512]{1,0:T(8,128)(2,1)} %collective-permute-done.62.refs_5_, bf16[512,512]{1,0:T(8,128)(2,1)} %collective-permute-done.61.refs_2_, bf16[512,512]{1,0:T(8,128)(2,1)} %collective-permute-done.46.refs_4_.refs_5_, bf16[512,512]{1,0:T(8,128)(2,1)} %collective-permute-done.37.refs_1_.refs_2_, ...), kind=kLoop, calls=%fused_computation.1 | loop fusion | flops 4718592 | bytes 3145729 | tf_op jit(solution)/shard_map/jit(_where)/select_n | solution.py:377
  259.5 5.7 %shard_map.65.refs_9_ = f32[768,9216]{1,0:T(8,128)} custom-call(bf16[768,512]{1,0:T(8,128)(2,1)} %shard_map.62.refs_0_.refs_1_, bf16[512,512]{1,0:T(8,128)(2,1)} %collective-permute-done.56.refs_1_, bf16[512,1024]{1,0:T(8,128)(2,1)} %collective-permute-done.60.refs_2_.refs_4_, ...), custom_call_target="tpu_custom_call", output_to_operand_aliasing={{}: (6, {})} | custom-call | flops 999999986991104 | bytes 1 | tf_op jit(solution)/shard_map/pallas_call | solution.py:251
  265.5 2.9 %maximum_select_fusion.2 = bf16[512,1024]{1,0:T(8,128)(2,1)} fusion(bf16[512,512]{1,0:T(8,128)(2,1)} %collective-permute-done.58.refs_5_, bf16[512,512]{1,0:T(8,128)(2,1)} %collective-permute-done.57.refs_2_, bf16[512,512]{1,0:T(8,128)(2,1)} %collective-permute-done.49.refs_5_.refs_6_, bf16[512,512]{1,0:T(8,128)(2,1)} %collective-permute-done.40.refs_2_.refs_3_, ...), kind=kLoop, calls=%fused_computation.2 | loop fusion | flops 4718592 | bytes 3145729 | tf_op jit(solution)/shard_map/jit(_where)/select_n | solution.py:377
  269.3 6.8 %shard_map.66.refs_9_ = f32[768,9216]{1,0:T(8,128)} custom-call(bf16[768,512]{1,0:T(8,128)(2,1)} %shard_map.57.refs_0_, bf16[768,512]{1,0:T(8,128)(2,1)} %shard_map.62.refs_0_.refs_1_, bf16[512,512]{1,0:T(8,128)(2,1)} %collective-permute-done.61.refs_2_, bf16[512,1024]{1,0:T(8,128)(2,1)} %collective-permute-done.63.refs_3_.refs_7_, ...), custom_call_target="tpu_custom_call", output_to_operand_aliasing={{}: (9, {})} | custom-call | flops 999999986991104 | bytes 1 | tf_op jit(solution)/shard_map/pallas_call | solution.py:251
  276.1 6.8 %shard_map.67 = f32[768,9216]{1,0:T(8,128)} custom-call(bf16[768,512]{1,0:T(8,128)(2,1)} %shard_map.57.refs_0_, bf16[768,512]{1,0:T(8,128)(2,1)} %shard_map.62.refs_0_.refs_1_, bf16[512,512]{1,0:T(8,128)(2,1)} %collective-permute-done.57.refs_2_, bf16[512,1024]{1,0:T(8,128)(2,1)} %collective-permute-done.64.refs_3_.refs_7_, ...), custom_call_target="tpu_custom_call", output_to_operand_aliasing={{}: (9, {})} | custom-call | flops 999999986991104 | bytes 1 | tf_op jit(solution)/shard_map/pallas_call | solution.py:251
  (155 shorter events, 76.6 us)
Async XLA Ops:
  6.0 13.3 %collective-permute-start.2 = (bf16[512,256]{1,0:T(8,128)(2,1)}, bf16[512,256]{1,0:T(8,128)(2,1)}, u32[]{:S(2)}, u32[]{:S(2)}) collective-permute-start(bf16[512,256]{1,0:T(8,128)(2,1)} %pad_maximum_fusion.1.ko_ref.vo_ref), channel_id=1, source_target_pairs={{0,1},{1,2},{2,3},{4,5},{5,6},{6,7},{8,9},{9,10},{10,11},{12,13},{... | collective-permute-start | bytes 786440 | tf_op jit(solution)/shard_map/ppermute | solution.py:24
  16.4 13.5 %collective-permute-start.1 = (bf16[512,512]{1,0:T(8,128)(2,1)}, bf16[512,512]{1,0:T(8,128)(2,1)}, u32[]{:S(2)}, u32[]{:S(2)}) collective-permute-start(bf16[512,512]{1,0:T(8,128)(2,1)} %shard_map.46.refs_0_.refs_2_), channel_id=1, source_target_pairs={{0,1},{1,2},{2,3},{3,0},{4,5},{5,6},{6,7},{7,4},{8,9},{9,10},{10,1... | collective-permute-start | bytes 1572872 | tf_op jit(solution)/shard_map/ppermute | solution.py:30
  18.1 11.9 %collective-permute-start.3 = (bf16[512,512]{1,0:T(8,128)(2,1)}, bf16[512,512]{1,0:T(8,128)(2,1)}, u32[]{:S(2)}, u32[]{:S(2)}) collective-permute-start(bf16[512,512]{1,0:T(8,128)(2,1)} %shard_map.46.refs_0_.refs_2_), channel_id=1, source_target_pairs={{0,8},{4,12},{8,0},{12,4},{1,9},{5,13},{9,1},{13,5},{2,10},{6,14},... | collective-permute-start | bytes 1572872 | tf_op jit(solution)/shard_map/ppermute | solution.py:35
  25.8 19.8 %collective-permute-start.10 = (bf16[512,512]{1,0:T(8,128)(2,1)}, bf16[512,512]{1,0:T(8,128)(2,1)}, u32[]{:S(2)}, u32[]{:S(2)}) collective-permute-start(bf16[512,512]{1,0:T(8,128)(2,1)} %shard_map.49.refs_1_.refs_4_), channel_id=1, source_target_pairs={{0,8},{4,12},{8,0},{12,4},{1,9},{5,13},{9,1},{13,5},{2,10},{6,14},... | collective-permute-start | bytes 1572872 | tf_op jit(solution)/shard_map/ppermute | solution.py:35
  26.0 19.6 %collective-permute-start.9 = (bf16[512,512]{1,0:T(8,128)(2,1)}, bf16[512,512]{1,0:T(8,128)(2,1)}, u32[]{:S(2)}, u32[]{:S(2)}) collective-permute-start(bf16[512,512]{1,0:T(8,128)(2,1)} %shard_map.49.refs_1_.refs_4_), channel_id=1, source_target_pairs={{0,1},{1,2},{2,3},{3,0},{4,5},{5,6},{6,7},{7,4},{8,9},{9,10},{10,1... | collective-permute-start | bytes 1572872 | tf_op jit(solution)/shard_map/ppermute | solution.py:30
  30.8 14.8 %collective-permute-start.20 = (bf16[512,512]{1,0:T(8,128)(2,1)}, bf16[512,512]{1,0:T(8,128)(2,1)}, u32[]{:S(2)}, u32[]{:S(2)}) collective-permute-start(bf16[512,512]{1,0:T(8,128)(2,1)} %broadcast_select_fusion.17), channel_id=1, source_target_pairs={{0,4},{4,0},{8,12},{12,8},{1,5},{5,1},{9,13},{13,9},{2,6},{6,2},{1... | collective-permute-start | bytes 1572872 | tf_op jit(solution)/shard_map/ppermute | solution.py:35
  43.0 15.7 %collective-permute-start.4 = (bf16[512,512]{1,0:T(8,128)(2,1)}, bf16[512,512]{1,0:T(8,128)(2,1)}, u32[]{:S(2)}, u32[]{:S(2)}) collective-permute-start(bf16[512,512]{1,0:T(8,128)(2,1)} %shard_map.48.refs_2_.refs_6_), channel_id=1, source_target_pairs={{0,1},{1,2},{2,3},{3,0},{4,5},{5,6},{6,7},{7,4},{8,9},{9,10},{10,1... | collective-permute-start | bytes 1572872 | tf_op jit(solution)/shard_map/ppermute | solution.py:30
  44.3 14.4 %collective-permute-start.5 = (bf16[512,512]{1,0:T(8,128)(2,1)}, bf16[512,512]{1,0:T(8,128)(2,1)}, u32[]{:S(2)}, u32[]{:S(2)}) collective-permute-start(bf16[512,512]{1,0:T(8,128)(2,1)} %shard_map.48.refs_2_.refs_6_), channel_id=1, source_target_pairs={{0,8},{4,12},{8,0},{12,4},{1,9},{5,13},{9,1},{13,5},{2,10},{6,14},... | collective-permute-start | bytes 1572872 | tf_op jit(solution)/shard_map/ppermute | solution.py:35
  46.5 12.2 %collective-permute-start.21 = (bf16[512,512]{1,0:T(8,128)(2,1)}, bf16[512,512]{1,0:T(8,128)(2,1)}, u32[]{:S(2)}, u32[]{:S(2)}) collective-permute-start(bf16[512,512]{1,0:T(8,128)(2,1)} %broadcast_select_fusion.16), channel_id=1, source_target_pairs={{0,4},{4,0},{8,12},{12,8},{1,5},{5,1},{9,13},{13,9},{2,6},{6,2},{1... | collective-permute-start | bytes 1572872 | tf_op jit(solution)/shard_map/ppermute | solution.py:35
  53.1 16.8 %collective-permute-start.11 = (bf16[512,512]{1,0:T(8,128)(2,1)}, bf16[512,512]{1,0:T(8,128)(2,1)}, u32[]{:S(2)}, u32[]{:S(2)}) collective-permute-start(bf16[512,512]{1,0:T(8,128)(2,1)} %shard_map.51.refs_3_.refs_2_), channel_id=1, source_target_pairs={{0,1},{1,2},{2,3},{3,0},{4,5},{5,6},{6,7},{7,4},{8,9},{9,10},{10,1... | collective-permute-start | bytes 1572872 | tf_op jit(solution)/shard_map/ppermute | solution.py:30
  54.4 15.5 %collective-permute-start.12 = (bf16[512,512]{1,0:T(8,128)(2,1)}, bf16[512,512]{1,0:T(8,128)(2,1)}, u32[]{:S(2)}, u32[]{:S(2)}) collective-permute-start(bf16[512,512]{1,0:T(8,128)(2,1)} %shard_map.51.refs_3_.refs_2_), channel_id=1, source_target_pairs={{0,8},{4,12},{8,0},{12,4},{1,9},{5,13},{9,1},{13,5},{2,10},{6,14},... | collective-permute-start | bytes 1572872 | tf_op jit(solution)/shard_map/ppermute | solution.py:35
  66.8 15.7 %collective-permute-start.6 = (bf16[512,512]{1,0:T(8,128)(2,1)}, bf16[512,512]{1,0:T(8,128)(2,1)}, u32[]{:S(2)}, u32[]{:S(2)}) collective-permute-start(bf16[512,512]{1,0:T(8,128)(2,1)} %shard_map.47.refs_4_), channel_id=1, source_target_pairs={{0,1},{1,2},{2,3},{3,0},{4,5},{5,6},{6,7},{7,4},{8,9},{9,10},{10,1... | collective-permute-start | bytes 1572872 | tf_op jit(solution)/shard_map/ppermute | solution.py:30
  67.9 14.6 %collective-permute-start.7 = (bf16[512,512]{1,0:T(8,128)(2,1)}, bf16[512,512]{1,0:T(8,128)(2,1)}, u32[]{:S(2)}, u32[]{:S(2)}) collective-permute-start(bf16[512,512]{1,0:T(8,128)(2,1)} %shard_map.47.refs_4_), channel_id=1, source_target_pairs={{0,8},{4,12},{8,0},{12,4},{1,9},{5,13},{9,1},{13,5},{2,10},{6,14},... | collective-permute-start | bytes 1572872 | tf_op jit(solution)/shard_map/ppermute | solution.py:35
  77.6 16.1 %collective-permute-start.13 = (bf16[512,512]{1,0:T(8,128)(2,1)}, bf16[512,512]{1,0:T(8,128)(2,1)}, u32[]{:S(2)}, u32[]{:S(2)}) collective-permute-start(bf16[512,512]{1,0:T(8,128)(2,1)} %shard_map.50.refs_5_.refs_6_), channel_id=1, source_target_pairs={{0,1},{1,2},{2,3},{3,0},{4,5},{5,6},{6,7},{7,4},{8,9},{9,10},{10,1... | collective-permute-start | bytes 1572872 | tf_op jit(solution)/shard_map/ppermute | solution.py:30
  78.5 15.2 %collective-permute-start.14 = (bf16[512,512]{1,0:T(8,128)(2,1)}, bf16[512,512]{1,0:T(8,128)(2,1)}, u32[]{:S(2)}, u32[]{:S(2)}) collective-permute-start(bf16[512,512]{1,0:T(8,128)(2,1)} %shard_map.50.refs_5_.refs_6_), channel_id=1, source_target_pairs={{0,8},{4,12},{8,0},{12,4},{1,9},{5,13},{9,1},{13,5},{2,10},{6,14},... | collective-permute-start | bytes 1572872 | tf_op jit(solution)/shard_map/ppermute | solution.py:35
  83.3 11.7 %collective-permute-start.24 = (bf16[512,512]{1,0:T(8,128)(2,1)}, bf16[512,512]{1,0:T(8,128)(2,1)}, u32[]{:S(2)}, u32[]{:S(2)}) collective-permute-start(bf16[512,512]{1,0:T(8,128)(2,1)} %broadcast_select_fusion.13), channel_id=1, source_target_pairs={{0,4},{4,0},{8,12},{12,8},{1,5},{5,1},{9,13},{13,9},{2,6},{6,2},{1... | collective-permute-start | bytes 1572872 | tf_op jit(solution)/shard_map/ppermute | solution.py:35
  87.9 16.1 %collective-permute-start.16 = (bf16[512,512]{1,0:T(8,128)(2,1)}, bf16[512,512]{1,0:T(8,128)(2,1)}, u32[]{:S(2)}, u32[]{:S(2)}) collective-permute-start(bf16[512,512]{1,0:T(8,128)(2,1)} %collective-permute-done.1.refs_0_.refs_3_), channel_id=1, source_target_pairs={{0,8},{4,12},{8,0},{12,4},{1,9},{5,13},{9,1},{13,5},{2,10},{6,14},... | collective-permute-start | bytes 1572872 | tf_op jit(solution)/shard_map/ppermute | solution.py:35
  89.3 15.3 %collective-permute-start.8 = (bf16[512,512]{1,0:T(8,128)(2,1)}, bf16[512,512]{1,0:T(8,128)(2,1)}, u32[]{:S(2)}, u32[]{:S(2)}) collective-permute-start(bf16[512,512]{1,0:T(8,128)(2,1)} %collective-permute-done.1.refs_0_.refs_3_), channel_id=1, source_target_pairs={{0,1},{1,2},{2,3},{3,0},{4,5},{5,6},{6,7},{7,4},{8,9},{9,10},{10,1... | collective-permute-start | bytes 1572872 | tf_op jit(solution)/shard_map/ppermute | solution.py:30
  93.6 22.5 %collective-permute-start.15 = (bf16[512,512]{1,0:T(8,128)(2,1)}, bf16[512,512]{1,0:T(8,128)(2,1)}, u32[]{:S(2)}, u32[]{:S(2)}) collective-permute-start(bf16[512,512]{1,0:T(8,128)(2,1)} %collective-permute-done.9.refs_1_.refs_5_), channel_id=1, source_target_pairs={{0,1},{1,2},{2,3},{3,0},{4,5},{5,6},{6,7},{7,4},{8,9},{9,10},{10,1... | collective-permute-start | bytes 1572872 | tf_op jit(solution)/shard_map/ppermute | solution.py:30
  93.7 22.5 %collective-permute-start.18 = (bf16[512,512]{1,0:T(8,128)(2,1)}, bf16[512,512]{1,0:T(8,128)(2,1)}, u32[]{:S(2)}, u32[]{:S(2)}) collective-permute-start(bf16[512,512]{1,0:T(8,128)(2,1)} %collective-permute-done.9.refs_1_.refs_5_), channel_id=1, source_target_pairs={{0,8},{4,12},{8,0},{12,4},{1,9},{5,13},{9,1},{13,5},{2,10},{6,14},... | collective-permute-start | bytes 1572872 | tf_op jit(solution)/shard_map/ppermute | solution.py:35
  115.1 15.7 %collective-permute-start.17 = (bf16[512,512]{1,0:T(8,128)(2,1)}, bf16[512,512]{1,0:T(8,128)(2,1)}, u32[]{:S(2)}, u32[]{:S(2)}) collective-permute-start(bf16[512,512]{1,0:T(8,128)(2,1)} %collective-permute-done.4.refs_2_.refs_7_), channel_id=1, source_target_pairs={{0,1},{1,2},{2,3},{3,0},{4,5},{5,6},{6,7},{7,4},{8,9},{9,10},{10,1... | collective-permute-start | bytes 1572872 | tf_op jit(solution)/shard_map/ppermute | solution.py:30
  115.2 15.7 %collective-permute-start.27 = (bf16[512,512]{1,0:T(8,128)(2,1)}, bf16[512,512]{1,0:T(8,128)(2,1)}, u32[]{:S(2)}, u32[]{:S(2)}) collective-permute-start(bf16[512,512]{1,0:T(8,128)(2,1)} %collective-permute-done.4.refs_2_.refs_7_), channel_id=1, source_target_pairs={{0,8},{4,12},{8,0},{12,4},{1,9},{5,13},{9,1},{13,5},{2,10},{6,14},... | collective-permute-start | bytes 1572872 | tf_op jit(solution)/shard_map/ppermute | solution.py:35
  116.2 26.9 %collective-permute-start.30 = (bf16[512,512]{1,0:T(8,128)(2,1)}, bf16[512,512]{1,0:T(8,128)(2,1)}, u32[]{:S(2)}, u32[]{:S(2)}) collective-permute-start(bf16[512,512]{1,0:T(8,128)(2,1)} %collective-permute-done.11.refs_3_), channel_id=1, source_target_pairs={{0,8},{4,12},{8,0},{12,4},{1,9},{5,13},{9,1},{13,5},{2,10},{6,14},... | collective-permute-start | bytes 1572872 | tf_op jit(solution)/shard_map/ppermute | solution.py:35
  117.4 25.7 %collective-permute-start.19 = (bf16[512,512]{1,0:T(8,128)(2,1)}, bf16[512,512]{1,0:T(8,128)(2,1)}, u32[]{:S(2)}, u32[]{:S(2)}) collective-permute-start(bf16[512,512]{1,0:T(8,128)(2,1)} %collective-permute-done.11.refs_3_), channel_id=1, source_target_pairs={{0,1},{1,2},{2,3},{3,0},{4,5},{5,6},{6,7},{7,4},{8,9},{9,10},{10,1... | collective-permute-start | bytes 1572872 | tf_op jit(solution)/shard_map/ppermute | solution.py:30
  119.3 12.4 %collective-permute-start.29 = (bf16[512,512]{1,0:T(8,128)(2,1)}, bf16[512,512]{1,0:T(8,128)(2,1)}, u32[]{:S(2)}, u32[]{:S(2)}) collective-permute-start(bf16[512,512]{1,0:T(8,128)(2,1)} %broadcast_select_fusion.10), channel_id=1, source_target_pairs={{0,4},{4,0},{8,12},{12,8},{1,5},{5,1},{9,13},{13,9},{2,6},{6,2},{1... | collective-permute-start | bytes 1572872 | tf_op jit(solution)/shard_map/ppermute | solution.py:35
  130.8 20.7 %collective-permute-start.33 = (bf16[512,512]{1,0:T(8,128)(2,1)}, bf16[512,512]{1,0:T(8,128)(2,1)}, u32[]{:S(2)}, u32[]{:S(2)}) collective-permute-start(bf16[512,512]{1,0:T(8,128)(2,1)} %collective-permute-done.6.refs_4_.refs_5_), channel_id=1, source_target_pairs={{0,8},{4,12},{8,0},{12,4},{1,9},{5,13},{9,1},{13,5},{2,10},{6,14},... | collective-permute-start | bytes 1572872 | tf_op jit(solution)/shard_map/ppermute | solution.py:35
  131.8 21.5 %collective-permute-start.28 = (bf16[512,512]{1,0:T(8,128)(2,1)}, bf16[512,512]{1,0:T(8,128)(2,1)}, u32[]{:S(2)}, u32[]{:S(2)}) collective-permute-start(bf16[512,512]{1,0:T(8,128)(2,1)} %collective-permute-done.6.refs_4_.refs_5_), channel_id=1, source_target_pairs={{0,1},{1,2},{2,3},{3,0},{4,5},{5,6},{6,7},{7,4},{8,9},{9,10},{10,1... | collective-permute-start | bytes 1572872 | tf_op jit(solution)/shard_map/ppermute | solution.py:30
  144.4 21.5 %collective-permute-start.36 = (bf16[512,512]{1,0:T(8,128)(2,1)}, bf16[512,512]{1,0:T(8,128)(2,1)}, u32[]{:S(2)}, u32[]{:S(2)}) collective-permute-start(bf16[512,512]{1,0:T(8,128)(2,1)} %collective-permute-done.13.refs_5_.refs_7_), channel_id=1, source_target_pairs={{0,8},{4,12},{8,0},{12,4},{1,9},{5,13},{9,1},{13,5},{2,10},{6,14},... | collective-permute-start | bytes 1572872 | tf_op jit(solution)/shard_map/ppermute | solution.py:35
  145.4 20.5 %collective-permute-start.31 = (bf16[512,512]{1,0:T(8,128)(2,1)}, bf16[512,512]{1,0:T(8,128)(2,1)}, u32[]{:S(2)}, u32[]{:S(2)}) collective-permute-start(bf16[512,512]{1,0:T(8,128)(2,1)} %collective-permute-done.13.refs_5_.refs_7_), channel_id=1, source_target_pairs={{0,1},{1,2},{2,3},{3,0},{4,5},{5,6},{6,7},{7,4},{8,9},{9,10},{10,1... | collective-permute-start | bytes 1572872 | tf_op jit(solution)/shard_map/ppermute | solution.py:30
  153.3 20.8 %collective-permute-start.39 = (bf16[512,512]{1,0:T(8,128)(2,1)}, bf16[512,512]{1,0:T(8,128)(2,1)}, u32[]{:S(2)}, u32[]{:S(2)}) collective-permute-start(bf16[512,512]{1,0:T(8,128)(2,1)} %collective-permute-done.8.refs_0_.refs_1_), channel_id=1, source_target_pairs={{0,8},{4,12},{8,0},{12,4},{1,9},{5,13},{9,1},{13,5},{2,10},{6,14},... | collective-permute-start | bytes 1572872 | tf_op jit(solution)/shard_map/ppermute | solution.py:35
  154.3 21.5 %collective-permute-start.34 = (bf16[512,512]{1,0:T(8,128)(2,1)}, bf16[512,512]{1,0:T(8,128)(2,1)}, u32[]{:S(2)}, u32[]{:S(2)}) collective-permute-start(bf16[512,512]{1,0:T(8,128)(2,1)} %collective-permute-done.8.refs_0_.refs_1_), channel_id=1, source_target_pairs={{0,1},{1,2},{2,3},{3,0},{4,5},{5,6},{6,7},{7,4},{8,9},{9,10},{10,1... | collective-permute-start | bytes 1572872 | tf_op jit(solution)/shard_map/ppermute | solution.py:30
  170.1 17.8 %collective-permute-start.42 = (bf16[512,512]{1,0:T(8,128)(2,1)}, bf16[512,512]{1,0:T(8,128)(2,1)}, u32[]{:S(2)}, u32[]{:S(2)}) collective-permute-start(bf16[512,512]{1,0:T(8,128)(2,1)} %collective-permute-done.15.refs_1_.refs_2_), channel_id=1, source_target_pairs={{0,8},{4,12},{8,0},{12,4},{1,9},{5,13},{9,1},{13,5},{2,10},{6,14},... | collective-permute-start | bytes 1572872 | tf_op jit(solution)/shard_map/ppermute | solution.py:35
  170.9 17.0 %collective-permute-start.37 = (bf16[512,512]{1,0:T(8,128)(2,1)}, bf16[512,512]{1,0:T(8,128)(2,1)}, u32[]{:S(2)}, u32[]{:S(2)}) collective-permute-start(bf16[512,512]{1,0:T(8,128)(2,1)} %collective-permute-done.15.refs_1_.refs_2_), channel_id=1, source_target_pairs={{0,1},{1,2},{2,3},{3,0},{4,5},{5,6},{6,7},{7,4},{8,9},{9,10},{10,1... | collective-permute-start | bytes 1572872 | tf_op jit(solution)/shard_map/ppermute | solution.py:30
  175.8 24.0 %collective-permute-start.45 = (bf16[512,512]{1,0:T(8,128)(2,1)}, bf16[512,512]{1,0:T(8,128)(2,1)}, u32[]{:S(2)}, u32[]{:S(2)}) collective-permute-start(bf16[512,512]{1,0:T(8,128)(2,1)} %collective-permute-done.17.refs_2_.refs_3_), channel_id=1, source_target_pairs={{0,8},{4,12},{8,0},{12,4},{1,9},{5,13},{9,1},{13,5},{2,10},{6,14},... | collective-permute-start | bytes 1572872 | tf_op jit(solution)/shard_map/ppermute | solution.py:35
  176.7 23.0 %collective-permute-start.40 = (bf16[512,512]{1,0:T(8,128)(2,1)}, bf16[512,512]{1,0:T(8,128)(2,1)}, u32[]{:S(2)}, u32[]{:S(2)}) collective-permute-start(bf16[512,512]{1,0:T(8,128)(2,1)} %collective-permute-done.17.refs_2_.refs_3_), channel_id=1, source_target_pairs={{0,1},{1,2},{2,3},{3,0},{4,5},{5,6},{6,7},{7,4},{8,9},{9,10},{10,1... | collective-permute-start | bytes 1572872 | tf_op jit(solution)/shard_map/ppermute | solution.py:30
  188.0 23.8 %collective-permute-start.48 = (bf16[512,512]{1,0:T(8,128)(2,1)}, bf16[512,512]{1,0:T(8,128)(2,1)}, u32[]{:S(2)}, u32[]{:S(2)}) collective-permute-start(bf16[512,512]{1,0:T(8,128)(2,1)} %collective-permute-done.19.refs_3_.refs_4_), channel_id=1, source_target_pairs={{0,8},{4,12},{8,0},{12,4},{1,9},{5,13},{9,1},{13,5},{2,10},{6,14},... | collective-permute-start | bytes 1572872 | tf_op jit(solution)/shard_map/ppermute | solution.py:35
  188.5 23.2 %collective-permute-start.43 = (bf16[512,512]{1,0:T(8,128)(2,1)}, bf16[512,512]{1,0:T(8,128)(2,1)}, u32[]{:S(2)}, u32[]{:S(2)}) collective-permute-start(bf16[512,512]{1,0:T(8,128)(2,1)} %collective-permute-done.19.refs_3_.refs_4_), channel_id=1, source_target_pairs={{0,1},{1,2},{2,3},{3,0},{4,5},{5,6},{6,7},{7,4},{8,9},{9,10},{10,1... | collective-permute-start | bytes 1572872 | tf_op jit(solution)/shard_map/ppermute | solution.py:30
  191.0 12.0 %collective-permute-start.47 = (bf16[512,512]{1,0:T(8,128)(2,1)}, bf16[512,512]{1,0:T(8,128)(2,1)}, u32[]{:S(2)}, u32[]{:S(2)}) collective-permute-start(bf16[512,512]{1,0:T(8,128)(2,1)} %broadcast_select_fusion.4), channel_id=1, source_target_pairs={{0,4},{4,0},{8,12},{12,8},{1,5},{5,1},{9,13},{13,9},{2,6},{6,2},{1... | collective-permute-start | bytes 1572872 | tf_op jit(solution)/shard_map/ppermute | solution.py:35
  199.8 19.2 %collective-permute-start.51 = (bf16[512,512]{1,0:T(8,128)(2,1)}, bf16[512,512]{1,0:T(8,128)(2,1)}, u32[]{:S(2)}, u32[]{:S(2)}) collective-permute-start(bf16[512,512]{1,0:T(8,128)(2,1)} %collective-permute-done.28.refs_4_.refs_5_), channel_id=1, source_target_pairs={{0,8},{4,12},{8,0},{12,4},{1,9},{5,13},{9,1},{13,5},{2,10},{6,14},... | collective-permute-start | bytes 1572872 | tf_op jit(solution)/shard_map/ppermute | solution.py:35
  201.2 19.3 %collective-permute-start.46 = (bf16[512,512]{1,0:T(8,128)(2,1)}, bf16[512,512]{1,0:T(8,128)(2,1)}, u32[]{:S(2)}, u32[]{:S(2)}) collective-permute-start(bf16[512,512]{1,0:T(8,128)(2,1)} %collective-permute-done.28.refs_4_.refs_5_), channel_id=1, source_target_pairs={{0,1},{1,2},{2,3},{3,0},{4,5},{5,6},{6,7},{7,4},{8,9},{9,10},{10,1... | collective-permute-start | bytes 1572872 | tf_op jit(solution)/shard_map/ppermute | solution.py:30
  213.0 18.9 %collective-permute-start.50 = (bf16[512,512]{1,0:T(8,128)(2,1)}, bf16[512,512]{1,0:T(8,128)(2,1)}, u32[]{:S(2)}, u32[]{:S(2)}) collective-permute-start(bf16[512,512]{1,0:T(8,128)(2,1)} %collective-permute-done.31.refs_5_.refs_6_), channel_id=1, source_target_pairs={{0,8},{4,12},{8,0},{12,4},{1,9},{5,13},{9,1},{13,5},{2,10},{6,14},... | collective-permute-start | bytes 1572872 | tf_op jit(solution)/shard_map/ppermute | solution.py:35
  213.5 18.4 %collective-permute-start.49 = (bf16[512,512]{1,0:T(8,128)(2,1)}, bf16[512,512]{1,0:T(8,128)(2,1)}, u32[]{:S(2)}, u32[]{:S(2)}) collective-permute-start(bf16[512,512]{1,0:T(8,128)(2,1)} %collective-permute-done.31.refs_5_.refs_6_), channel_id=1, source_target_pairs={{0,1},{1,2},{2,3},{3,0},{4,5},{5,6},{6,7},{7,4},{8,9},{9,10},{10,1... | collective-permute-start | bytes 1572872 | tf_op jit(solution)/shard_map/ppermute | solution.py:30
  220.4 21.0 %collective-permute-start.56 = (bf16[512,512]{1,0:T(8,128)(2,1)}, bf16[512,512]{1,0:T(8,128)(2,1)}, u32[]{:S(2)}, u32[]{:S(2)}) collective-permute-start(bf16[512,512]{1,0:T(8,128)(2,1)} %collective-permute-done.34.refs_0_.refs_1_), channel_id=1, source_target_pairs={{0,8},{4,12},{8,0},{12,4},{1,9},{5,13},{9,1},{13,5},{2,10},{6,14},... | collective-permute-start | bytes 1572872 | tf_op jit(solution)/shard_map/ppermute | solution.py:35
  221.4 21.5 %collective-permute-start.55 = (bf16[512,512]{1,0:T(8,128)(2,1)}, bf16[512,512]{1,0:T(8,128)(2,1)}, u32[]{:S(2)}, u32[]{:S(2)}) collective-permute-start(bf16[512,512]{1,0:T(8,128)(2,1)} %collective-permute-done.48.refs_3_), channel_id=1, source_target_pairs={{0,1},{1,2},{2,3},{3,0},{4,5},{5,6},{6,7},{7,4},{8,9},{9,10},{10,1... | collective-permute-start | bytes 1572872 | tf_op jit(solution)/shard_map/ppermute | solution.py:30
  237.6 19.0 %collective-permute-start.61 = (bf16[512,512]{1,0:T(8,128)(2,1)}, bf16[512,512]{1,0:T(8,128)(2,1)}, u32[]{:S(2)}, u32[]{:S(2)}) collective-permute-start(bf16[512,512]{1,0:T(8,128)(2,1)} %collective-permute-done.37.refs_1_.refs_2_), channel_id=1, source_target_pairs={{0,8},{4,12},{8,0},{12,4},{1,9},{5,13},{9,1},{13,5},{2,10},{6,14},... | collective-permute-start | bytes 1572872 | tf_op jit(solution)/shard_map/ppermute | solution.py:35
  238.6 17.9 %collective-permute-start.62 = (bf16[512,512]{1,0:T(8,128)(2,1)}, bf16[512,512]{1,0:T(8,128)(2,1)}, u32[]{:S(2)}, u32[]{:S(2)}) collective-permute-start(bf16[512,512]{1,0:T(8,128)(2,1)} %collective-permute-done.51.refs_4_), channel_id=1, source_target_pairs={{0,1},{1,2},{2,3},{3,0},{4,5},{5,6},{6,7},{7,4},{8,9},{9,10},{10,1... | collective-permute-start | bytes 1572872 | tf_op jit(solution)/shard_map/ppermute | solution.py:30
  242.9 22.2 %collective-permute-start.57 = (bf16[512,512]{1,0:T(8,128)(2,1)}, bf16[512,512]{1,0:T(8,128)(2,1)}, u32[]{:S(2)}, u32[]{:S(2)}) collective-permute-start(bf16[512,512]{1,0:T(8,128)(2,1)} %collective-permute-done.40.refs_2_.refs_3_), channel_id=1, source_target_pairs={{0,8},{4,12},{8,0},{12,4},{1,9},{5,13},{9,1},{13,5},{2,10},{6,14},... | collective-permute-start | bytes 1572872 | tf_op jit(solution)/shard_map/ppermute | solution.py:35
  243.9 21.6 %collective-permute-start.58 = (bf16[512,512]{1,0:T(8,128)(2,1)}, bf16[512,512]{1,0:T(8,128)(2,1)}, u32[]{:S(2)}, u32[]{:S(2)}) collective-permute-start(bf16[512,512]{1,0:T(8,128)(2,1)} %collective-permute-done.50.refs_4_), channel_id=1, source_target_pairs={{0,1},{1,2},{2,3},{3,0},{4,5},{5,6},{6,7},{7,4},{8,9},{9,10},{10,1... | collective-permute-start | bytes 1572872 | tf_op jit(solution)/shard_map/ppermute | solution.py:30
  (29 other events, 246.0 us)

commit v2 on v1

--- a/solution.py
+++ b/solution.py
@@ -80,7 +80,8 @@
 
 def attend(queries, own_kv, prev_kv, start, first_head, heads):
     rows = queries.shape[0]
-    step = STEP if heads % STEP == 0 and first_head % STEP == 0 else 1
+    step = heads if first_head == 0 and heads <= 2 * STEP else STEP
+    step = step if heads % step == 0 and first_head % step == 0 else 1
     key_spec = pl.BlockSpec((PAGE, HD), lambda h: (0, 0))
     value_spec = pl.BlockSpec((PAGE, HD), lambda h: (0, 1))
     return pl.pallas_call(
@@ -331,14 +332,15 @@
     work = {
         done - 12: [("rows", 0)],
         done - 11: [("rows", 1)],
-        done - 10: [((0,), everything[:half], [0, 1], False)],
-        done - 9: [((0,), everything[half:], [0, 1], False)],
+        done - 9: [((0,), everything[:half], [0, 1], False)],
         done - 8: [(moved, [0, 1], [0, 1], False)],
+        done - 7: [((0,), everything[half:], [0, 1], False)],
         done - 6: [(moved, [2, 3], [0, 1], False)],
         done - 5: [("rows", 2)],
         done - 4: [(moved, [4, 5], [0, 1], False)],
-        done - 3: [((0,), everything, [2], False)],
+        done - 3: [((0,), everything[:half], [2], False)],
         done - 2: [(moved, [0, 1], [2], False)],
+        done - 1: [((0,), everything[half:], [2], False)],
         done: [(moved, [2, 3], [2], False)],
         done + 1: [("rows", 3)],
         done + 2: [((0,), everything, [3], True)],

time: 285 us -> 284 us (level)
  waiting for transfers between devices: 44.9 us -> 38.5 us
    ppermute x42, waiting for transfers between devices: 19.5 us -> 8.51 us  [over_tensor(): return lax.ppermute(value, 'tensor', [(t, t ^ bit) for t in range(count)])]
    ppermute x21, waiting for transfers between devices: 25.4 us -> 30 us  [from_behind(): return lax.ppermute(value, axis, pairs)]
    pallas_call x12 -> x13, Pallas kernels: 85.4 us -> 87.8 us  [gram(): pl.pallas_call(functools.partial(gram_kernel, runs, places, counts, start...]
  transfers between devices with their start and end apart: 65 -> 65, of which waited for: 17 -> 16; matrix products, arithmetic and copies ran while one was open for 13% -> 13% of each run, Pallas kernels for 42% -> 42%
where the time goes in v2:
time: 284 us; the launch traced here: 282 us
  Pallas kernels  126 us (44%)
  starting transfers between devices  74.9 us (26%)
  waiting for transfers between devices  38.5 us (14%)
  other arithmetic  36.5 us (13%)
  local copies, waits for them, and re-layouts  5.11 us (2%)
    pallas_call x13, Pallas kernels, gram(): pl.pallas_call(functools.partial(gram_kernel, runs, places, counts, start...  87.8 us
    ppermute x42, starting transfers between devices, over_tensor(): return lax.ppermute(value, 'tensor', [(t, t ^ bit) for t in range(count)])  55.5 us
    select_n x21, other arithmetic, per_device(): sent = jnp.where(even, *[jnp.concatenate(x, 1) for x in pair])  35.8 us
    ppermute x21, waiting for transfers between devices, from_behind(): return lax.ppermute(value, axis, pairs)  30 us
    pallas_call x6, Pallas kernels, attend(): pl.pallas_call(attend_kernel, grid=(heads // step,), out_shape=jax.ShapeD...  29.3 us
    ppermute x21, starting transfers between devices, from_behind(): return lax.ppermute(value, axis, pairs)  11.4 us
    pallas_call x4, Pallas kernels, rows_of(): pl.pallas_call(functools.partial(rows_kernel, widths, rows), out_shape=ja...  9.21 us
    ppermute x42, waiting for transfers between devices, over_tensor(): return lax.ppermute(value, 'tensor', [(t, t ^ bit) for t in range(count)])  8.51 us
  transfers between devices with their start and end apart: 65, of which 16 were waited for; matrix products, arithmetic and copies ran while one was open for 13% of the time, Pallas kernels for 42%

profile of v2, /device:TPU:1, one launch (start us, length us, event | category | flops | bytes accessed | tf_op | source)
XLA Modules:
  0.0 282.0 jit_solution(905392896358794019)
XLA Ops:
  1.2 4.0 %collective-permute-start = (bf16[512,256]{1,0:T(8,128)(2,1)S(1)}, bf16[512,256]{1,0:T(8,128)(2,1)S(1)}, u32[]{:S(2)}, u32[]{:S(2)}) collective-permute-start(bf16[512,256]{1,0:T(8,128)(2,1)S(1)} %pad_maximum_fusion.ko_ref.vo_ref), channel_id=1, source_target_pairs={{0,1},{1,2},{2,3},{4,5},{5,6},{6,7},{8,9},{9,10},{10,11},{12,13},{... | collective-permute-start | bytes 786440 | tf_op jit(solution)/shard_map/ppermute | solution.py:24
  6.0 3.9 %collective-permute-start.2 = (bf16[512,256]{1,0:T(8,128)(2,1)}, bf16[512,256]{1,0:T(8,128)(2,1)}, u32[]{:S(2)}, u32[]{:S(2)}) collective-permute-start(bf16[512,256]{1,0:T(8,128)(2,1)} %pad_maximum_fusion.1.ko_ref.vo_ref), channel_id=1, source_target_pairs={{0,1},{1,2},{2,3},{4,5},{5,6},{6,7},{8,9},{9,10},{10,11},{12,13},{... | collective-permute-start | bytes 786440 | tf_op jit(solution)/shard_map/ppermute | solution.py:24
  11.5 4.5 %shard_map.46.refs_0_.refs_2_ = bf16[512,512]{1,0:T(8,128)(2,1)} custom-call(s32[512,1]{1,0:T(8,128)} %copy.16.start_ref, bf16[512,3072]{1,0:T(8,128)(2,1)} %q_ref.11, bf16[512,256]{1,0:T(8,128)(2,1)} %copy-done.10, bf16[512,256]{1,0:T(8,128)(2,1)} %copy-done.7, bf16[512,256]{1,0:T(8,128)(2,1)} %copy-done.10, bf16[512,256]{1,0:T(8,128)(2,1)} %copy-done.7), custom_call_target="tpu_custom_call" | custom-call | flops 999999986991104 | bytes 1 | tf_op jit(solution)/shard_map/pallas_call | solution.py:87
  20.4 5.0 %shard_map.49.refs_1_.refs_4_ = bf16[512,512]{1,0:T(8,128)(2,1)} custom-call(s32[512,1]{1,0:T(8,128)} %copy.19.start_ref, bf16[512,3072]{1,0:T(8,128)(2,1)} %q_ref.11, bf16[512,256]{1,0:T(8,128)(2,1)} %copy-done.10, bf16[512,256]{1,0:T(8,128)(2,1)} %copy-done.7, bf16[512,256]{1,0:T(8,128)(2,1)} %copy-done.10, bf16[512,256]{1,0:T(8,128)(2,1)} %copy-done.7), custom_call_target="tpu_custom_call" | custom-call | flops 999999986991104 | bytes 1 | tf_op jit(solution)/shard_map/pallas_call | solution.py:87
  26.9 2.6 collective-permute-done.1.refs_0_.refs_3_
  30.4 7.2 %collective-permute-start.22 = (bf16[512,512]{1,0:T(8,128)(2,1)}, bf16[512,512]{1,0:T(8,128)(2,1)}, u32[]{:S(2)}, u32[]{:S(2)}) collective-permute-start(bf16[512,512]{1,0:T(8,128)(2,1)} %broadcast_select_fusion.17), channel_id=1, source_target_pairs={{0,4},{4,0},{8,12},{12,8},{1,5},{5,1},{9,13},{13,9},{2,6},{6,2},{1... | collective-permute-start | bytes 1572872 | tf_op jit(solution)/shard_map/ppermute | solution.py:35
  37.6 5.0 %shard_map.48.refs_2_.refs_6_ = bf16[512,512]{1,0:T(8,128)(2,1)} custom-call(s32[512,1]{1,0:T(8,128)} %copy.16.start_ref, bf16[512,3072]{1,0:T(8,128)(2,1)} %q_ref.11, bf16[512,256]{1,0:T(8,128)(2,1)} %copy-done.10, bf16[512,256]{1,0:T(8,128)(2,1)} %copy-done.7, bf16[512,256]{1,0:T(8,128)(2,1)} %copy-done.10, bf16[512,256]{1,0:T(8,128)(2,1)} %copy-done.7), custom_call_target="tpu_custom_call" | custom-call | flops 999999986991104 | bytes 1 | tf_op jit(solution)/shard_map/pallas_call | solution.py:87
  47.7 5.0 %shard_map.51.refs_3_.refs_2_ = bf16[512,512]{1,0:T(8,128)(2,1)} custom-call(s32[512,1]{1,0:T(8,128)} %copy.16.start_ref, bf16[512,3072]{1,0:T(8,128)(2,1)} %q_ref.11, bf16[512,256]{1,0:T(8,128)(2,1)} %collective-permute-done.2.kp_ref.vp_ref, bf16[512,256]{1,0:T(8,128)(2,1)} %pad_maximum_fusion.1.ko_ref.vo_ref, ...), custom_call_target="tpu_custom_call" | custom-call | flops 999999986991104 | bytes 1 | tf_op jit(solution)/shard_map/pallas_call | solution.py:87
  54.1 4.1 %collective-permute-done.4.refs_2_.refs_7_ = bf16[512,512]{1,0:T(8,128)(2,1)} collective-permute-done((bf16[512,512]{1,0:T(8,128)(2,1)}, bf16[512,512]{1,0:T(8,128)(2,1)}, u32[]{:S(2)}, u32[]{:S(2)}) %collective-permute-start.4) | collective-permute-done | bytes 524320 | tf_op jit(solution)/shard_map/ppermute | solution.py:30
  59.1 2.2 collective-permute-start.24
  61.3 4.9 %shard_map.47.refs_4_ = bf16[512,512]{1,0:T(8,128)(2,1)} custom-call(s32[512,1]{1,0:T(8,128)} %copy.16.start_ref, bf16[512,3072]{1,0:T(8,128)(2,1)} %q_ref.11, bf16[512,256]{1,0:T(8,128)(2,1)} %collective-permute-done.2.kp_ref.vp_ref, bf16[512,256]{1,0:T(8,128)(2,1)} %pad_maximum_fusion.1.ko_ref.vo_ref, ...), custom_call_target="tpu_custom_call" | custom-call | flops 999999986991104 | bytes 1 | tf_op jit(solution)/shard_map/pallas_call | solution.py:87
  72.1 5.0 %shard_map.50.refs_5_.refs_6_ = bf16[512,512]{1,0:T(8,128)(2,1)} custom-call(s32[512,1]{1,0:T(8,128)} %copy.16.start_ref, bf16[512,3072]{1,0:T(8,128)(2,1)} %q_ref.11, bf16[512,256]{1,0:T(8,128)(2,1)} %collective-permute-done.2.kp_ref.vp_ref, bf16[512,256]{1,0:T(8,128)(2,1)} %pad_maximum_fusion.1.ko_ref.vo_ref, ...), custom_call_target="tpu_custom_call" | custom-call | flops 999999986991104 | bytes 1 | tf_op jit(solution)/shard_map/pallas_call | solution.py:87
  79.4 2.5 collective-permute-done.6.refs_4_.refs_5_
  82.0 2.2 collective-permute-start.26
  85.5 7.7 %collective-permute-done.13.refs_5_.refs_7_ = bf16[512,512]{1,0:T(8,128)(2,1)} collective-permute-done((bf16[512,512]{1,0:T(8,128)(2,1)}, bf16[512,512]{1,0:T(8,128)(2,1)}, u32[]{:S(2)}, u32[]{:S(2)}) %collective-permute-start.13) | collective-permute-done | bytes 524320 | tf_op jit(solution)/shard_map/ppermute | solution.py:30
  95.9 2.3 shard_map.52.refs_0_
  99.7 4.0 %collective-permute-done.16.refs_3_ = bf16[512,512]{1,0:T(8,128)(2,1)} collective-permute-done((bf16[512,512]{1,0:T(8,128)(2,1)}, bf16[512,512]{1,0:T(8,128)(2,1)}, u32[]{:S(2)}, u32[]{:S(2)}) %collective-permute-start.16) | collective-permute-done | bytes 524320 | tf_op jit(solution)/shard_map/ppermute | solution.py:35
  104.5 1.9 broadcast_select_fusion.11
  107.4 2.3 shard_map.53.refs_1_
  111.2 4.5 %collective-permute-done.15.refs_1_.refs_2_ = bf16[512,512]{1,0:T(8,128)(2,1)} collective-permute-done((bf16[512,512]{1,0:T(8,128)(2,1)}, bf16[512,512]{1,0:T(8,128)(2,1)}, u32[]{:S(2)}, u32[]{:S(2)}) %collective-permute-start.15) | collective-permute-done | bytes 524320 | tf_op jit(solution)/shard_map/ppermute | solution.py:30
  115.7 1.9 broadcast_select_fusion.10
  118.7 6.6 %shard_map.54.refs_10_ = bf16[768,9216]{1,0:T(8,128)(2,1)} custom-call(bf16[768,512]{1,0:T(8,128)(2,1)} %shard_map.52.refs_0_, bf16[768,512]{1,0:T(8,128)(2,1)} %shard_map.53.refs_1_, bf16[512,512]{1,0:T(8,128)(2,1)} %shard_map.46.refs_0_.refs_2_, bf16[512,512]{1,0:T(8,128)(2,1)} %collective-permute-done.1.refs_0_.refs_3_, ...), custom_call_target="tpu_custom_call" | custom-call | flops 999999986991104 | bytes 1 | tf_op jit(solution)/shard_map/pallas_call | solution.py:252
  128.3 1.9 broadcast_select_fusion.9
  131.2 8.0 %shard_map.55.refs_8_ = bf16[768,9216]{1,0:T(8,128)(2,1)} custom-call(bf16[768,512]{1,0:T(8,128)(2,1)} %shard_map.52.refs_0_, bf16[768,512]{1,0:T(8,128)(2,1)} %shard_map.53.refs_1_, bf16[512,512]{1,0:T(8,128)(2,1)} %collective-permute-done.3.refs_2_, bf16[512,512]{1,0:T(8,128)(2,1)} %collective-permute-done.16.refs_3_, ...), custom_call_target="tpu_custom_call", output_to_operand_aliasing={{}: (10, {})} | custom-call | flops 999999986991104 | bytes 1 | tf_op jit(solution)/shard_map/pallas_call | solution.py:252
  142.3 1.9 broadcast_select_fusion.8
  145.7 6.7 %shard_map.57.refs_10_ = bf16[768,9216]{1,0:T(8,128)(2,1)} custom-call(bf16[768,512]{1,0:T(8,128)(2,1)} %shard_map.52.refs_0_, bf16[768,512]{1,0:T(8,128)(2,1)} %shard_map.53.refs_1_, bf16[512,512]{1,0:T(8,128)(2,1)} %shard_map.51.refs_3_.refs_2_, bf16[512,512]{1,0:T(8,128)(2,1)} %collective-permute-done.11.refs_3_, ...), custom_call_target="tpu_custom_call", output_to_operand_aliasing={{}: (8, {})} | custom-call | flops 999999986991104 | bytes 1 | tf_op jit(solution)/shard_map/pallas_call | solution.py:252
  153.6 1.9 broadcast_select_fusion.7
  156.9 8.0 %shard_map.58.refs_10_ = bf16[768,9216]{1,0:T(8,128)(2,1)} custom-call(bf16[768,512]{1,0:T(8,128)(2,1)} %shard_map.52.refs_0_, bf16[768,512]{1,0:T(8,128)(2,1)} %shard_map.53.refs_1_, bf16[512,512]{1,0:T(8,128)(2,1)} %collective-permute-done.5.refs_2_, bf16[512,512]{1,0:T(8,128)(2,1)} %collective-permute-done.20.refs_3_, ...), custom_call_target="tpu_custom_call", output_to_operand_aliasing={{}: (10, {})} | custom-call | flops 999999986991104 | bytes 1 | tf_op jit(solution)/shard_map/pallas_call | solution.py:252
  164.9 1.9 broadcast_select_fusion.6
  166.8 2.3 shard_map.56.refs_0_
  176.0 1.9 broadcast_select_fusion.5
  179.4 8.1 %shard_map.59.refs_4_ = bf16[768,9216]{1,0:T(8,128)(2,1)} custom-call(bf16[768,512]{1,0:T(8,128)(2,1)} %shard_map.52.refs_0_, bf16[768,512]{1,0:T(8,128)(2,1)} %shard_map.53.refs_1_, bf16[512,512]{1,0:T(8,128)(2,1)} %collective-permute-done.7.refs_2_, bf16[512,512]{1,0:T(8,128)(2,1)} %collective-permute-done.33.refs_3_, ...), custom_call_target="tpu_custom_call", output_to_operand_aliasing={{}: (10, {})} | custom-call | flops 999999986991104 | bytes 1 | tf_op jit(solution)/shard_map/pallas_call | solution.py:252
  190.8 5.3 %shard_map.60.refs_5_ = bf16[768,9216]{1,0:T(8,128)(2,1)} custom-call(bf16[768,512]{1,0:T(8,128)(2,1)} %shard_map.56.refs_0_, bf16[512,512]{1,0:T(8,128)(2,1)} %collective-permute-done.8.refs_0_.refs_1_, bf16[512,512]{1,0:T(8,128)(2,1)} %collective-permute-done.15.refs_1_.refs_2_, ...), custom_call_target="tpu_custom_call", output_to_operand_aliasing={{}: (4, {})} | custom-call | flops 999999986991104 | bytes 1 | tf_op jit(solution)/shard_map/pallas_call | solution.py:252
  202.0 6.3 %shard_map.61.refs_4_ = bf16[768,9216]{1,0:T(8,128)(2,1)} custom-call(bf16[768,512]{1,0:T(8,128)(2,1)} %shard_map.56.refs_0_, bf16[512,512]{1,0:T(8,128)(2,1)} %collective-permute-done.39.refs_1_, bf16[512,512]{1,0:T(8,128)(2,1)} %collective-permute-done.44.refs_2_, ...), custom_call_target="tpu_custom_call", output_to_operand_aliasing={{}: (5, {})} | custom-call | flops 999999986991104 | bytes 1 | tf_op jit(solution)/shard_map/pallas_call | solution.py:252
  210.3 1.9 broadcast_select_fusion.2
  213.1 5.4 %shard_map.63.refs_5_ = bf16[768,9216]{1,0:T(8,128)(2,1)} custom-call(bf16[768,512]{1,0:T(8,128)(2,1)} %shard_map.56.refs_0_, bf16[512,512]{1,0:T(8,128)(2,1)} %collective-permute-done.19.refs_3_.refs_1_, bf16[512,512]{1,0:T(8,128)(2,1)} %collective-permute-done.21.refs_4_.refs_2_, ...), custom_call_target="tpu_custom_call", output_to_operand_aliasing={{}: (4, {})} | custom-call | flops 999999986991104 | bytes 1 | tf_op jit(solution)/shard_map/pallas_call | solution.py:252
  221.0 1.9 broadcast_select_fusion.1
  224.3 6.3 %shard_map.64.refs_7_.refs_5_.refs_8_ = bf16[768,9216]{1,0:T(8,128)(2,1)} custom-call(bf16[768,512]{1,0:T(8,128)(2,1)} %shard_map.56.refs_0_, bf16[512,512]{1,0:T(8,128)(2,1)} %collective-permute-done.45.refs_1_, bf16[512,512]{1,0:T(8,128)(2,1)} %collective-permute-done.52.refs_2_, ...), custom_call_target="tpu_custom_call", output_to_operand_aliasing={{}: (5, {})} | custom-call | flops 999999986991104 | bytes 1 | tf_op jit(solution)/shard_map/pallas_call | solution.py:252
  230.6 1.9 broadcast_select_fusion
  234.2 2.3 shard_map.62.refs_0_.refs_1_
  237.7 2.8 collective-permute-done.56.refs_1_
  243.5 2.8 %maximum_select_fusion = bf16[512,1024]{1,0:T(8,128)(2,1)} fusion(bf16[512,512]{1,0:T(8,128)(2,1)} %collective-permute-done.55.refs_3_, bf16[512,512]{1,0:T(8,128)(2,1)} %collective-permute-done.56.refs_1_, bf16[512,512]{1,0:T(8,128)(2,1)} %collective-permute-done.43.refs_3_.refs_4_, bf16[512,512]{1,0:T(8,128)(2,1)} %collective-permute-done.34.refs_0_.refs_1_, ...), kind=kLoop, calls=%fused_computation | loop fusion | flops 4718592 | bytes 3145729 | tf_op jit(solution)/shard_map/jit(_where)/select_n | solution.py:379
  247.8 7.9 %shard_map.65.refs_6_ = f32[768,9216]{1,0:T(8,128)} custom-call(bf16[768,512]{1,0:T(8,128)(2,1)} %shard_map.62.refs_0_.refs_1_, bf16[512,512]{1,0:T(8,128)(2,1)} %collective-permute-done.34.refs_0_.refs_1_, bf16[512,512]{1,0:T(8,128)(2,1)} %collective-permute-done.37.refs_1_.refs_2_, bf16[512,512]{1,0:T(8,128)(2,1)} %collective-permute-done.40.refs_2_.refs_3_, ...), custom_call_target="tpu_custom_call" | custom-call | flops 999999986991104 | bytes 1 | tf_op jit(solution)/shard_map/pallas_call | solution.py:252
  255.7 2.9 %maximum_select_fusion.1 = bf16[512,1024]{1,0:T(8,128)(2,1)} fusion(bf16[512,512]{1,0:T(8,128)(2,1)} %collective-permute-done.62.refs_5_, bf16[512,512]{1,0:T(8,128)(2,1)} %collective-permute-done.61.refs_2_, bf16[512,512]{1,0:T(8,128)(2,1)} %collective-permute-done.46.refs_4_.refs_5_, bf16[512,512]{1,0:T(8,128)(2,1)} %collective-permute-done.37.refs_1_.refs_2_, ...), kind=kLoop, calls=%fused_computation.1 | loop fusion | flops 4718592 | bytes 3145729 | tf_op jit(solution)/shard_map/jit(_where)/select_n | solution.py:379
  258.6 5.7 %shard_map.66.refs_9_ = f32[768,9216]{1,0:T(8,128)} custom-call(bf16[768,512]{1,0:T(8,128)(2,1)} %shard_map.62.refs_0_.refs_1_, bf16[512,512]{1,0:T(8,128)(2,1)} %collective-permute-done.56.refs_1_, bf16[512,1024]{1,0:T(8,128)(2,1)} %collective-permute-done.60.refs_2_.refs_4_, ...), custom_call_target="tpu_custom_call", output_to_operand_aliasing={{}: (6, {})} | custom-call | flops 999999986991104 | bytes 1 | tf_op jit(solution)/shard_map/pallas_call | solution.py:252
  264.3 2.9 %maximum_select_fusion.2 = bf16[512,1024]{1,0:T(8,128)(2,1)} fusion(bf16[512,512]{1,0:T(8,128)(2,1)} %collective-permute-done.58.refs_5_, bf16[512,512]{1,0:T(8,128)(2,1)} %collective-permute-done.57.refs_2_, bf16[512,512]{1,0:T(8,128)(2,1)} %collective-permute-done.49.refs_5_.refs_6_, bf16[512,512]{1,0:T(8,128)(2,1)} %collective-permute-done.40.refs_2_.refs_3_, ...), kind=kLoop, calls=%fused_computation.2 | loop fusion | flops 4718592 | bytes 3145729 | tf_op jit(solution)/shard_map/jit(_where)/select_n | solution.py:379
  268.2 6.8 %shard_map.67.refs_9_ = f32[768,9216]{1,0:T(8,128)} custom-call(bf16[768,512]{1,0:T(8,128)(2,1)} %shard_map.56.refs_0_, bf16[768,512]{1,0:T(8,128)(2,1)} %shard_map.62.refs_0_.refs_1_, bf16[512,512]{1,0:T(8,128)(2,1)} %collective-permute-done.61.refs_2_, bf16[512,1024]{1,0:T(8,128)(2,1)} %collective-permute-done.63.refs_3_.refs_7_, ...), custom_call_target="tpu_custom_call", output_to_operand_aliasing={{}: (9, {})} | custom-call | flops 999999986991104 | bytes 1 | tf_op jit(solution)/shard_map/pallas_call | solution.py:252
  275.0 6.8 %shard_map.68 = f32[768,9216]{1,0:T(8,128)} custom-call(bf16[768,512]{1,0:T(8,128)(2,1)} %shard_map.56.refs_0_, bf16[768,512]{1,0:T(8,128)(2,1)} %shard_map.62.refs_0_.refs_1_, bf16[512,512]{1,0:T(8,128)(2,1)} %collective-permute-done.57.refs_2_, bf16[512,1024]{1,0:T(8,128)(2,1)} %collective-permute-done.64.refs_3_.refs_7_, ...), custom_call_target="tpu_custom_call", output_to_operand_aliasing={{}: (9, {})} | custom-call | flops 999999986991104 | bytes 1 | tf_op jit(solution)/shard_map/pallas_call | solution.py:252
  (154 shorter events, 79.6 us)
Async XLA Ops:
  6.0 12.9 %collective-permute-start.2 = (bf16[512,256]{1,0:T(8,128)(2,1)}, bf16[512,256]{1,0:T(8,128)(2,1)}, u32[]{:S(2)}, u32[]{:S(2)}) collective-permute-start(bf16[512,256]{1,0:T(8,128)(2,1)} %pad_maximum_fusion.1.ko_ref.vo_ref), channel_id=1, source_target_pairs={{0,1},{1,2},{2,3},{4,5},{5,6},{6,7},{8,9},{9,10},{10,11},{12,13},{... | collective-permute-start | bytes 786440 | tf_op jit(solution)/shard_map/ppermute | solution.py:24
  16.0 13.5 %collective-permute-start.1 = (bf16[512,512]{1,0:T(8,128)(2,1)}, bf16[512,512]{1,0:T(8,128)(2,1)}, u32[]{:S(2)}, u32[]{:S(2)}) collective-permute-start(bf16[512,512]{1,0:T(8,128)(2,1)} %shard_map.46.refs_0_.refs_2_), channel_id=1, source_target_pairs={{0,1},{1,2},{2,3},{3,0},{4,5},{5,6},{6,7},{7,4},{8,9},{9,10},{10,1... | collective-permute-start | bytes 1572872 | tf_op jit(solution)/shard_map/ppermute | solution.py:30
  17.6 11.9 %collective-permute-start.3 = (bf16[512,512]{1,0:T(8,128)(2,1)}, bf16[512,512]{1,0:T(8,128)(2,1)}, u32[]{:S(2)}, u32[]{:S(2)}) collective-permute-start(bf16[512,512]{1,0:T(8,128)(2,1)} %shard_map.46.refs_0_.refs_2_), channel_id=1, source_target_pairs={{0,8},{4,12},{8,0},{12,4},{1,9},{5,13},{9,1},{13,5},{2,10},{6,14},... | collective-permute-start | bytes 1572872 | tf_op jit(solution)/shard_map/ppermute | solution.py:35
  25.4 19.8 %collective-permute-start.10 = (bf16[512,512]{1,0:T(8,128)(2,1)}, bf16[512,512]{1,0:T(8,128)(2,1)}, u32[]{:S(2)}, u32[]{:S(2)}) collective-permute-start(bf16[512,512]{1,0:T(8,128)(2,1)} %shard_map.49.refs_1_.refs_4_), channel_id=1, source_target_pairs={{0,8},{4,12},{8,0},{12,4},{1,9},{5,13},{9,1},{13,5},{2,10},{6,14},... | collective-permute-start | bytes 1572872 | tf_op jit(solution)/shard_map/ppermute | solution.py:35
  25.6 19.6 %collective-permute-start.9 = (bf16[512,512]{1,0:T(8,128)(2,1)}, bf16[512,512]{1,0:T(8,128)(2,1)}, u32[]{:S(2)}, u32[]{:S(2)}) collective-permute-start(bf16[512,512]{1,0:T(8,128)(2,1)} %shard_map.49.refs_1_.refs_4_), channel_id=1, source_target_pairs={{0,1},{1,2},{2,3},{3,0},{4,5},{5,6},{6,7},{7,4},{8,9},{9,10},{10,1... | collective-permute-start | bytes 1572872 | tf_op jit(solution)/shard_map/ppermute | solution.py:30
  30.4 14.8 %collective-permute-start.22 = (bf16[512,512]{1,0:T(8,128)(2,1)}, bf16[512,512]{1,0:T(8,128)(2,1)}, u32[]{:S(2)}, u32[]{:S(2)}) collective-permute-start(bf16[512,512]{1,0:T(8,128)(2,1)} %broadcast_select_fusion.17), channel_id=1, source_target_pairs={{0,4},{4,0},{8,12},{12,8},{1,5},{5,1},{9,13},{13,9},{2,6},{6,2},{1... | collective-permute-start | bytes 1572872 | tf_op jit(solution)/shard_map/ppermute | solution.py:35
  42.5 15.7 %collective-permute-start.4 = (bf16[512,512]{1,0:T(8,128)(2,1)}, bf16[512,512]{1,0:T(8,128)(2,1)}, u32[]{:S(2)}, u32[]{:S(2)}) collective-permute-start(bf16[512,512]{1,0:T(8,128)(2,1)} %shard_map.48.refs_2_.refs_6_), channel_id=1, source_target_pairs={{0,1},{1,2},{2,3},{3,0},{4,5},{5,6},{6,7},{7,4},{8,9},{9,10},{10,1... | collective-permute-start | bytes 1572872 | tf_op jit(solution)/shard_map/ppermute | solution.py:30
  43.8 14.4 %collective-permute-start.5 = (bf16[512,512]{1,0:T(8,128)(2,1)}, bf16[512,512]{1,0:T(8,128)(2,1)}, u32[]{:S(2)}, u32[]{:S(2)}) collective-permute-start(bf16[512,512]{1,0:T(8,128)(2,1)} %shard_map.48.refs_2_.refs_6_), channel_id=1, source_target_pairs={{0,8},{4,12},{8,0},{12,4},{1,9},{5,13},{9,1},{13,5},{2,10},{6,14},... | collective-permute-start | bytes 1572872 | tf_op jit(solution)/shard_map/ppermute | solution.py:35
  46.0 12.2 %collective-permute-start.23 = (bf16[512,512]{1,0:T(8,128)(2,1)}, bf16[512,512]{1,0:T(8,128)(2,1)}, u32[]{:S(2)}, u32[]{:S(2)}) collective-permute-start(bf16[512,512]{1,0:T(8,128)(2,1)} %broadcast_select_fusion.16), channel_id=1, source_target_pairs={{0,4},{4,0},{8,12},{12,8},{1,5},{5,1},{9,13},{13,9},{2,6},{6,2},{1... | collective-permute-start | bytes 1572872 | tf_op jit(solution)/shard_map/ppermute | solution.py:35
  52.6 16.8 %collective-permute-start.11 = (bf16[512,512]{1,0:T(8,128)(2,1)}, bf16[512,512]{1,0:T(8,128)(2,1)}, u32[]{:S(2)}, u32[]{:S(2)}) collective-permute-start(bf16[512,512]{1,0:T(8,128)(2,1)} %shard_map.51.refs_3_.refs_2_), channel_id=1, source_target_pairs={{0,1},{1,2},{2,3},{3,0},{4,5},{5,6},{6,7},{7,4},{8,9},{9,10},{10,1... | collective-permute-start | bytes 1572872 | tf_op jit(solution)/shard_map/ppermute | solution.py:30
  53.9 15.5 %collective-permute-start.12 = (bf16[512,512]{1,0:T(8,128)(2,1)}, bf16[512,512]{1,0:T(8,128)(2,1)}, u32[]{:S(2)}, u32[]{:S(2)}) collective-permute-start(bf16[512,512]{1,0:T(8,128)(2,1)} %shard_map.51.refs_3_.refs_2_), channel_id=1, source_target_pairs={{0,8},{4,12},{8,0},{12,4},{1,9},{5,13},{9,1},{13,5},{2,10},{6,14},... | collective-permute-start | bytes 1572872 | tf_op jit(solution)/shard_map/ppermute | solution.py:35
  66.3 15.7 %collective-permute-start.6 = (bf16[512,512]{1,0:T(8,128)(2,1)}, bf16[512,512]{1,0:T(8,128)(2,1)}, u32[]{:S(2)}, u32[]{:S(2)}) collective-permute-start(bf16[512,512]{1,0:T(8,128)(2,1)} %shard_map.47.refs_4_), channel_id=1, source_target_pairs={{0,1},{1,2},{2,3},{3,0},{4,5},{5,6},{6,7},{7,4},{8,9},{9,10},{10,1... | collective-permute-start | bytes 1572872 | tf_op jit(solution)/shard_map/ppermute | solution.py:30
  67.3 14.6 %collective-permute-start.7 = (bf16[512,512]{1,0:T(8,128)(2,1)}, bf16[512,512]{1,0:T(8,128)(2,1)}, u32[]{:S(2)}, u32[]{:S(2)}) collective-permute-start(bf16[512,512]{1,0:T(8,128)(2,1)} %shard_map.47.refs_4_), channel_id=1, source_target_pairs={{0,8},{4,12},{8,0},{12,4},{1,9},{5,13},{9,1},{13,5},{2,10},{6,14},... | collective-permute-start | bytes 1572872 | tf_op jit(solution)/shard_map/ppermute | solution.py:35
  70.3 11.6 %collective-permute-start.25 = (bf16[512,512]{1,0:T(8,128)(2,1)}, bf16[512,512]{1,0:T(8,128)(2,1)}, u32[]{:S(2)}, u32[]{:S(2)}) collective-permute-start(bf16[512,512]{1,0:T(8,128)(2,1)} %broadcast_select_fusion.14), channel_id=1, source_target_pairs={{0,4},{4,0},{8,12},{12,8},{1,5},{5,1},{9,13},{13,9},{2,6},{6,2},{1... | collective-permute-start | bytes 1572872 | tf_op jit(solution)/shard_map/ppermute | solution.py:35
  77.1 16.1 %collective-permute-start.13 = (bf16[512,512]{1,0:T(8,128)(2,1)}, bf16[512,512]{1,0:T(8,128)(2,1)}, u32[]{:S(2)}, u32[]{:S(2)}) collective-permute-start(bf16[512,512]{1,0:T(8,128)(2,1)} %shard_map.50.refs_5_.refs_6_), channel_id=1, source_target_pairs={{0,1},{1,2},{2,3},{3,0},{4,5},{5,6},{6,7},{7,4},{8,9},{9,10},{10,1... | collective-permute-start | bytes 1572872 | tf_op jit(solution)/shard_map/ppermute | solution.py:30
  78.1 15.2 %collective-permute-start.14 = (bf16[512,512]{1,0:T(8,128)(2,1)}, bf16[512,512]{1,0:T(8,128)(2,1)S(1)}, u32[]{:S(2)}, u32[]{:S(2)}) collective-permute-start(bf16[512,512]{1,0:T(8,128)(2,1)} %shard_map.50.refs_5_.refs_6_), channel_id=1, source_target_pairs={{0,8},{4,12},{8,0},{12,4},{1,9},{5,13},{9,1},{13,5},{2,10},{6,14},... | collective-permute-start | bytes 1572872 | tf_op jit(solution)/shard_map/ppermute | solution.py:35
  82.0 11.3 %collective-permute-start.26 = (bf16[512,512]{1,0:T(8,128)(2,1)S(1)}, bf16[512,512]{1,0:T(8,128)(2,1)}, u32[]{:S(2)}, u32[]{:S(2)}) collective-permute-start(bf16[512,512]{1,0:T(8,128)(2,1)S(1)} %broadcast_select_fusion.13), channel_id=1, source_target_pairs={{0,4},{4,0},{8,12},{12,8},{1,5},{5,1},{9,13},{13,9},{2,6},{6,2},{1... | collective-permute-start | bytes 1572872 | tf_op jit(solution)/shard_map/ppermute | solution.py:35
  84.2 19.4 %collective-permute-start.16 = (bf16[512,512]{1,0:T(8,128)(2,1)}, bf16[512,512]{1,0:T(8,128)(2,1)}, u32[]{:S(2)}, u32[]{:S(2)}) collective-permute-start(bf16[512,512]{1,0:T(8,128)(2,1)} %collective-permute-done.1.refs_0_.refs_3_), channel_id=1, source_target_pairs={{0,8},{4,12},{8,0},{12,4},{1,9},{5,13},{9,1},{13,5},{2,10},{6,14},... | collective-permute-start | bytes 1572872 | tf_op jit(solution)/shard_map/ppermute | solution.py:35
  85.5 18.9 %collective-permute-start.8 = (bf16[512,512]{1,0:T(8,128)(2,1)}, bf16[512,512]{1,0:T(8,128)(2,1)}, u32[]{:S(2)}, u32[]{:S(2)}) collective-permute-start(bf16[512,512]{1,0:T(8,128)(2,1)} %collective-permute-done.1.refs_0_.refs_3_), channel_id=1, source_target_pairs={{0,1},{1,2},{2,3},{3,0},{4,5},{5,6},{6,7},{7,4},{8,9},{9,10},{10,1... | collective-permute-start | bytes 1572872 | tf_op jit(solution)/shard_map/ppermute | solution.py:30
  98.2 17.5 %collective-permute-start.15 = (bf16[512,512]{1,0:T(8,128)(2,1)}, bf16[512,512]{1,0:T(8,128)(2,1)}, u32[]{:S(2)}, u32[]{:S(2)}) collective-permute-start(bf16[512,512]{1,0:T(8,128)(2,1)} %collective-permute-done.9.refs_1_.refs_5_), channel_id=1, source_target_pairs={{0,1},{1,2},{2,3},{3,0},{4,5},{5,6},{6,7},{7,4},{8,9},{9,10},{10,1... | collective-permute-start | bytes 1572872 | tf_op jit(solution)/shard_map/ppermute | solution.py:30
  98.3 17.4 %collective-permute-start.18 = (bf16[512,512]{1,0:T(8,128)(2,1)}, bf16[512,512]{1,0:T(8,128)(2,1)}, u32[]{:S(2)}, u32[]{:S(2)}) collective-permute-start(bf16[512,512]{1,0:T(8,128)(2,1)} %collective-permute-done.9.refs_1_.refs_5_), channel_id=1, source_target_pairs={{0,8},{4,12},{8,0},{12,4},{1,9},{5,13},{9,1},{13,5},{2,10},{6,14},... | collective-permute-start | bytes 1572872 | tf_op jit(solution)/shard_map/ppermute | solution.py:35
  109.7 17.2 %collective-permute-start.17 = (bf16[512,512]{1,0:T(8,128)(2,1)}, bf16[512,512]{1,0:T(8,128)(2,1)}, u32[]{:S(2)}, u32[]{:S(2)}) collective-permute-start(bf16[512,512]{1,0:T(8,128)(2,1)} %collective-permute-done.4.refs_2_.refs_7_), channel_id=1, source_target_pairs={{0,1},{1,2},{2,3},{3,0},{4,5},{5,6},{6,7},{7,4},{8,9},{9,10},{10,1... | collective-permute-start | bytes 1572872 | tf_op jit(solution)/shard_map/ppermute | solution.py:30
  109.8 17.2 %collective-permute-start.20 = (bf16[512,512]{1,0:T(8,128)(2,1)}, bf16[512,512]{1,0:T(8,128)(2,1)}, u32[]{:S(2)}, u32[]{:S(2)}) collective-permute-start(bf16[512,512]{1,0:T(8,128)(2,1)} %collective-permute-done.4.refs_2_.refs_7_), channel_id=1, source_target_pairs={{0,8},{4,12},{8,0},{12,4},{1,9},{5,13},{9,1},{13,5},{2,10},{6,14},... | collective-permute-start | bytes 1572872 | tf_op jit(solution)/shard_map/ppermute | solution.py:35
  125.3 15.7 %collective-permute-start.19 = (bf16[512,512]{1,0:T(8,128)(2,1)}, bf16[512,512]{1,0:T(8,128)(2,1)}, u32[]{:S(2)}, u32[]{:S(2)}) collective-permute-start(bf16[512,512]{1,0:T(8,128)(2,1)} %collective-permute-done.11.refs_3_), channel_id=1, source_target_pairs={{0,1},{1,2},{2,3},{3,0},{4,5},{5,6},{6,7},{7,4},{8,9},{9,10},{10,1... | collective-permute-start | bytes 1572872 | tf_op jit(solution)/shard_map/ppermute | solution.py:30
  125.4 15.7 %collective-permute-start.30 = (bf16[512,512]{1,0:T(8,128)(2,1)}, bf16[512,512]{1,0:T(8,128)(2,1)}, u32[]{:S(2)}, u32[]{:S(2)}) collective-permute-start(bf16[512,512]{1,0:T(8,128)(2,1)} %collective-permute-done.11.refs_3_), channel_id=1, source_target_pairs={{0,8},{4,12},{8,0},{12,4},{1,9},{5,13},{9,1},{13,5},{2,10},{6,14},... | collective-permute-start | bytes 1572872 | tf_op jit(solution)/shard_map/ppermute | solution.py:35
  127.0 25.4 %collective-permute-start.33 = (bf16[512,512]{1,0:T(8,128)(2,1)}, bf16[512,512]{1,0:T(8,128)(2,1)}, u32[]{:S(2)}, u32[]{:S(2)}) collective-permute-start(bf16[512,512]{1,0:T(8,128)(2,1)} %collective-permute-done.6.refs_4_.refs_5_), channel_id=1, source_target_pairs={{0,8},{4,12},{8,0},{12,4},{1,9},{5,13},{9,1},{13,5},{2,10},{6,14},... | collective-permute-start | bytes 1572872 | tf_op jit(solution)/shard_map/ppermute | solution.py:35
  128.3 24.1 %collective-permute-start.21 = (bf16[512,512]{1,0:T(8,128)(2,1)}, bf16[512,512]{1,0:T(8,128)(2,1)}, u32[]{:S(2)}, u32[]{:S(2)}) collective-permute-start(bf16[512,512]{1,0:T(8,128)(2,1)} %collective-permute-done.6.refs_4_.refs_5_), channel_id=1, source_target_pairs={{0,1},{1,2},{2,3},{3,0},{4,5},{5,6},{6,7},{7,4},{8,9},{9,10},{10,1... | collective-permute-start | bytes 1572872 | tf_op jit(solution)/shard_map/ppermute | solution.py:30
  130.2 12.2 %collective-permute-start.32 = (bf16[512,512]{1,0:T(8,128)(2,1)}, bf16[512,512]{1,0:T(8,128)(2,1)}, u32[]{:S(2)}, u32[]{:S(2)}) collective-permute-start(bf16[512,512]{1,0:T(8,128)(2,1)} %broadcast_select_fusion.9), channel_id=1, source_target_pairs={{0,4},{4,0},{8,12},{12,8},{1,5},{5,1},{9,13},{13,9},{2,6},{6,2},{1... | collective-permute-start | bytes 1572872 | tf_op jit(solution)/shard_map/ppermute | solution.py:35
  141.0 23.9 %collective-permute-start.36 = (bf16[512,512]{1,0:T(8,128)(2,1)}, bf16[512,512]{1,0:T(8,128)(2,1)}, u32[]{:S(2)}, u32[]{:S(2)}) collective-permute-start(bf16[512,512]{1,0:T(8,128)(2,1)} %collective-permute-done.13.refs_5_.refs_7_), channel_id=1, source_target_pairs={{0,8},{4,12},{8,0},{12,4},{1,9},{5,13},{9,1},{13,5},{2,10},{6,14},... | collective-permute-start | bytes 1572872 | tf_op jit(solution)/shard_map/ppermute | solution.py:35
  142.3 22.6 %collective-permute-start.31 = (bf16[512,512]{1,0:T(8,128)(2,1)}, bf16[512,512]{1,0:T(8,128)(2,1)}, u32[]{:S(2)}, u32[]{:S(2)}) collective-permute-start(bf16[512,512]{1,0:T(8,128)(2,1)} %collective-permute-done.13.refs_5_.refs_7_), channel_id=1, source_target_pairs={{0,1},{1,2},{2,3},{3,0},{4,5},{5,6},{6,7},{7,4},{8,9},{9,10},{10,1... | collective-permute-start | bytes 1572872 | tf_op jit(solution)/shard_map/ppermute | solution.py:30
  152.4 20.6 %collective-permute-start.39 = (bf16[512,512]{1,0:T(8,128)(2,1)}, bf16[512,512]{1,0:T(8,128)(2,1)}, u32[]{:S(2)}, u32[]{:S(2)}) collective-permute-start(bf16[512,512]{1,0:T(8,128)(2,1)} %collective-permute-done.8.refs_0_.refs_1_), channel_id=1, source_target_pairs={{0,8},{4,12},{8,0},{12,4},{1,9},{5,13},{9,1},{13,5},{2,10},{6,14},... | collective-permute-start | bytes 1572872 | tf_op jit(solution)/shard_map/ppermute | solution.py:35
  153.6 21.2 %collective-permute-start.34 = (bf16[512,512]{1,0:T(8,128)(2,1)}, bf16[512,512]{1,0:T(8,128)(2,1)}, u32[]{:S(2)}, u32[]{:S(2)}) collective-permute-start(bf16[512,512]{1,0:T(8,128)(2,1)} %collective-permute-done.8.refs_0_.refs_1_), channel_id=1, source_target_pairs={{0,1},{1,2},{2,3},{3,0},{4,5},{5,6},{6,7},{7,4},{8,9},{9,10},{10,1... | collective-permute-start | bytes 1572872 | tf_op jit(solution)/shard_map/ppermute | solution.py:30
  169.1 18.3 %collective-permute-start.42 = (bf16[512,512]{1,0:T(8,128)(2,1)}, bf16[512,512]{1,0:T(8,128)(2,1)}, u32[]{:S(2)}, u32[]{:S(2)}) collective-permute-start(bf16[512,512]{1,0:T(8,128)(2,1)} %collective-permute-done.15.refs_1_.refs_2_), channel_id=1, source_target_pairs={{0,8},{4,12},{8,0},{12,4},{1,9},{5,13},{9,1},{13,5},{2,10},{6,14},... | collective-permute-start | bytes 1572872 | tf_op jit(solution)/shard_map/ppermute | solution.py:35
  170.2 17.2 %collective-permute-start.37 = (bf16[512,512]{1,0:T(8,128)(2,1)}, bf16[512,512]{1,0:T(8,128)(2,1)}, u32[]{:S(2)}, u32[]{:S(2)}) collective-permute-start(bf16[512,512]{1,0:T(8,128)(2,1)} %collective-permute-done.15.refs_1_.refs_2_), channel_id=1, source_target_pairs={{0,1},{1,2},{2,3},{3,0},{4,5},{5,6},{6,7},{7,4},{8,9},{9,10},{10,1... | collective-permute-start | bytes 1572872 | tf_op jit(solution)/shard_map/ppermute | solution.py:30
  174.7 21.4 %collective-permute-start.45 = (bf16[512,512]{1,0:T(8,128)(2,1)}, bf16[512,512]{1,0:T(8,128)(2,1)}, u32[]{:S(2)}, u32[]{:S(2)}) collective-permute-start(bf16[512,512]{1,0:T(8,128)(2,1)} %collective-permute-done.17.refs_2_.refs_3_), channel_id=1, source_target_pairs={{0,8},{4,12},{8,0},{12,4},{1,9},{5,13},{9,1},{13,5},{2,10},{6,14},... | collective-permute-start | bytes 1572872 | tf_op jit(solution)/shard_map/ppermute | solution.py:35
  176.0 20.9 %collective-permute-start.40 = (bf16[512,512]{1,0:T(8,128)(2,1)}, bf16[512,512]{1,0:T(8,128)(2,1)}, u32[]{:S(2)}, u32[]{:S(2)}) collective-permute-start(bf16[512,512]{1,0:T(8,128)(2,1)} %collective-permute-done.17.refs_2_.refs_3_), channel_id=1, source_target_pairs={{0,1},{1,2},{2,3},{3,0},{4,5},{5,6},{6,7},{7,4},{8,9},{9,10},{10,1... | collective-permute-start | bytes 1572872 | tf_op jit(solution)/shard_map/ppermute | solution.py:30
  187.5 20.9 %collective-permute-start.48 = (bf16[512,512]{1,0:T(8,128)(2,1)}, bf16[512,512]{1,0:T(8,128)(2,1)}, u32[]{:S(2)}, u32[]{:S(2)}) collective-permute-start(bf16[512,512]{1,0:T(8,128)(2,1)} %collective-permute-done.19.refs_3_.refs_1_), channel_id=1, source_target_pairs={{0,8},{4,12},{8,0},{12,4},{1,9},{5,13},{9,1},{13,5},{2,10},{6,14},... | collective-permute-start | bytes 1572872 | tf_op jit(solution)/shard_map/ppermute | solution.py:35
  187.6 20.8 %collective-permute-start.43 = (bf16[512,512]{1,0:T(8,128)(2,1)}, bf16[512,512]{1,0:T(8,128)(2,1)}, u32[]{:S(2)}, u32[]{:S(2)}) collective-permute-start(bf16[512,512]{1,0:T(8,128)(2,1)} %collective-permute-done.19.refs_3_.refs_1_), channel_id=1, source_target_pairs={{0,1},{1,2},{2,3},{3,0},{4,5},{5,6},{6,7},{7,4},{8,9},{9,10},{10,1... | collective-permute-start | bytes 1572872 | tf_op jit(solution)/shard_map/ppermute | solution.py:30
  196.9 21.6 %collective-permute-start.51 = (bf16[512,512]{1,0:T(8,128)(2,1)}, bf16[512,512]{1,0:T(8,128)(2,1)}, u32[]{:S(2)}, u32[]{:S(2)}) collective-permute-start(bf16[512,512]{1,0:T(8,128)(2,1)} %collective-permute-done.21.refs_4_.refs_2_), channel_id=1, source_target_pairs={{0,8},{4,12},{8,0},{12,4},{1,9},{5,13},{9,1},{13,5},{2,10},{6,14},... | collective-permute-start | bytes 1572872 | tf_op jit(solution)/shard_map/ppermute | solution.py:35
  198.5 20.9 %collective-permute-start.46 = (bf16[512,512]{1,0:T(8,128)(2,1)}, bf16[512,512]{1,0:T(8,128)(2,1)}, u32[]{:S(2)}, u32[]{:S(2)}) collective-permute-start(bf16[512,512]{1,0:T(8,128)(2,1)} %collective-permute-done.21.refs_4_.refs_2_), channel_id=1, source_target_pairs={{0,1},{1,2},{2,3},{3,0},{4,5},{5,6},{6,7},{7,4},{8,9},{9,10},{10,1... | collective-permute-start | bytes 1572872 | tf_op jit(solution)/shard_map/ppermute | solution.py:30
  208.4 22.2 %collective-permute-start.50 = (bf16[512,512]{1,0:T(8,128)(2,1)}, bf16[512,512]{1,0:T(8,128)(2,1)}, u32[]{:S(2)}, u32[]{:S(2)}) collective-permute-start(bf16[512,512]{1,0:T(8,128)(2,1)} %collective-permute-done.31.refs_5_.refs_3_), channel_id=1, source_target_pairs={{0,8},{4,12},{8,0},{12,4},{1,9},{5,13},{9,1},{13,5},{2,10},{6,14},... | collective-permute-start | bytes 1572872 | tf_op jit(solution)/shard_map/ppermute | solution.py:35
  209.7 20.9 %collective-permute-start.49 = (bf16[512,512]{1,0:T(8,128)(2,1)}, bf16[512,512]{1,0:T(8,128)(2,1)}, u32[]{:S(2)}, u32[]{:S(2)}) collective-permute-start(bf16[512,512]{1,0:T(8,128)(2,1)} %collective-permute-done.31.refs_5_.refs_3_), channel_id=1, source_target_pairs={{0,1},{1,2},{2,3},{3,0},{4,5},{5,6},{6,7},{7,4},{8,9},{9,10},{10,1... | collective-permute-start | bytes 1572872 | tf_op jit(solution)/shard_map/ppermute | solution.py:30
  219.4 21.0 %collective-permute-start.56 = (bf16[512,512]{1,0:T(8,128)(2,1)}, bf16[512,512]{1,0:T(8,128)(2,1)}, u32[]{:S(2)}, u32[]{:S(2)}) collective-permute-start(bf16[512,512]{1,0:T(8,128)(2,1)} %collective-permute-done.34.refs_0_.refs_1_), channel_id=1, source_target_pairs={{0,8},{4,12},{8,0},{12,4},{1,9},{5,13},{9,1},{13,5},{2,10},{6,14},... | collective-permute-start | bytes 1572872 | tf_op jit(solution)/shard_map/ppermute | solution.py:35
  221.0 20.9 %collective-permute-start.55 = (bf16[512,512]{1,0:T(8,128)(2,1)}, bf16[512,512]{1,0:T(8,128)(2,1)}, u32[]{:S(2)}, u32[]{:S(2)}) collective-permute-start(bf16[512,512]{1,0:T(8,128)(2,1)} %collective-permute-done.48.refs_3_), channel_id=1, source_target_pairs={{0,1},{1,2},{2,3},{3,0},{4,5},{5,6},{6,7},{7,4},{8,9},{9,10},{10,1... | collective-permute-start | bytes 1572872 | tf_op jit(solution)/shard_map/ppermute | solution.py:30
  236.6 19.1 %collective-permute-start.61 = (bf16[512,512]{1,0:T(8,128)(2,1)}, bf16[512,512]{1,0:T(8,128)(2,1)}, u32[]{:S(2)}, u32[]{:S(2)}) collective-permute-start(bf16[512,512]{1,0:T(8,128)(2,1)} %collective-permute-done.37.refs_1_.refs_2_), channel_id=1, source_target_pairs={{0,8},{4,12},{8,0},{12,4},{1,9},{5,13},{9,1},{13,5},{2,10},{6,14},... | collective-permute-start | bytes 1572872 | tf_op jit(solution)/shard_map/ppermute | solution.py:35
  237.7 18.0 %collective-permute-start.62 = (bf16[512,512]{1,0:T(8,128)(2,1)}, bf16[512,512]{1,0:T(8,128)(2,1)}, u32[]{:S(2)}, u32[]{:S(2)}) collective-permute-start(bf16[512,512]{1,0:T(8,128)(2,1)} %collective-permute-done.51.refs_4_), channel_id=1, source_target_pairs={{0,1},{1,2},{2,3},{3,0},{4,5},{5,6},{6,7},{7,4},{8,9},{9,10},{10,1... | collective-permute-start | bytes 1572872 | tf_op jit(solution)/shard_map/ppermute | solution.py:30
  241.9 22.4 %collective-permute-start.57 = (bf16[512,512]{1,0:T(8,128)(2,1)}, bf16[512,512]{1,0:T(8,128)(2,1)}, u32[]{:S(2)}, u32[]{:S(2)}) collective-permute-start(bf16[512,512]{1,0:T(8,128)(2,1)} %collective-permute-done.40.refs_2_.refs_3_), channel_id=1, source_target_pairs={{0,8},{4,12},{8,0},{12,4},{1,9},{5,13},{9,1},{13,5},{2,10},{6,14},... | collective-permute-start | bytes 1572872 | tf_op jit(solution)/shard_map/ppermute | solution.py:35
  243.5 20.9 %collective-permute-start.58 = (bf16[512,512]{1,0:T(8,128)(2,1)}, bf16[512,512]{1,0:T(8,128)(2,1)}, u32[]{:S(2)}, u32[]{:S(2)}) collective-permute-start(bf16[512,512]{1,0:T(8,128)(2,1)} %collective-permute-done.50.refs_4_), channel_id=1, source_target_pairs={{0,1},{1,2},{2,3},{3,0},{4,5},{5,6},{6,7},{7,4},{8,9},{9,10},{10,1... | collective-permute-start | bytes 1572872 | tf_op jit(solution)/shard_map/ppermute | solution.py:30
  (28 other events, 245.6 us)

commit v3 on v2

--- a/solution.py
+++ b/solution.py
@@ -354,8 +354,7 @@
         before = ended.get(step - 2, [])
         if step < CHUNKS:
             first = step * size
-            some = tie(start, *[prev for _, prev in kv]) if step == 1 else start
-            own[step, 0] = attend(queries, *kv[first // per_kv], some, first, size)
+            own[step, 0] = attend(queries, *kv[first // per_kv], start, first, size)
         arrived = []
         if step < len(over_z):
             kind, c, r = over_z[step]

time: 284 us -> 284 us (level)
  transfers between devices with their start and end apart: 65 -> 65, of which waited for: 16 -> 15; matrix products, arithmetic and copies ran while one was open for 13% -> 12% of each run, Pallas kernels for 42% -> 42%
where the time goes in v3:
time: 284 us; the launch traced here: 282 us
  Pallas kernels  126 us (44%)
  starting transfers between devices  75.2 us (26%)
  waiting for transfers between devices  39.8 us (14%)
  other arithmetic  36.5 us (13%)
  local copies, waits for them, and re-layouts  3.54 us (1%)
    pallas_call x13, Pallas kernels, gram(): pl.pallas_call(functools.partial(gram_kernel, runs, places, counts, start...  87.8 us
    ppermute x42, starting transfers between devices, over_tensor(): return lax.ppermute(value, 'tensor', [(t, t ^ bit) for t in range(count)])  54.6 us
    select_n x21, other arithmetic, per_device(): sent = jnp.where(even, *[jnp.concatenate(x, 1) for x in pair])  35.7 us
    ppermute x21, waiting for transfers between devices, from_behind(): return lax.ppermute(value, axis, pairs)  31.6 us
    pallas_call x6, Pallas kernels, attend(): pl.pallas_call(attend_kernel, grid=(heads // step,), out_shape=jax.ShapeD...  29.3 us
    ppermute x21, starting transfers between devices, from_behind(): return lax.ppermute(value, axis, pairs)  12.7 us
    pallas_call x4, Pallas kernels, rows_of(): pl.pallas_call(functools.partial(rows_kernel, widths, rows), out_shape=ja...  9.21 us
    ppermute x42, waiting for transfers between devices, over_tensor(): return lax.ppermute(value, 'tensor', [(t, t ^ bit) for t in range(count)])  8.23 us
  transfers between devices with their start and end apart: 65, of which 15 were waited for; matrix products, arithmetic and copies ran while one was open for 12% of the time, Pallas kernels for 42%

profile of v3, /device:TPU:1, one launch (start us, length us, event | category | flops | bytes accessed | tf_op | source)
XLA Modules:
  0.0 282.0 jit_solution(15587825238052571425)
XLA Ops:
  1.2 4.0 %collective-permute-start = (bf16[512,256]{1,0:T(8,128)(2,1)S(1)}, bf16[512,256]{1,0:T(8,128)(2,1)S(1)}, u32[]{:S(2)}, u32[]{:S(2)}) collective-permute-start(bf16[512,256]{1,0:T(8,128)(2,1)S(1)} %pad_maximum_fusion.ko_ref.vo_ref), channel_id=1, source_target_pairs={{0,1},{1,2},{2,3},{4,5},{5,6},{6,7},{8,9},{9,10},{10,11},{12,13},{... | collective-permute-start | bytes 786440 | tf_op jit(solution)/shard_map/ppermute | solution.py:24
  6.0 3.9 %collective-permute-start.2 = (bf16[512,256]{1,0:T(8,128)(2,1)}, bf16[512,256]{1,0:T(8,128)(2,1)}, u32[]{:S(2)}, u32[]{:S(2)}) collective-permute-start(bf16[512,256]{1,0:T(8,128)(2,1)} %pad_maximum_fusion.1.ko_ref.vo_ref), channel_id=1, source_target_pairs={{0,1},{1,2},{2,3},{4,5},{5,6},{6,7},{8,9},{9,10},{10,11},{12,13},{... | collective-permute-start | bytes 786440 | tf_op jit(solution)/shard_map/ppermute | solution.py:24
  11.5 4.5 %shard_map.46.refs_0_.refs_2_ = bf16[512,512]{1,0:T(8,128)(2,1)} custom-call(s32[512,1]{1,0:T(8,128)} %copy.16.start_ref, bf16[512,3072]{1,0:T(8,128)(2,1)} %q_ref.11, bf16[512,256]{1,0:T(8,128)(2,1)} %copy-done.9, bf16[512,256]{1,0:T(8,128)(2,1)} %copy-done.7, bf16[512,256]{1,0:T(8,128)(2,1)} %copy-done.9, bf16[512,256]{1,0:T(8,128)(2,1)} %copy-done.7), custom_call_target="tpu_custom_call" | custom-call | flops 999999986991104 | bytes 1 | tf_op jit(solution)/shard_map/pallas_call | solution.py:87
  18.8 5.0 %shard_map.49.refs_1_.refs_4_ = bf16[512,512]{1,0:T(8,128)(2,1)} custom-call(s32[512,1]{1,0:T(8,128)} %copy.16.start_ref, bf16[512,3072]{1,0:T(8,128)(2,1)} %q_ref.11, bf16[512,256]{1,0:T(8,128)(2,1)} %copy-done.9, bf16[512,256]{1,0:T(8,128)(2,1)} %copy-done.7, bf16[512,256]{1,0:T(8,128)(2,1)} %copy-done.9, bf16[512,256]{1,0:T(8,128)(2,1)} %copy-done.7), custom_call_target="tpu_custom_call" | custom-call | flops 999999986991104 | bytes 1 | tf_op jit(solution)/shard_map/pallas_call | solution.py:87
  25.3 4.1 %collective-permute-done.1.refs_0_.refs_3_ = bf16[512,512]{1,0:T(8,128)(2,1)} collective-permute-done((bf16[512,512]{1,0:T(8,128)(2,1)}, bf16[512,512]{1,0:T(8,128)(2,1)}, u32[]{:S(2)}, u32[]{:S(2)}) %collective-permute-start.1) | collective-permute-done | bytes 524320 | tf_op jit(solution)/shard_map/ppermute | solution.py:30
  30.3 7.3 %collective-permute-start.22 = (bf16[512,512]{1,0:T(8,128)(2,1)}, bf16[512,512]{1,0:T(8,128)(2,1)}, u32[]{:S(2)}, u32[]{:S(2)}) collective-permute-start(bf16[512,512]{1,0:T(8,128)(2,1)} %broadcast_select_fusion.17), channel_id=1, source_target_pairs={{0,4},{4,0},{8,12},{12,8},{1,5},{5,1},{9,13},{13,9},{2,6},{6,2},{1... | collective-permute-start | bytes 1572872 | tf_op jit(solution)/shard_map/ppermute | solution.py:35
  37.6 5.0 %shard_map.48.refs_2_.refs_6_ = bf16[512,512]{1,0:T(8,128)(2,1)} custom-call(s32[512,1]{1,0:T(8,128)} %copy.16.start_ref, bf16[512,3072]{1,0:T(8,128)(2,1)} %q_ref.11, bf16[512,256]{1,0:T(8,128)(2,1)} %copy-done.9, bf16[512,256]{1,0:T(8,128)(2,1)} %copy-done.7, bf16[512,256]{1,0:T(8,128)(2,1)} %copy-done.9, bf16[512,256]{1,0:T(8,128)(2,1)} %copy-done.7), custom_call_target="tpu_custom_call" | custom-call | flops 999999986991104 | bytes 1 | tf_op jit(solution)/shard_map/pallas_call | solution.py:87
  47.6 5.0 %shard_map.51.refs_3_.refs_2_ = bf16[512,512]{1,0:T(8,128)(2,1)} custom-call(s32[512,1]{1,0:T(8,128)} %copy.16.start_ref, bf16[512,3072]{1,0:T(8,128)(2,1)} %q_ref.11, bf16[512,256]{1,0:T(8,128)(2,1)} %collective-permute-done.2.kp_ref.vp_ref, bf16[512,256]{1,0:T(8,128)(2,1)} %pad_maximum_fusion.1.ko_ref.vo_ref, ...), custom_call_target="tpu_custom_call" | custom-call | flops 999999986991104 | bytes 1 | tf_op jit(solution)/shard_map/pallas_call | solution.py:87
  54.2 4.1 %collective-permute-done.4.refs_2_.refs_7_ = bf16[512,512]{1,0:T(8,128)(2,1)} collective-permute-done((bf16[512,512]{1,0:T(8,128)(2,1)}, bf16[512,512]{1,0:T(8,128)(2,1)}, u32[]{:S(2)}, u32[]{:S(2)}) %collective-permute-start.4) | collective-permute-done | bytes 524320 | tf_op jit(solution)/shard_map/ppermute | solution.py:30
  59.1 2.2 collective-permute-start.24
  61.4 4.9 %shard_map.47.refs_4_ = bf16[512,512]{1,0:T(8,128)(2,1)} custom-call(s32[512,1]{1,0:T(8,128)} %copy.16.start_ref, bf16[512,3072]{1,0:T(8,128)(2,1)} %q_ref.11, bf16[512,256]{1,0:T(8,128)(2,1)} %collective-permute-done.2.kp_ref.vp_ref, bf16[512,256]{1,0:T(8,128)(2,1)} %pad_maximum_fusion.1.ko_ref.vo_ref, ...), custom_call_target="tpu_custom_call" | custom-call | flops 999999986991104 | bytes 1 | tf_op jit(solution)/shard_map/pallas_call | solution.py:87
  72.2 5.0 %shard_map.50.refs_5_.refs_6_ = bf16[512,512]{1,0:T(8,128)(2,1)} custom-call(s32[512,1]{1,0:T(8,128)} %copy.16.start_ref, bf16[512,3072]{1,0:T(8,128)(2,1)} %q_ref.11, bf16[512,256]{1,0:T(8,128)(2,1)} %collective-permute-done.2.kp_ref.vp_ref, bf16[512,256]{1,0:T(8,128)(2,1)} %pad_maximum_fusion.1.ko_ref.vo_ref, ...), custom_call_target="tpu_custom_call" | custom-call | flops 999999986991104 | bytes 1 | tf_op jit(solution)/shard_map/pallas_call | solution.py:87
  79.2 2.8 collective-permute-done.6.refs_4_.refs_5_
  82.1 2.2 collective-permute-start.26
  85.9 7.4 %collective-permute-done.13.refs_5_.refs_7_ = bf16[512,512]{1,0:T(8,128)(2,1)} collective-permute-done((bf16[512,512]{1,0:T(8,128)(2,1)}, bf16[512,512]{1,0:T(8,128)(2,1)}, u32[]{:S(2)}, u32[]{:S(2)}) %collective-permute-start.13) | collective-permute-done | bytes 524320 | tf_op jit(solution)/shard_map/ppermute | solution.py:30
  96.0 2.3 shard_map.52.refs_0_
  99.8 3.7 %collective-permute-done.16.refs_3_ = bf16[512,512]{1,0:T(8,128)(2,1)} collective-permute-done((bf16[512,512]{1,0:T(8,128)(2,1)}, bf16[512,512]{1,0:T(8,128)(2,1)}, u32[]{:S(2)}, u32[]{:S(2)}) %collective-permute-start.16) | collective-permute-done | bytes 524320 | tf_op jit(solution)/shard_map/ppermute | solution.py:35
  104.5 1.9 broadcast_select_fusion.11
  107.5 2.3 shard_map.53.refs_1_
  111.5 4.3 %collective-permute-done.15.refs_1_.refs_2_ = bf16[512,512]{1,0:T(8,128)(2,1)} collective-permute-done((bf16[512,512]{1,0:T(8,128)(2,1)}, bf16[512,512]{1,0:T(8,128)(2,1)}, u32[]{:S(2)}, u32[]{:S(2)}) %collective-permute-start.15) | collective-permute-done | bytes 524320 | tf_op jit(solution)/shard_map/ppermute | solution.py:30
  115.8 1.9 broadcast_select_fusion.10
  118.7 6.7 %shard_map.54.refs_10_ = bf16[768,9216]{1,0:T(8,128)(2,1)} custom-call(bf16[768,512]{1,0:T(8,128)(2,1)} %shard_map.52.refs_0_, bf16[768,512]{1,0:T(8,128)(2,1)} %shard_map.53.refs_1_, bf16[512,512]{1,0:T(8,128)(2,1)} %shard_map.46.refs_0_.refs_2_, bf16[512,512]{1,0:T(8,128)(2,1)} %collective-permute-done.1.refs_0_.refs_3_, ...), custom_call_target="tpu_custom_call" | custom-call | flops 999999986991104 | bytes 1 | tf_op jit(solution)/shard_map/pallas_call | solution.py:252
  128.3 1.9 broadcast_select_fusion.9
  131.4 8.0 %shard_map.55.refs_8_ = bf16[768,9216]{1,0:T(8,128)(2,1)} custom-call(bf16[768,512]{1,0:T(8,128)(2,1)} %shard_map.52.refs_0_, bf16[768,512]{1,0:T(8,128)(2,1)} %shard_map.53.refs_1_, bf16[512,512]{1,0:T(8,128)(2,1)} %collective-permute-done.3.refs_2_, bf16[512,512]{1,0:T(8,128)(2,1)} %collective-permute-done.16.refs_3_, ...), custom_call_target="tpu_custom_call", output_to_operand_aliasing={{}: (10, {})} | custom-call | flops 999999986991104 | bytes 1 | tf_op jit(solution)/shard_map/pallas_call | solution.py:252
  142.3 1.9 broadcast_select_fusion.8
  145.7 6.6 %shard_map.57.refs_10_ = bf16[768,9216]{1,0:T(8,128)(2,1)} custom-call(bf16[768,512]{1,0:T(8,128)(2,1)} %shard_map.52.refs_0_, bf16[768,512]{1,0:T(8,128)(2,1)} %shard_map.53.refs_1_, bf16[512,512]{1,0:T(8,128)(2,1)} %shard_map.51.refs_3_.refs_2_, bf16[512,512]{1,0:T(8,128)(2,1)} %collective-permute-done.11.refs_3_, ...), custom_call_target="tpu_custom_call", output_to_operand_aliasing={{}: (8, {})} | custom-call | flops 999999986991104 | bytes 1 | tf_op jit(solution)/shard_map/pallas_call | solution.py:252
  153.6 1.9 broadcast_select_fusion.7
  156.9 8.0 %shard_map.58.refs_10_ = bf16[768,9216]{1,0:T(8,128)(2,1)} custom-call(bf16[768,512]{1,0:T(8,128)(2,1)} %shard_map.52.refs_0_, bf16[768,512]{1,0:T(8,128)(2,1)} %shard_map.53.refs_1_, bf16[512,512]{1,0:T(8,128)(2,1)} %collective-permute-done.5.refs_2_, bf16[512,512]{1,0:T(8,128)(2,1)} %collective-permute-done.20.refs_3_, ...), custom_call_target="tpu_custom_call", output_to_operand_aliasing={{}: (10, {})} | custom-call | flops 999999986991104 | bytes 1 | tf_op jit(solution)/shard_map/pallas_call | solution.py:252
  165.0 1.9 broadcast_select_fusion.6
  166.9 2.3 shard_map.56.refs_0_
  176.0 1.9 broadcast_select_fusion.5
  179.4 8.0 %shard_map.59.refs_4_ = bf16[768,9216]{1,0:T(8,128)(2,1)} custom-call(bf16[768,512]{1,0:T(8,128)(2,1)} %shard_map.52.refs_0_, bf16[768,512]{1,0:T(8,128)(2,1)} %shard_map.53.refs_1_, bf16[512,512]{1,0:T(8,128)(2,1)} %collective-permute-done.7.refs_2_, bf16[512,512]{1,0:T(8,128)(2,1)} %collective-permute-done.33.refs_3_, ...), custom_call_target="tpu_custom_call", output_to_operand_aliasing={{}: (10, {})} | custom-call | flops 999999986991104 | bytes 1 | tf_op jit(solution)/shard_map/pallas_call | solution.py:252
  188.4 1.9 broadcast_select_fusion.4
  190.8 5.4 %shard_map.60.refs_5_ = bf16[768,9216]{1,0:T(8,128)(2,1)} custom-call(bf16[768,512]{1,0:T(8,128)(2,1)} %shard_map.56.refs_0_, bf16[512,512]{1,0:T(8,128)(2,1)} %collective-permute-done.8.refs_0_.refs_1_, bf16[512,512]{1,0:T(8,128)(2,1)} %collective-permute-done.15.refs_1_.refs_2_, ...), custom_call_target="tpu_custom_call", output_to_operand_aliasing={{}: (4, {})} | custom-call | flops 999999986991104 | bytes 1 | tf_op jit(solution)/shard_map/pallas_call | solution.py:252
  201.9 6.3 %shard_map.61.refs_4_ = bf16[768,9216]{1,0:T(8,128)(2,1)} custom-call(bf16[768,512]{1,0:T(8,128)(2,1)} %shard_map.56.refs_0_, bf16[512,512]{1,0:T(8,128)(2,1)} %collective-permute-done.39.refs_1_, bf16[512,512]{1,0:T(8,128)(2,1)} %collective-permute-done.44.refs_2_, ...), custom_call_target="tpu_custom_call", output_to_operand_aliasing={{}: (5, {})} | custom-call | flops 999999986991104 | bytes 1 | tf_op jit(solution)/shard_map/pallas_call | solution.py:252
  213.2 5.3 %shard_map.63.refs_5_ = bf16[768,9216]{1,0:T(8,128)(2,1)} custom-call(bf16[768,512]{1,0:T(8,128)(2,1)} %shard_map.56.refs_0_, bf16[512,512]{1,0:T(8,128)(2,1)} %collective-permute-done.19.refs_3_.refs_1_, bf16[512,512]{1,0:T(8,128)(2,1)} %collective-permute-done.21.refs_4_.refs_2_, ...), custom_call_target="tpu_custom_call", output_to_operand_aliasing={{}: (4, {})} | custom-call | flops 999999986991104 | bytes 1 | tf_op jit(solution)/shard_map/pallas_call | solution.py:252
  220.9 1.9 broadcast_select_fusion.1
  224.4 6.3 %shard_map.64.refs_7_.refs_5_.refs_8_ = bf16[768,9216]{1,0:T(8,128)(2,1)} custom-call(bf16[768,512]{1,0:T(8,128)(2,1)} %shard_map.56.refs_0_, bf16[512,512]{1,0:T(8,128)(2,1)} %collective-permute-done.45.refs_1_, bf16[512,512]{1,0:T(8,128)(2,1)} %collective-permute-done.52.refs_2_, ...), custom_call_target="tpu_custom_call", output_to_operand_aliasing={{}: (5, {})} | custom-call | flops 999999986991104 | bytes 1 | tf_op jit(solution)/shard_map/pallas_call | solution.py:252
  230.8 1.9 broadcast_select_fusion
  234.2 2.3 shard_map.62.refs_0_.refs_1_
  237.7 2.7 collective-permute-done.56.refs_1_
  243.4 2.9 %maximum_select_fusion = bf16[512,1024]{1,0:T(8,128)(2,1)} fusion(bf16[512,512]{1,0:T(8,128)(2,1)} %collective-permute-done.55.refs_3_, bf16[512,512]{1,0:T(8,128)(2,1)} %collective-permute-done.56.refs_1_, bf16[512,512]{1,0:T(8,128)(2,1)} %collective-permute-done.43.refs_3_.refs_4_, bf16[512,512]{1,0:T(8,128)(2,1)} %collective-permute-done.34.refs_0_.refs_1_, ...), kind=kLoop, calls=%fused_computation | loop fusion | flops 4718592 | bytes 3145729 | tf_op jit(solution)/shard_map/jit(_where)/select_n | solution.py:378
  247.8 8.0 %shard_map.65.refs_6_ = f32[768,9216]{1,0:T(8,128)} custom-call(bf16[768,512]{1,0:T(8,128)(2,1)} %shard_map.62.refs_0_.refs_1_, bf16[512,512]{1,0:T(8,128)(2,1)} %collective-permute-done.34.refs_0_.refs_1_, bf16[512,512]{1,0:T(8,128)(2,1)} %collective-permute-done.37.refs_1_.refs_2_, bf16[512,512]{1,0:T(8,128)(2,1)} %collective-permute-done.40.refs_2_.refs_3_, ...), custom_call_target="tpu_custom_call" | custom-call | flops 999999986991104 | bytes 1 | tf_op jit(solution)/shard_map/pallas_call | solution.py:252
  255.8 2.9 %maximum_select_fusion.1 = bf16[512,1024]{1,0:T(8,128)(2,1)} fusion(bf16[512,512]{1,0:T(8,128)(2,1)} %collective-permute-done.62.refs_5_, bf16[512,512]{1,0:T(8,128)(2,1)} %collective-permute-done.61.refs_2_, bf16[512,512]{1,0:T(8,128)(2,1)} %collective-permute-done.46.refs_4_.refs_5_, bf16[512,512]{1,0:T(8,128)(2,1)} %collective-permute-done.37.refs_1_.refs_2_, ...), kind=kLoop, calls=%fused_computation.1 | loop fusion | flops 4718592 | bytes 3145729 | tf_op jit(solution)/shard_map/jit(_where)/select_n | solution.py:378
  258.7 5.7 %shard_map.66.refs_9_ = f32[768,9216]{1,0:T(8,128)} custom-call(bf16[768,512]{1,0:T(8,128)(2,1)} %shard_map.62.refs_0_.refs_1_, bf16[512,512]{1,0:T(8,128)(2,1)} %collective-permute-done.56.refs_1_, bf16[512,1024]{1,0:T(8,128)(2,1)} %collective-permute-done.60.refs_2_.refs_4_, ...), custom_call_target="tpu_custom_call", output_to_operand_aliasing={{}: (6, {})} | custom-call | flops 999999986991104 | bytes 1 | tf_op jit(solution)/shard_map/pallas_call | solution.py:252
  264.4 2.9 %maximum_select_fusion.2 = bf16[512,1024]{1,0:T(8,128)(2,1)} fusion(bf16[512,512]{1,0:T(8,128)(2,1)} %collective-permute-done.58.refs_5_, bf16[512,512]{1,0:T(8,128)(2,1)} %collective-permute-done.57.refs_2_, bf16[512,512]{1,0:T(8,128)(2,1)} %collective-permute-done.49.refs_5_.refs_6_, bf16[512,512]{1,0:T(8,128)(2,1)} %collective-permute-done.40.refs_2_.refs_3_, ...), kind=kLoop, calls=%fused_computation.2 | loop fusion | flops 4718592 | bytes 3145729 | tf_op jit(solution)/shard_map/jit(_where)/select_n | solution.py:378
  268.3 6.8 %shard_map.67.refs_9_ = f32[768,9216]{1,0:T(8,128)} custom-call(bf16[768,512]{1,0:T(8,128)(2,1)} %shard_map.56.refs_0_, bf16[768,512]{1,0:T(8,128)(2,1)} %shard_map.62.refs_0_.refs_1_, bf16[512,512]{1,0:T(8,128)(2,1)} %collective-permute-done.61.refs_2_, bf16[512,1024]{1,0:T(8,128)(2,1)} %collective-permute-done.63.refs_3_.refs_7_, ...), custom_call_target="tpu_custom_call", output_to_operand_aliasing={{}: (9, {})} | custom-call | flops 999999986991104 | bytes 1 | tf_op jit(solution)/shard_map/pallas_call | solution.py:252
  275.1 6.8 %shard_map.68 = f32[768,9216]{1,0:T(8,128)} custom-call(bf16[768,512]{1,0:T(8,128)(2,1)} %shard_map.56.refs_0_, bf16[768,512]{1,0:T(8,128)(2,1)} %shard_map.62.refs_0_.refs_1_, bf16[512,512]{1,0:T(8,128)(2,1)} %collective-permute-done.57.refs_2_, bf16[512,1024]{1,0:T(8,128)(2,1)} %collective-permute-done.64.refs_3_.refs_7_, ...), custom_call_target="tpu_custom_call", output_to_operand_aliasing={{}: (9, {})} | custom-call | flops 999999986991104 | bytes 1 | tf_op jit(solution)/shard_map/pallas_call | solution.py:252
  (151 shorter events, 78.7 us)
Async XLA Ops:
  6.0 41.6 %collective-permute-start.2 = (bf16[512,256]{1,0:T(8,128)(2,1)}, bf16[512,256]{1,0:T(8,128)(2,1)}, u32[]{:S(2)}, u32[]{:S(2)}) collective-permute-start(bf16[512,256]{1,0:T(8,128)(2,1)} %pad_maximum_fusion.1.ko_ref.vo_ref), channel_id=1, source_target_pairs={{0,1},{1,2},{2,3},{4,5},{5,6},{6,7},{8,9},{9,10},{10,11},{12,13},{... | collective-permute-start | bytes 786440 | tf_op jit(solution)/shard_map/ppermute | solution.py:24
  15.9 13.5 %collective-permute-start.1 = (bf16[512,512]{1,0:T(8,128)(2,1)}, bf16[512,512]{1,0:T(8,128)(2,1)}, u32[]{:S(2)}, u32[]{:S(2)}) collective-permute-start(bf16[512,512]{1,0:T(8,128)(2,1)} %shard_map.46.refs_0_.refs_2_), channel_id=1, source_target_pairs={{0,1},{1,2},{2,3},{3,0},{4,5},{5,6},{6,7},{7,4},{8,9},{9,10},{10,1... | collective-permute-start | bytes 1572872 | tf_op jit(solution)/shard_map/ppermute | solution.py:30
  17.6 11.9 %collective-permute-start.3 = (bf16[512,512]{1,0:T(8,128)(2,1)}, bf16[512,512]{1,0:T(8,128)(2,1)}, u32[]{:S(2)}, u32[]{:S(2)}) collective-permute-start(bf16[512,512]{1,0:T(8,128)(2,1)} %shard_map.46.refs_0_.refs_2_), channel_id=1, source_target_pairs={{0,8},{4,12},{8,0},{12,4},{1,9},{5,13},{9,1},{13,5},{2,10},{6,14},... | collective-permute-start | bytes 1572872 | tf_op jit(solution)/shard_map/ppermute | solution.py:35
  23.8 20.1 %collective-permute-start.10 = (bf16[512,512]{1,0:T(8,128)(2,1)}, bf16[512,512]{1,0:T(8,128)(2,1)}, u32[]{:S(2)}, u32[]{:S(2)}) collective-permute-start(bf16[512,512]{1,0:T(8,128)(2,1)} %shard_map.49.refs_1_.refs_4_), channel_id=1, source_target_pairs={{0,8},{4,12},{8,0},{12,4},{1,9},{5,13},{9,1},{13,5},{2,10},{6,14},... | collective-permute-start | bytes 1572872 | tf_op jit(solution)/shard_map/ppermute | solution.py:35
  24.0 21.1 %collective-permute-start.9 = (bf16[512,512]{1,0:T(8,128)(2,1)}, bf16[512,512]{1,0:T(8,128)(2,1)}, u32[]{:S(2)}, u32[]{:S(2)}) collective-permute-start(bf16[512,512]{1,0:T(8,128)(2,1)} %shard_map.49.refs_1_.refs_4_), channel_id=1, source_target_pairs={{0,1},{1,2},{2,3},{3,0},{4,5},{5,6},{6,7},{7,4},{8,9},{9,10},{10,1... | collective-permute-start | bytes 1572872 | tf_op jit(solution)/shard_map/ppermute | solution.py:30
  30.3 14.8 %collective-permute-start.22 = (bf16[512,512]{1,0:T(8,128)(2,1)}, bf16[512,512]{1,0:T(8,128)(2,1)}, u32[]{:S(2)}, u32[]{:S(2)}) collective-permute-start(bf16[512,512]{1,0:T(8,128)(2,1)} %broadcast_select_fusion.17), channel_id=1, source_target_pairs={{0,4},{4,0},{8,12},{12,8},{1,5},{5,1},{9,13},{13,9},{2,6},{6,2},{1... | collective-permute-start | bytes 1572872 | tf_op jit(solution)/shard_map/ppermute | solution.py:35
  42.6 15.7 %collective-permute-start.4 = (bf16[512,512]{1,0:T(8,128)(2,1)}, bf16[512,512]{1,0:T(8,128)(2,1)}, u32[]{:S(2)}, u32[]{:S(2)}) collective-permute-start(bf16[512,512]{1,0:T(8,128)(2,1)} %shard_map.48.refs_2_.refs_6_), channel_id=1, source_target_pairs={{0,1},{1,2},{2,3},{3,0},{4,5},{5,6},{6,7},{7,4},{8,9},{9,10},{10,1... | collective-permute-start | bytes 1572872 | tf_op jit(solution)/shard_map/ppermute | solution.py:30
  43.9 14.4 %collective-permute-start.5 = (bf16[512,512]{1,0:T(8,128)(2,1)}, bf16[512,512]{1,0:T(8,128)(2,1)}, u32[]{:S(2)}, u32[]{:S(2)}) collective-permute-start(bf16[512,512]{1,0:T(8,128)(2,1)} %shard_map.48.refs_2_.refs_6_), channel_id=1, source_target_pairs={{0,8},{4,12},{8,0},{12,4},{1,9},{5,13},{9,1},{13,5},{2,10},{6,14},... | collective-permute-start | bytes 1572872 | tf_op jit(solution)/shard_map/ppermute | solution.py:35
  46.0 12.3 %collective-permute-start.23 = (bf16[512,512]{1,0:T(8,128)(2,1)}, bf16[512,512]{1,0:T(8,128)(2,1)}, u32[]{:S(2)}, u32[]{:S(2)}) collective-permute-start(bf16[512,512]{1,0:T(8,128)(2,1)} %broadcast_select_fusion.16), channel_id=1, source_target_pairs={{0,4},{4,0},{8,12},{12,8},{1,5},{5,1},{9,13},{13,9},{2,6},{6,2},{1... | collective-permute-start | bytes 1572872 | tf_op jit(solution)/shard_map/ppermute | solution.py:35
  52.6 16.9 %collective-permute-start.11 = (bf16[512,512]{1,0:T(8,128)(2,1)}, bf16[512,512]{1,0:T(8,128)(2,1)}, u32[]{:S(2)}, u32[]{:S(2)}) collective-permute-start(bf16[512,512]{1,0:T(8,128)(2,1)} %shard_map.51.refs_3_.refs_2_), channel_id=1, source_target_pairs={{0,1},{1,2},{2,3},{3,0},{4,5},{5,6},{6,7},{7,4},{8,9},{9,10},{10,1... | collective-permute-start | bytes 1572872 | tf_op jit(solution)/shard_map/ppermute | solution.py:30
  53.9 15.6 %collective-permute-start.12 = (bf16[512,512]{1,0:T(8,128)(2,1)}, bf16[512,512]{1,0:T(8,128)(2,1)}, u32[]{:S(2)}, u32[]{:S(2)}) collective-permute-start(bf16[512,512]{1,0:T(8,128)(2,1)} %shard_map.51.refs_3_.refs_2_), channel_id=1, source_target_pairs={{0,8},{4,12},{8,0},{12,4},{1,9},{5,13},{9,1},{13,5},{2,10},{6,14},... | collective-permute-start | bytes 1572872 | tf_op jit(solution)/shard_map/ppermute | solution.py:35
  66.3 15.7 %collective-permute-start.6 = (bf16[512,512]{1,0:T(8,128)(2,1)}, bf16[512,512]{1,0:T(8,128)(2,1)}, u32[]{:S(2)}, u32[]{:S(2)}) collective-permute-start(bf16[512,512]{1,0:T(8,128)(2,1)} %shard_map.47.refs_4_), channel_id=1, source_target_pairs={{0,1},{1,2},{2,3},{3,0},{4,5},{5,6},{6,7},{7,4},{8,9},{9,10},{10,1... | collective-permute-start | bytes 1572872 | tf_op jit(solution)/shard_map/ppermute | solution.py:30
  67.4 14.6 %collective-permute-start.7 = (bf16[512,512]{1,0:T(8,128)(2,1)}, bf16[512,512]{1,0:T(8,128)(2,1)}, u32[]{:S(2)}, u32[]{:S(2)}) collective-permute-start(bf16[512,512]{1,0:T(8,128)(2,1)} %shard_map.47.refs_4_), channel_id=1, source_target_pairs={{0,8},{4,12},{8,0},{12,4},{1,9},{5,13},{9,1},{13,5},{2,10},{6,14},... | collective-permute-start | bytes 1572872 | tf_op jit(solution)/shard_map/ppermute | solution.py:35
  70.4 11.6 %collective-permute-start.25 = (bf16[512,512]{1,0:T(8,128)(2,1)}, bf16[512,512]{1,0:T(8,128)(2,1)}, u32[]{:S(2)}, u32[]{:S(2)}) collective-permute-start(bf16[512,512]{1,0:T(8,128)(2,1)} %broadcast_select_fusion.14), channel_id=1, source_target_pairs={{0,4},{4,0},{8,12},{12,8},{1,5},{5,1},{9,13},{13,9},{2,6},{6,2},{1... | collective-permute-start | bytes 1572872 | tf_op jit(solution)/shard_map/ppermute | solution.py:35
  77.2 16.1 %collective-permute-start.13 = (bf16[512,512]{1,0:T(8,128)(2,1)}, bf16[512,512]{1,0:T(8,128)(2,1)}, u32[]{:S(2)}, u32[]{:S(2)}) collective-permute-start(bf16[512,512]{1,0:T(8,128)(2,1)} %shard_map.50.refs_5_.refs_6_), channel_id=1, source_target_pairs={{0,1},{1,2},{2,3},{3,0},{4,5},{5,6},{6,7},{7,4},{8,9},{9,10},{10,1... | collective-permute-start | bytes 1572872 | tf_op jit(solution)/shard_map/ppermute | solution.py:30
  78.0 15.3 %collective-permute-start.14 = (bf16[512,512]{1,0:T(8,128)(2,1)}, bf16[512,512]{1,0:T(8,128)(2,1)S(1)}, u32[]{:S(2)}, u32[]{:S(2)}) collective-permute-start(bf16[512,512]{1,0:T(8,128)(2,1)} %shard_map.50.refs_5_.refs_6_), channel_id=1, source_target_pairs={{0,8},{4,12},{8,0},{12,4},{1,9},{5,13},{9,1},{13,5},{2,10},{6,14},... | collective-permute-start | bytes 1572872 | tf_op jit(solution)/shard_map/ppermute | solution.py:35
  82.1 11.3 %collective-permute-start.26 = (bf16[512,512]{1,0:T(8,128)(2,1)S(1)}, bf16[512,512]{1,0:T(8,128)(2,1)}, u32[]{:S(2)}, u32[]{:S(2)}) collective-permute-start(bf16[512,512]{1,0:T(8,128)(2,1)S(1)} %broadcast_select_fusion.13), channel_id=1, source_target_pairs={{0,4},{4,0},{8,12},{12,8},{1,5},{5,1},{9,13},{13,9},{2,6},{6,2},{1... | collective-permute-start | bytes 1572872 | tf_op jit(solution)/shard_map/ppermute | solution.py:35
  84.3 19.3 %collective-permute-start.16 = (bf16[512,512]{1,0:T(8,128)(2,1)}, bf16[512,512]{1,0:T(8,128)(2,1)}, u32[]{:S(2)}, u32[]{:S(2)}) collective-permute-start(bf16[512,512]{1,0:T(8,128)(2,1)} %collective-permute-done.1.refs_0_.refs_3_), channel_id=1, source_target_pairs={{0,8},{4,12},{8,0},{12,4},{1,9},{5,13},{9,1},{13,5},{2,10},{6,14},... | collective-permute-start | bytes 1572872 | tf_op jit(solution)/shard_map/ppermute | solution.py:35
  85.5 19.0 %collective-permute-start.8 = (bf16[512,512]{1,0:T(8,128)(2,1)}, bf16[512,512]{1,0:T(8,128)(2,1)}, u32[]{:S(2)}, u32[]{:S(2)}) collective-permute-start(bf16[512,512]{1,0:T(8,128)(2,1)} %collective-permute-done.1.refs_0_.refs_3_), channel_id=1, source_target_pairs={{0,1},{1,2},{2,3},{3,0},{4,5},{5,6},{6,7},{7,4},{8,9},{9,10},{10,1... | collective-permute-start | bytes 1572872 | tf_op jit(solution)/shard_map/ppermute | solution.py:30
  98.3 17.5 %collective-permute-start.15 = (bf16[512,512]{1,0:T(8,128)(2,1)}, bf16[512,512]{1,0:T(8,128)(2,1)}, u32[]{:S(2)}, u32[]{:S(2)}) collective-permute-start(bf16[512,512]{1,0:T(8,128)(2,1)} %collective-permute-done.9.refs_1_.refs_5_), channel_id=1, source_target_pairs={{0,1},{1,2},{2,3},{3,0},{4,5},{5,6},{6,7},{7,4},{8,9},{9,10},{10,1... | collective-permute-start | bytes 1572872 | tf_op jit(solution)/shard_map/ppermute | solution.py:30
  98.6 17.2 %collective-permute-start.18 = (bf16[512,512]{1,0:T(8,128)(2,1)}, bf16[512,512]{1,0:T(8,128)(2,1)}, u32[]{:S(2)}, u32[]{:S(2)}) collective-permute-start(bf16[512,512]{1,0:T(8,128)(2,1)} %collective-permute-done.9.refs_1_.refs_5_), channel_id=1, source_target_pairs={{0,8},{4,12},{8,0},{12,4},{1,9},{5,13},{9,1},{13,5},{2,10},{6,14},... | collective-permute-start | bytes 1572872 | tf_op jit(solution)/shard_map/ppermute | solution.py:35
  109.8 17.2 %collective-permute-start.17 = (bf16[512,512]{1,0:T(8,128)(2,1)}, bf16[512,512]{1,0:T(8,128)(2,1)}, u32[]{:S(2)}, u32[]{:S(2)}) collective-permute-start(bf16[512,512]{1,0:T(8,128)(2,1)} %collective-permute-done.4.refs_2_.refs_7_), channel_id=1, source_target_pairs={{0,1},{1,2},{2,3},{3,0},{4,5},{5,6},{6,7},{7,4},{8,9},{9,10},{10,1... | collective-permute-start | bytes 1572872 | tf_op jit(solution)/shard_map/ppermute | solution.py:30
  110.2 16.8 %collective-permute-start.20 = (bf16[512,512]{1,0:T(8,128)(2,1)}, bf16[512,512]{1,0:T(8,128)(2,1)}, u32[]{:S(2)}, u32[]{:S(2)}) collective-permute-start(bf16[512,512]{1,0:T(8,128)(2,1)} %collective-permute-done.4.refs_2_.refs_7_), channel_id=1, source_target_pairs={{0,8},{4,12},{8,0},{12,4},{1,9},{5,13},{9,1},{13,5},{2,10},{6,14},... | collective-permute-start | bytes 1572872 | tf_op jit(solution)/shard_map/ppermute | solution.py:35
  125.4 15.7 %collective-permute-start.19 = (bf16[512,512]{1,0:T(8,128)(2,1)}, bf16[512,512]{1,0:T(8,128)(2,1)}, u32[]{:S(2)}, u32[]{:S(2)}) collective-permute-start(bf16[512,512]{1,0:T(8,128)(2,1)} %collective-permute-done.11.refs_3_), channel_id=1, source_target_pairs={{0,1},{1,2},{2,3},{3,0},{4,5},{5,6},{6,7},{7,4},{8,9},{9,10},{10,1... | collective-permute-start | bytes 1572872 | tf_op jit(solution)/shard_map/ppermute | solution.py:30
  125.8 15.3 %collective-permute-start.30 = (bf16[512,512]{1,0:T(8,128)(2,1)}, bf16[512,512]{1,0:T(8,128)(2,1)}, u32[]{:S(2)}, u32[]{:S(2)}) collective-permute-start(bf16[512,512]{1,0:T(8,128)(2,1)} %collective-permute-done.11.refs_3_), channel_id=1, source_target_pairs={{0,8},{4,12},{8,0},{12,4},{1,9},{5,13},{9,1},{13,5},{2,10},{6,14},... | collective-permute-start | bytes 1572872 | tf_op jit(solution)/shard_map/ppermute | solution.py:35
  127.0 25.3 %collective-permute-start.33 = (bf16[512,512]{1,0:T(8,128)(2,1)}, bf16[512,512]{1,0:T(8,128)(2,1)}, u32[]{:S(2)}, u32[]{:S(2)}) collective-permute-start(bf16[512,512]{1,0:T(8,128)(2,1)} %collective-permute-done.6.refs_4_.refs_5_), channel_id=1, source_target_pairs={{0,8},{4,12},{8,0},{12,4},{1,9},{5,13},{9,1},{13,5},{2,10},{6,14},... | collective-permute-start | bytes 1572872 | tf_op jit(solution)/shard_map/ppermute | solution.py:35
  128.3 24.1 %collective-permute-start.21 = (bf16[512,512]{1,0:T(8,128)(2,1)}, bf16[512,512]{1,0:T(8,128)(2,1)}, u32[]{:S(2)}, u32[]{:S(2)}) collective-permute-start(bf16[512,512]{1,0:T(8,128)(2,1)} %collective-permute-done.6.refs_4_.refs_5_), channel_id=1, source_target_pairs={{0,1},{1,2},{2,3},{3,0},{4,5},{5,6},{6,7},{7,4},{8,9},{9,10},{10,1... | collective-permute-start | bytes 1572872 | tf_op jit(solution)/shard_map/ppermute | solution.py:30
  130.2 12.2 %collective-permute-start.32 = (bf16[512,512]{1,0:T(8,128)(2,1)}, bf16[512,512]{1,0:T(8,128)(2,1)}, u32[]{:S(2)}, u32[]{:S(2)}) collective-permute-start(bf16[512,512]{1,0:T(8,128)(2,1)} %broadcast_select_fusion.9), channel_id=1, source_target_pairs={{0,4},{4,0},{8,12},{12,8},{1,5},{5,1},{9,13},{13,9},{2,6},{6,2},{1... | collective-permute-start | bytes 1572872 | tf_op jit(solution)/shard_map/ppermute | solution.py:35
  141.1 23.9 %collective-permute-start.36 = (bf16[512,512]{1,0:T(8,128)(2,1)}, bf16[512,512]{1,0:T(8,128)(2,1)}, u32[]{:S(2)}, u32[]{:S(2)}) collective-permute-start(bf16[512,512]{1,0:T(8,128)(2,1)} %collective-permute-done.13.refs_5_.refs_7_), channel_id=1, source_target_pairs={{0,8},{4,12},{8,0},{12,4},{1,9},{5,13},{9,1},{13,5},{2,10},{6,14},... | collective-permute-start | bytes 1572872 | tf_op jit(solution)/shard_map/ppermute | solution.py:35
  142.3 22.6 %collective-permute-start.31 = (bf16[512,512]{1,0:T(8,128)(2,1)}, bf16[512,512]{1,0:T(8,128)(2,1)}, u32[]{:S(2)}, u32[]{:S(2)}) collective-permute-start(bf16[512,512]{1,0:T(8,128)(2,1)} %collective-permute-done.13.refs_5_.refs_7_), channel_id=1, source_target_pairs={{0,1},{1,2},{2,3},{3,0},{4,5},{5,6},{6,7},{7,4},{8,9},{9,10},{10,1... | collective-permute-start | bytes 1572872 | tf_op jit(solution)/shard_map/ppermute | solution.py:30
  152.3 20.7 %collective-permute-start.39 = (bf16[512,512]{1,0:T(8,128)(2,1)}, bf16[512,512]{1,0:T(8,128)(2,1)}, u32[]{:S(2)}, u32[]{:S(2)}) collective-permute-start(bf16[512,512]{1,0:T(8,128)(2,1)} %collective-permute-done.8.refs_0_.refs_1_), channel_id=1, source_target_pairs={{0,8},{4,12},{8,0},{12,4},{1,9},{5,13},{9,1},{13,5},{2,10},{6,14},... | collective-permute-start | bytes 1572872 | tf_op jit(solution)/shard_map/ppermute | solution.py:35
  153.6 21.2 %collective-permute-start.34 = (bf16[512,512]{1,0:T(8,128)(2,1)}, bf16[512,512]{1,0:T(8,128)(2,1)}, u32[]{:S(2)}, u32[]{:S(2)}) collective-permute-start(bf16[512,512]{1,0:T(8,128)(2,1)} %collective-permute-done.8.refs_0_.refs_1_), channel_id=1, source_target_pairs={{0,1},{1,2},{2,3},{3,0},{4,5},{5,6},{6,7},{7,4},{8,9},{9,10},{10,1... | collective-permute-start | bytes 1572872 | tf_op jit(solution)/shard_map/ppermute | solution.py:30
  169.2 18.2 %collective-permute-start.42 = (bf16[512,512]{1,0:T(8,128)(2,1)}, bf16[512,512]{1,0:T(8,128)(2,1)}, u32[]{:S(2)}, u32[]{:S(2)}) collective-permute-start(bf16[512,512]{1,0:T(8,128)(2,1)} %collective-permute-done.15.refs_1_.refs_2_), channel_id=1, source_target_pairs={{0,8},{4,12},{8,0},{12,4},{1,9},{5,13},{9,1},{13,5},{2,10},{6,14},... | collective-permute-start | bytes 1572872 | tf_op jit(solution)/shard_map/ppermute | solution.py:35
  170.2 17.1 %collective-permute-start.37 = (bf16[512,512]{1,0:T(8,128)(2,1)}, bf16[512,512]{1,0:T(8,128)(2,1)}, u32[]{:S(2)}, u32[]{:S(2)}) collective-permute-start(bf16[512,512]{1,0:T(8,128)(2,1)} %collective-permute-done.15.refs_1_.refs_2_), channel_id=1, source_target_pairs={{0,1},{1,2},{2,3},{3,0},{4,5},{5,6},{6,7},{7,4},{8,9},{9,10},{10,1... | collective-permute-start | bytes 1572872 | tf_op jit(solution)/shard_map/ppermute | solution.py:30
  174.8 21.4 %collective-permute-start.45 = (bf16[512,512]{1,0:T(8,128)(2,1)}, bf16[512,512]{1,0:T(8,128)(2,1)}, u32[]{:S(2)}, u32[]{:S(2)}) collective-permute-start(bf16[512,512]{1,0:T(8,128)(2,1)} %collective-permute-done.17.refs_2_.refs_3_), channel_id=1, source_target_pairs={{0,8},{4,12},{8,0},{12,4},{1,9},{5,13},{9,1},{13,5},{2,10},{6,14},... | collective-permute-start | bytes 1572872 | tf_op jit(solution)/shard_map/ppermute | solution.py:35
  176.0 21.1 %collective-permute-start.40 = (bf16[512,512]{1,0:T(8,128)(2,1)}, bf16[512,512]{1,0:T(8,128)(2,1)}, u32[]{:S(2)}, u32[]{:S(2)}) collective-permute-start(bf16[512,512]{1,0:T(8,128)(2,1)} %collective-permute-done.17.refs_2_.refs_3_), channel_id=1, source_target_pairs={{0,1},{1,2},{2,3},{3,0},{4,5},{5,6},{6,7},{7,4},{8,9},{9,10},{10,1... | collective-permute-start | bytes 1572872 | tf_op jit(solution)/shard_map/ppermute | solution.py:30
  187.4 20.9 %collective-permute-start.48 = (bf16[512,512]{1,0:T(8,128)(2,1)}, bf16[512,512]{1,0:T(8,128)(2,1)}, u32[]{:S(2)}, u32[]{:S(2)}) collective-permute-start(bf16[512,512]{1,0:T(8,128)(2,1)} %collective-permute-done.19.refs_3_.refs_1_), channel_id=1, source_target_pairs={{0,8},{4,12},{8,0},{12,4},{1,9},{5,13},{9,1},{13,5},{2,10},{6,14},... | collective-permute-start | bytes 1572872 | tf_op jit(solution)/shard_map/ppermute | solution.py:35
  187.4 20.9 %collective-permute-start.43 = (bf16[512,512]{1,0:T(8,128)(2,1)}, bf16[512,512]{1,0:T(8,128)(2,1)}, u32[]{:S(2)}, u32[]{:S(2)}) collective-permute-start(bf16[512,512]{1,0:T(8,128)(2,1)} %collective-permute-done.19.refs_3_.refs_1_), channel_id=1, source_target_pairs={{0,1},{1,2},{2,3},{3,0},{4,5},{5,6},{6,7},{7,4},{8,9},{9,10},{10,1... | collective-permute-start | bytes 1572872 | tf_op jit(solution)/shard_map/ppermute | solution.py:30
  197.1 21.4 %collective-permute-start.51 = (bf16[512,512]{1,0:T(8,128)(2,1)}, bf16[512,512]{1,0:T(8,128)(2,1)}, u32[]{:S(2)}, u32[]{:S(2)}) collective-permute-start(bf16[512,512]{1,0:T(8,128)(2,1)} %collective-permute-done.21.refs_4_.refs_2_), channel_id=1, source_target_pairs={{0,8},{4,12},{8,0},{12,4},{1,9},{5,13},{9,1},{13,5},{2,10},{6,14},... | collective-permute-start | bytes 1572872 | tf_op jit(solution)/shard_map/ppermute | solution.py:35
  198.4 21.1 %collective-permute-start.46 = (bf16[512,512]{1,0:T(8,128)(2,1)}, bf16[512,512]{1,0:T(8,128)(2,1)}, u32[]{:S(2)}, u32[]{:S(2)}) collective-permute-start(bf16[512,512]{1,0:T(8,128)(2,1)} %collective-permute-done.21.refs_4_.refs_2_), channel_id=1, source_target_pairs={{0,1},{1,2},{2,3},{3,0},{4,5},{5,6},{6,7},{7,4},{8,9},{9,10},{10,1... | collective-permute-start | bytes 1572872 | tf_op jit(solution)/shard_map/ppermute | solution.py:30
  208.3 22.4 %collective-permute-start.50 = (bf16[512,512]{1,0:T(8,128)(2,1)}, bf16[512,512]{1,0:T(8,128)(2,1)}, u32[]{:S(2)}, u32[]{:S(2)}) collective-permute-start(bf16[512,512]{1,0:T(8,128)(2,1)} %collective-permute-done.31.refs_5_.refs_3_), channel_id=1, source_target_pairs={{0,8},{4,12},{8,0},{12,4},{1,9},{5,13},{9,1},{13,5},{2,10},{6,14},... | collective-permute-start | bytes 1572872 | tf_op jit(solution)/shard_map/ppermute | solution.py:35
  209.6 21.1 %collective-permute-start.49 = (bf16[512,512]{1,0:T(8,128)(2,1)}, bf16[512,512]{1,0:T(8,128)(2,1)}, u32[]{:S(2)}, u32[]{:S(2)}) collective-permute-start(bf16[512,512]{1,0:T(8,128)(2,1)} %collective-permute-done.31.refs_5_.refs_3_), channel_id=1, source_target_pairs={{0,1},{1,2},{2,3},{3,0},{4,5},{5,6},{6,7},{7,4},{8,9},{9,10},{10,1... | collective-permute-start | bytes 1572872 | tf_op jit(solution)/shard_map/ppermute | solution.py:30
  219.5 20.9 %collective-permute-start.56 = (bf16[512,512]{1,0:T(8,128)(2,1)}, bf16[512,512]{1,0:T(8,128)(2,1)}, u32[]{:S(2)}, u32[]{:S(2)}) collective-permute-start(bf16[512,512]{1,0:T(8,128)(2,1)} %collective-permute-done.34.refs_0_.refs_1_), channel_id=1, source_target_pairs={{0,8},{4,12},{8,0},{12,4},{1,9},{5,13},{9,1},{13,5},{2,10},{6,14},... | collective-permute-start | bytes 1572872 | tf_op jit(solution)/shard_map/ppermute | solution.py:35
  220.9 21.1 %collective-permute-start.55 = (bf16[512,512]{1,0:T(8,128)(2,1)}, bf16[512,512]{1,0:T(8,128)(2,1)}, u32[]{:S(2)}, u32[]{:S(2)}) collective-permute-start(bf16[512,512]{1,0:T(8,128)(2,1)} %collective-permute-done.48.refs_3_), channel_id=1, source_target_pairs={{0,1},{1,2},{2,3},{3,0},{4,5},{5,6},{6,7},{7,4},{8,9},{9,10},{10,1... | collective-permute-start | bytes 1572872 | tf_op jit(solution)/shard_map/ppermute | solution.py:30
  236.5 19.3 %collective-permute-start.61 = (bf16[512,512]{1,0:T(8,128)(2,1)}, bf16[512,512]{1,0:T(8,128)(2,1)}, u32[]{:S(2)}, u32[]{:S(2)}) collective-permute-start(bf16[512,512]{1,0:T(8,128)(2,1)} %collective-permute-done.37.refs_1_.refs_2_), channel_id=1, source_target_pairs={{0,8},{4,12},{8,0},{12,4},{1,9},{5,13},{9,1},{13,5},{2,10},{6,14},... | collective-permute-start | bytes 1572872 | tf_op jit(solution)/shard_map/ppermute | solution.py:35
  237.7 18.1 %collective-permute-start.62 = (bf16[512,512]{1,0:T(8,128)(2,1)}, bf16[512,512]{1,0:T(8,128)(2,1)}, u32[]{:S(2)}, u32[]{:S(2)}) collective-permute-start(bf16[512,512]{1,0:T(8,128)(2,1)} %collective-permute-done.51.refs_4_), channel_id=1, source_target_pairs={{0,1},{1,2},{2,3},{3,0},{4,5},{5,6},{6,7},{7,4},{8,9},{9,10},{10,1... | collective-permute-start | bytes 1572872 | tf_op jit(solution)/shard_map/ppermute | solution.py:30
  242.0 22.4 %collective-permute-start.57 = (bf16[512,512]{1,0:T(8,128)(2,1)}, bf16[512,512]{1,0:T(8,128)(2,1)}, u32[]{:S(2)}, u32[]{:S(2)}) collective-permute-start(bf16[512,512]{1,0:T(8,128)(2,1)} %collective-permute-done.40.refs_2_.refs_3_), channel_id=1, source_target_pairs={{0,8},{4,12},{8,0},{12,4},{1,9},{5,13},{9,1},{13,5},{2,10},{6,14},... | collective-permute-start | bytes 1572872 | tf_op jit(solution)/shard_map/ppermute | solution.py:35
  243.4 21.0 %collective-permute-start.58 = (bf16[512,512]{1,0:T(8,128)(2,1)}, bf16[512,512]{1,0:T(8,128)(2,1)}, u32[]{:S(2)}, u32[]{:S(2)}) collective-permute-start(bf16[512,512]{1,0:T(8,128)(2,1)} %collective-permute-done.50.refs_4_), channel_id=1, source_target_pairs={{0,1},{1,2},{2,3},{3,0},{4,5},{5,6},{6,7},{7,4},{8,9},{9,10},{10,1... | collective-permute-start | bytes 1572872 | tf_op jit(solution)/shard_map/ppermute | solution.py:30
  (27 other events, 241.0 us)
